TPU v7x, 32 devices: a whole 2x2x4 slice. The times are simulated.
32 devices in a mesh: dp: 8 (over z, x), mp: 4 (over y, core).
Axes of the slice: x: 2, y: 2, z: 4, core: 2. Of those that a mesh axis runs over, the one named last changes fastest.
Arguments:
- row_ids: int32 [8192, 16], P('dp', 'mp'), may hold values from 0 to 131071, as said below
- counts: int32 [8], replicated, may hold values from 256 to 1024, as said below
- labels: int32 [8192, 5], P(('dp', 'mp')), may hold values from 0 to 1
- label_mask: int32 [8192, 5], P(('dp', 'mp')), may hold values 0 or 1
- embeddings: float32 [16, 131072, 64], P(None, ('dp', 'mp')), may hold values from -6 to 6
- embed_first: float32 [16, 131072, 64], P(None, ('dp', 'mp')), may hold values from -8.940697e-08 to 8.940697e-08
- embed_second: float32 [16, 131072, 64], P(None, ('dp', 'mp')), may hold values from 3.7252903e-17 to 1.4901161e-16
- expert_in: float32 [1024, 8, 512], P('dp', None, 'mp'), may hold values from -0.1875 to 0.1875
- in_first: float32 [1024, 8, 512], P('dp', None, 'mp'), may hold values from -9.536743e-06 to 9.536743e-06
- in_second: float32 [1024, 8, 512], P('dp', None, 'mp'), may hold values from 4.7683716e-13 to 1.9073486e-12
- expert_out: float32 [512, 8, 512], P('dp', None, 'mp'), may hold values from -0.25 to 0.25
- out_first: float32 [512, 8, 512], P('dp', None, 'mp'), may hold values from -9.536743e-06 to 9.536743e-06
- out_second: float32 [512, 8, 512], P('dp', None, 'mp'), may hold values from 4.7683716e-13 to 1.9073486e-12
- gating: float32 [1024, 40], replicated, may hold values from -0.09375 to 0.09375
- gating_first: float32 [1024, 40], replicated, may hold values from -3.0517578e-05 to 3.0517578e-05
- gating_second: float32 [1024, 40], replicated, may hold values from 4.2915346e-12 to 1.7166138e-11
- towers: float32 [512, 1280], replicated, may hold values from -1 to 1
- towers_first: float32 [512, 1280], replicated, may hold values from -3.0517578e-05 to 3.0517578e-05
- towers_second: float32 [512, 1280], replicated, may hold values from 4.2915346e-12 to 1.7166138e-11
- heads: float32 [5, 256], replicated, may hold values from -0.75 to 0.75
- heads_first: float32 [5, 256], replicated, may hold values from -3.0517578e-05 to 3.0517578e-05
- heads_second: float32 [5, 256], replicated, may hold values from 4.2915346e-12 to 1.7166138e-11
- biases: float32 [9517], replicated, may hold values from -1 to 1
- biases_first: float32 [9517], replicated, may hold values from -0.00010681152 to 0.00010681152
- biases_second: float32 [9517], replicated, may hold values from 4.7683715e-11 to 1.9073486e-10
Outputs:
- embed_next: float32 [16, 131072, 64], P(None, ('dp', 'mp'))
- embed_moment: float32 [16, 131072, 64], P(None, ('dp', 'mp'))
- embed_square: float32 [16, 131072, 64], P(None, ('dp', 'mp'))
- in_next: float32 [1024, 8, 512], P('dp', None, 'mp')
- in_moment: float32 [1024, 8, 512], P('dp', None, 'mp')
- in_square: float32 [1024, 8, 512], P('dp', None, 'mp')
- in_copy: bfloat16 [1024, 8, 512], P('dp', None, 'mp')
- out_next: float32 [512, 8, 512], P('dp', None, 'mp')
- out_moment: float32 [512, 8, 512], P('dp', None, 'mp')
- out_square: float32 [512, 8, 512], P('dp', None, 'mp')
- out_copy: bfloat16 [512, 8, 512], P('dp', None, 'mp')
- gating_next: float32 [1024, 40], replicated
- gating_moment: float32 [1024, 40], replicated
- gating_square: float32 [1024, 40], replicated
- towers_next: float32 [512, 1280], replicated
- towers_moment: float32 [512, 1280], replicated
- towers_square: float32 [512, 1280], replicated
- heads_next: float32 [5, 256], replicated
- heads_moment: float32 [5, 256], replicated
- heads_square: float32 [5, 256], replicated
- biases_next: float32 [9517], replicated
- biases_moment: float32 [9517], replicated
- biases_square: float32 [9517], replicated
- grad_norm: float32 [1], replicated
- loss: float32 [2], replicated
- stats: float32 [14], replicated
Inputs may be any that keep to these rules, and one draw needn't show every extreme that they name: `row_ids`: row r of a table lies on the device of index r // 4096 over dp+mp. Of the 4096 ids in the block of one index of dp (its 1024 samples) and one index of mp (its 4 tables), at most 256 fall on the rows of any one device, and some device receives exactly 256 from every such block. `counts`: the last index of dp uses all 1024 slots.
All inputs are finite; a program needn't handle non-finite values. No bound on the sum of `label_mask` on one device may be relied on, other than what follows from the above.
Results may differ from a plain program's by a relative error of at most 0.0076.
Values may be sent and summed in bfloat16 or wider, within the bound.
A program may use at most 256 MiB of HBM per device.

v0:
```python
import jax
import jax.numpy as jnp
from jax import lax
from jax.sharding import PartitionSpec as P

TABLES = 16
D_EMB = 64
ROWS_DEV = 4096
EXPERTS = 8
HID = 512
OUT = 512
TASKS = 5
TH = 256
STEP = 3


HIGH = lax.Precision.HIGHEST
beta_one = 0.5
beta_two = 0.5
adam_eps = 1e-08
decay = 0.01
clip_max = 0.002
rate_table = 0.5
rate_dense = 0.02
stat_eps = 1e-06


def unpack(vector):
    first = EXPERTS * HID
    second = first + EXPERTS * OUT
    third = second + TASKS * EXPERTS
    fourth = third + TASKS * TH
    return (
        vector[:first].reshape(EXPERTS, HID),
        vector[first:second].reshape(EXPERTS, OUT),
        vector[second:third].reshape(TASKS, EXPERTS),
        vector[third:fourth].reshape(TASKS, TH),
        vector[fourth:],
    )


def adamw(weight, first, second, gradient, rate):
    first_next = beta_one * first + (1.0 - beta_one) * gradient
    second_next = beta_two * second + (1.0 - beta_two) * gradient * gradient
    corrected = first_next / (1.0 - beta_one**STEP)
    scaled = jnp.sqrt(second_next / (1.0 - beta_two**STEP))
    return (
        weight - rate * (corrected / (scaled + adam_eps) + decay * weight),
        first_next,
        second_next,
    )


def gelu_pair(value):
    result, back = jax.vjp(jax.nn.gelu, value)
    return (result, back(jnp.ones_like(value))[0])


def body(
    row_ids,
    counts,
    labels,
    label_mask,
    embeddings,
    embed_first,
    embed_second,
    expert_in,
    in_first,
    in_second,
    expert_out,
    out_first,
    out_second,
    gating,
    gating_first,
    gating_second,
    towers,
    towers_first,
    towers_second,
    heads,
    heads_first,
    heads_second,
    biases,
    biases_first,
    biases_second,
):
    devices = lax.axis_size(("dp", "mp"))
    mp_count = lax.axis_size("mp")
    mp_index = lax.axis_index("mp")
    samples = row_ids.shape[0]
    tables_here = row_ids.shape[1]
    own_rows = samples // mp_count
    requests = samples * tables_here
    capacity = 2 * requests // devices
    wanted = row_ids.reshape(-1)
    owner = wanted // ROWS_DEV
    table_number = mp_index * tables_here + jnp.tile(
        jnp.arange(tables_here, dtype=jnp.int32), samples
    )
    request_code = table_number * ROWS_DEV + wanted % ROWS_DEV
    onehot = (owner[:, None] == jnp.arange(devices, dtype=jnp.int32)[None, :]).astype(jnp.int32)
    slot_index = jnp.sum(jnp.cumsum(onehot, axis=0) * onehot, axis=1) - 1
    target = owner * capacity + slot_index
    outgoing = jnp.full((devices * capacity,), -1, jnp.int32).at[target].set(request_code)
    asked = lax.all_to_all(
        outgoing.reshape(devices, capacity), ("dp", "mp"), split_axis=0, concat_axis=0, tiled=True
    ).reshape(-1)
    filled = asked >= 0
    safe_code = jnp.maximum(asked, 0)
    flat_table = embeddings.reshape(-1, D_EMB)
    found = jnp.where(filled[:, None], flat_table[safe_code], 0.0).astype(jnp.bfloat16)
    returned = lax.all_to_all(
        found.reshape(devices, capacity * D_EMB),
        ("dp", "mp"),
        split_axis=0,
        concat_axis=0,
        tiled=True,
    )
    embedded = returned.reshape(devices * capacity, D_EMB)[target].reshape(
        samples, tables_here * D_EMB
    )
    valid_all = (jnp.arange(samples, dtype=jnp.int32) < counts[lax.axis_index("dp")]).astype(
        jnp.float32
    )
    own_start = mp_index * own_rows
    valid_own = lax.dynamic_slice_in_dim(valid_all, own_start, own_rows, 0)
    embed_float = embedded.astype(jnp.float32)
    input_sq = jnp.sum(valid_all[:, None] * embed_float * embed_float)
    inner_bias, outer_bias, gate_bias, tower_bias, head_bias = unpack(biases)
    in_rows, out_rows = (
        lax.all_gather(expert_in.astype(jnp.bfloat16), "dp", axis=0, tiled=True),
        lax.all_gather(expert_out.astype(jnp.bfloat16), "dp", axis=0, tiled=True),
    )
    inputs = lax.all_gather(embedded, "mp", axis=1, tiled=True)
    own_inputs = lax.dynamic_slice_in_dim(inputs, own_start, own_rows, 0)
    in_full, out_full = (in_rows, out_rows)
    hidden_here = in_full.shape[2]
    bias_here = lax.dynamic_slice_in_dim(inner_bias, mp_index * hidden_here, hidden_here, 1)
    preact = (
        jnp.einsum("si,ieh->seh", inputs, in_full, preferred_element_type=jnp.float32) + bias_here
    )
    hidden_float, hidden_slope = gelu_pair(preact)
    hidden = hidden_float.astype(jnp.bfloat16)
    expert_y = (
        lax.psum_scatter(
            jnp.einsum("seh,oeh->seo", hidden, out_full, preferred_element_type=jnp.float32),
            "mp",
            scatter_dimension=0,
            tiled=True,
        )
        + outer_bias
    )
    gating_low = gating.astype(jnp.bfloat16)
    gate_logit = jnp.dot(
        own_inputs, gating_low, preferred_element_type=jnp.float32
    ) + gate_bias.reshape(-1)
    gates = jax.nn.softmax(gate_logit.reshape(own_rows, TASKS, EXPERTS), axis=-1)
    mixed = jnp.einsum("ske,seo->sko", gates, expert_y, precision=HIGH)
    mixed_low = mixed.astype(jnp.bfloat16)
    tower_low = towers.astype(jnp.bfloat16).reshape(OUT, TASKS, TH)
    tower_pre = (
        jnp.einsum("sko,okj->skj", mixed_low, tower_low, preferred_element_type=jnp.float32)
        + tower_bias
    )
    tower_act, tower_slope = gelu_pair(tower_pre)
    logits = jnp.sum(tower_act * heads, axis=-1) + head_bias
    target_float = labels.astype(jnp.float32)
    weights = valid_own[:, None] * label_mask.astype(jnp.float32)
    loss_here = jnp.sum(weights * (jax.nn.softplus(logits) - target_float * logits))
    valid_rows = valid_own[:, None, None]
    expert_sq = jnp.sum(valid_rows * expert_y * expert_y, axis=(0, 2))
    mixed_sq = jnp.sum(valid_rows * mixed * mixed, axis=(0, 2))
    logit_grad = weights * (jax.nn.sigmoid(logits) - target_float)
    heads_grad = jnp.einsum("sk,skj->kj", logit_grad, tower_act, precision=HIGH)
    head_bias_grad = jnp.sum(logit_grad, axis=0)
    tower_grad = (logit_grad[:, :, None] * heads * tower_slope).astype(jnp.bfloat16)
    towers_grad = jnp.einsum(
        "sko,skj->okj", mixed_low, tower_grad, preferred_element_type=jnp.float32
    ).reshape(OUT, TASKS * TH)
    tower_bias_grad = jnp.sum(tower_grad.astype(jnp.float32), axis=0)
    mixed_grad = jnp.einsum(
        "skj,okj->sko", tower_grad, tower_low, preferred_element_type=jnp.float32
    )
    gate_grad = jnp.einsum("sko,seo->ske", mixed_grad, expert_y, precision=HIGH)
    gate_logit_grad = gates * (gate_grad - jnp.sum(gates * gate_grad, axis=-1, keepdims=True))
    gate_logit_grad = gate_logit_grad.reshape(own_rows, TASKS * EXPERTS).astype(jnp.bfloat16)
    output_grad = jnp.einsum("ske,sko->seo", gates, mixed_grad, precision=HIGH).astype(jnp.bfloat16)
    gating_grad = jnp.einsum(
        "si,sk->ik", own_inputs, gate_logit_grad, preferred_element_type=jnp.float32
    )
    gate_bias_grad = jnp.sum(gate_logit_grad.astype(jnp.float32), axis=0)
    outer_bias_grad = jnp.sum(output_grad.astype(jnp.float32), axis=0)
    input_gate_grad = jnp.einsum(
        "sk,ik->si", gate_logit_grad, gating_low, preferred_element_type=jnp.float32
    )
    output_rows = lax.all_gather(output_grad, "mp", axis=0, tiled=True)
    hidden_grad = jnp.einsum(
        "seo,oeh->seh", output_rows, out_full, preferred_element_type=jnp.float32
    )
    preact_grad = (hidden_grad * hidden_slope).astype(jnp.bfloat16)
    out_grad = jnp.einsum("seo,seh->oeh", output_rows, hidden, preferred_element_type=jnp.float32)
    in_grad = jnp.einsum("si,seh->ieh", inputs, preact_grad, preferred_element_type=jnp.float32)
    inner_bias_part = jnp.sum(preact_grad.astype(jnp.float32), axis=0)
    input_grad = jnp.einsum("seh,ieh->si", preact_grad, in_full, preferred_element_type=jnp.float32)
    own_part = lax.dynamic_slice_in_dim(input_grad, own_start, own_rows, 0) + input_gate_grad
    input_grad = lax.dynamic_update_slice_in_dim(input_grad, own_part, own_start, 0)
    embed_grad = lax.psum_scatter(input_grad, "mp", scatter_dimension=1, tiled=True)
    inner_bias_grad = lax.dynamic_update_slice_in_dim(
        jnp.zeros((EXPERTS, HID), jnp.float32), inner_bias_part, mp_index * hidden_here, 1
    )
    in_grad, out_grad = (
        lax.psum_scatter(in_grad, "dp", scatter_dimension=0, tiled=True),
        lax.psum_scatter(out_grad, "dp", scatter_dimension=0, tiled=True),
    )
    back_rows = (
        jnp.zeros((devices * capacity, D_EMB), jnp.float32)
        .at[target]
        .set(embed_grad.reshape(requests, D_EMB))
    )
    arrived = lax.all_to_all(
        back_rows.reshape(devices, capacity * D_EMB),
        ("dp", "mp"),
        split_axis=0,
        concat_axis=0,
        tiled=True,
    ).reshape(-1, D_EMB)
    table_grad = (
        jnp.zeros_like(flat_table)
        .at[safe_code]
        .add(jnp.where(filled[:, None], arrived, 0.0))
        .reshape(embeddings.shape)
    )
    large_sq = (
        jnp.sum(table_grad * table_grad) + jnp.sum(in_grad * in_grad) + jnp.sum(out_grad * out_grad)
    )
    bias_grad = jnp.concatenate(
        [
            inner_bias_grad.reshape(-1),
            outer_bias_grad.reshape(-1),
            gate_bias_grad,
            tower_bias_grad.reshape(-1),
            head_bias_grad,
        ]
    )
    sums_here = jnp.concatenate(
        [loss_here[None], input_sq[None], expert_sq, mixed_sq, jnp.sum(weights)[None]]
    )
    gating_sum, towers_sum, heads_sum, bias_sum, sums, large_total = lax.psum(
        (gating_grad, towers_grad, heads_grad, bias_grad, sums_here, large_sq), ("dp", "mp")
    )
    weight_total = sums[-1]
    small_sq = (
        jnp.sum(gating_sum * gating_sum)
        + jnp.sum(towers_sum * towers_sum)
        + jnp.sum(heads_sum * heads_sum)
        + jnp.sum(bias_sum * bias_sum)
    )
    grad_norm = jnp.sqrt(large_total + small_sq) / weight_total
    factor = jnp.minimum(1.0, clip_max / grad_norm) / weight_total
    embed_out = adamw(embeddings, embed_first, embed_second, table_grad * factor, rate_table)
    in_out = adamw(expert_in, in_first, in_second, in_grad * factor, rate_dense)
    out_out = adamw(expert_out, out_first, out_second, out_grad * factor, rate_dense)
    gating_out = adamw(gating, gating_first, gating_second, gating_sum * factor, rate_dense)
    towers_out = adamw(towers, towers_first, towers_second, towers_sum * factor, rate_dense)
    heads_out = adamw(heads, heads_first, heads_second, heads_sum * factor, rate_dense)
    biases_out = adamw(biases, biases_first, biases_second, bias_sum * factor, rate_dense)
    n_valid = jnp.sum(counts).astype(jnp.float32)
    widths = jnp.concatenate(
        [
            jnp.full((1,), TABLES * D_EMB, jnp.float32),
            jnp.full((EXPERTS + TASKS,), OUT, jnp.float32),
        ]
    )
    stats = jnp.sqrt(sums[1 : 2 + EXPERTS + TASKS] / (n_valid * widths) + stat_eps)
    loss = jnp.stack([sums[0], weight_total])
    return (
        embed_out[0],
        embed_out[1],
        embed_out[2],
        in_out[0],
        in_out[1],
        in_out[2],
        in_out[0].astype(jnp.bfloat16),
        out_out[0],
        out_out[1],
        out_out[2],
        out_out[0].astype(jnp.bfloat16),
        gating_out[0],
        gating_out[1],
        gating_out[2],
        towers_out[0],
        towers_out[1],
        towers_out[2],
        heads_out[0],
        heads_out[1],
        heads_out[2],
        biases_out[0],
        biases_out[1],
        biases_out[2],
        grad_norm.reshape(1),
        loss,
        stats,
    )


def solution(mesh):
    placed = (
        P("dp", "mp"),
        P(),
        P(("dp", "mp"), None),
        P(("dp", "mp"), None),
        P(None, ("dp", "mp"), None),
        P(None, ("dp", "mp"), None),
        P(None, ("dp", "mp"), None),
        P("dp", None, "mp"),
        P("dp", None, "mp"),
        P("dp", None, "mp"),
        P("dp", None, "mp"),
        P("dp", None, "mp"),
        P("dp", None, "mp"),
        P(),
        P(),
        P(),
        P(),
        P(),
        P(),
        P(),
        P(),
        P(),
        P(),
        P(),
        P(),
    )
    return jax.shard_map(
        body,
        mesh=mesh,
        in_specs=placed,
        out_specs=(
            P(None, ("dp", "mp"), None),
            P(None, ("dp", "mp"), None),
            P(None, ("dp", "mp"), None),
            P("dp", None, "mp"),
            P("dp", None, "mp"),
            P("dp", None, "mp"),
            P("dp", None, "mp"),
            P("dp", None, "mp"),
            P("dp", None, "mp"),
            P("dp", None, "mp"),
            P("dp", None, "mp"),
            P(),
            P(),
            P(),
            P(),
            P(),
            P(),
            P(),
            P(),
            P(),
            P(),
            P(),
            P(),
            P(),
            P(),
            P(),
        ),
        check_vma=False,
    )
```

profile of v0, /device:TPU:0, one launch (start us, length us, event | category | flops | bytes accessed | tf_op | source)
XLA Modules:
  0.0 1143.6 jit_solution(8336994644905862189)
XLA Ops:
  9.1 9.2 reduce-window.6
  20.4 16.1 %scatter_custom_fusion = s32[8192]{0:T(1024)} fusion(s32[4096]{0:T(1024)S(1)} %bitcast.105, s32[4096]{0:T(1024)S(1)} %get-tuple-element.223, s32[]{:T(128)} %constant.43.clone.1), kind=kCustom, calls=%fused_computation.160 | custom fusion | bytes 32772 | tf_op jit(solution)/shard_map/scatter | solution.py:103
  36.5 7.3 all-to-all-start
  44.6 19.3 %copy.277 = bf16[16,4096,64]{2,1,0:T(8,128)(2,1)} copy(f32[16,4096,64]{1,2,0:T(8,128)} %param.29) | data formatting | bytes 25165824 | tf_op args[4]
  67.9 29.8 %gather_fusion = bf16[8192,64]{1,0:T(8,128)(2,1)S(1)} fusion(bf16[65536,64]{1,0:T(8,128)(2,1)} %bitcast.95, s32[8192]{0:T(1024)S(1)} %broadcast_clamp_fusion), kind=kCustom, calls=%fused_computation | custom fusion | bytes 2129920 | tf_op jit(solution)/shard_map/gather | solution.py:110
  110.5 26.0 %all-to-all-done.1 = bf16[32,2,8192]{2,1,0:T(2,128)(2,1)S(1)} async-done(((bf16[32,2,8192]{2,1,0:T(2,128)(2,1)}), bf16[32,2,8192]{2,1,0:T(2,128)(2,1)S(1)}, u32[]{:S(2)}, u32[]{:S(2)}) %all-to-all-start.1) | async-done | bytes 1048608 | tf_op jit(solution)/shard_map/all_to_all | solution.py:111
  146.2 12.1 %gather_fusion.1 = bf16[4096,64]{1,0:T(8,128)(2,1)S(1)} fusion(bf16[8192,64]{1,0:T(8,128)(2,1)S(1)} %reshape.316, s32[4096]{0:T(1024)S(1)} %broadcast_clamp_fusion.1), kind=kCustom, calls=%fused_computation.1 | custom fusion | bytes 1064960 | tf_op jit(solution)/shard_map/gather | solution.py:118
  160.8 21.1 %all-gather.5.cloned.1.call-done = bf16[1024,1024]{1,0:T(8,128)(2,1)} async-done(((bf16[1024,256]{1,0:T(8,128)(2,1)}), bf16[1024,1024]{1,0:T(8,128)(2,1)}) %all-gather.5.cloned.1.call-update) | async-done | bytes 2097168 | tf_op jit(solution)/shard_map/all_gather | solution.py:133
  188.4 36.4 %all-gather.9.cloned.1.call-done = bf16[512,8,128]{2,0,1:T(8,128)(2,1)} async-done(((bf16[64,8,128]{2,0,1:T(8,128)(2,1)}), bf16[512,8,128]{2,0,1:T(8,128)(2,1)}) %all-gather.9.cloned.1.call-update) | async-done | bytes 1048592 | tf_op jit(solution)/shard_map/all_gather | solution.py:131
  224.9 11.0 convolution_bitcast_fusion
  242.3 118.6 %reduce-scatter.5.cloned.1.call-done = f32[256,8,512]{2,0,1:T(8,128)} async-done(((f32[1024,8,512]{2,0,1:T(8,128)}), f32[256,8,512]{2,0,1:T(8,128)}) %reduce-scatter.5.cloned.1.call-update) | async-done | bytes 4194320 | tf_op jit(solution)/shard_map/reduce_scatter | solution.py:144
  364.6 7.1 fusion.22
  383.5 14.3 %fusion.9 = f32[256,5,8]{2,1,0:T(8,128)} fusion(f32[256,5,512]{2,0,1:T(8,128)S(1)} %convolution_bitcast_fusion.2, f32[256,8,512]{2,0,1:T(8,128)} %copy-done.1), kind=kOutput, calls=%fused_computation.26 | convolution fusion | flops 62914560 | bytes 6856704 | tf_op jit(solution)/shard_map/sko,seo->ske/dot_general | solution.py:183
  400.0 41.8 %all-gather.11.cloned.1.call-done = bf16[1024,8,512]{2,1,0:T(8,128)(2,1)} async-done(((bf16[256,8,512]{2,1,0:T(8,128)(2,1)}), bf16[1024,8,512]{2,1,0:T(8,128)(2,1)}) %all-gather.11.cloned.1.call-update) | async-done | bytes 8388624 | tf_op jit(solution)/shard_map/all_gather | solution.py:195
  441.8 9.6 convert_reduce_fusion.1
  465.3 11.8 %fusion.42 = f32[512,8,128]{0,2,1:T(8,128)S(1)} fusion(bf16[1024,8,512]{2,1,0:T(8,128)(2,1)} %all-gather.11.cloned.1.call-done, f32[1024,8,128]{2,0,1:T(8,128)} %fusion.33, f32[8,128]{1,0:T(8,128)S(1)} %copy-done.41), kind=kOutput, calls=%fused_computation.70 | convolution fusion | flops 1084227584 | bytes 14684160 | tf_op jit(solution)/shard_map/seo,seh->oeh/dot_general | solution.py:200
  479.1 6.6 fusion.31
  485.8 17.2 %reduce-scatter.7.cloned.1.call-done = f32[1024,256]{1,0:T(8,128)} async-done(((f32[1024,1024]{1,0:T(8,128)}), f32[1024,256]{1,0:T(8,128)}) %reduce-scatter.7.cloned.1.call-update) | async-done | bytes 1048592 | tf_op jit(solution)/shard_map/reduce_scatter | solution.py:206
  504.6 13.0 %scatter_custom_fusion.1 = f32[8192,64]{1,0:T(8,128)} fusion(s32[4096]{0:T(1024)} %bitcast.107, f32[4096,64]{1,0:T(8,128)S(1)} %reshape.356, f32[]{:T(128)} %constant.42.clone.1), kind=kCustom, calls=%fused_computation.63 | custom fusion | bytes 2097664 | tf_op jit(solution)/shard_map/scatter | solution.py:217
  534.2 130.8 %all-reduce.4.cloned.1.call-done = (f32[1024,40]{0,1:T(8,128)}, f32[512,1280]{1,0:T(8,128)}) async-done(((f32[1024,40]{0,1:T(8,128)}, f32[512,1280]{1,0:T(8,128)}), (f32[1024,40]{0,1:T(8,128)}, f32[512,1280]{1,0:T(8,128)})) %all-reduce.4.cloned.1.call-update) | async-done | bytes 2785296 | tf_op jit(solution)/shard_map/psum | solution.py:247
  671.0 65.7 %reduce-scatter.11.cloned.1.call-done = f32[64,8,128]{2,1,0:T(8,128)} async-done(((f32[512,8,128]{2,1,0:T(8,128)}), f32[64,8,128]{2,1,0:T(8,128)}) %reduce-scatter.11.cloned.1.call-update) | async-done | bytes 262160 | tf_op jit(solution)/shard_map/reduce_scatter | solution.py:212
  738.3 89.7 %reduce-scatter.9.cloned.1.call-done = f32[128,8,128]{2,0,1:T(8,128)} async-done(((f32[1024,8,128]{2,0,1:T(8,128)}), f32[128,8,128]{2,0,1:T(8,128)}) %reduce-scatter.9.cloned.1.call-update) | async-done | bytes 524304 | tf_op jit(solution)/shard_map/reduce_scatter | solution.py:211
  829.8 6.7 reduce.5
  839.6 68.3 %scatter_custom_fusion.2 = f32[65536,64]{1,0:T(8,128)} fusion(s32[8192]{0:T(1024)} %bitcast.102, f32[]{:T(128)} %constant.42.clone.1, f32[8192,64]{1,0:T(8,128)} %reshape.322, pred[8192]{0:T(1024)(128)(4,1)S(1)} %ge.15), kind=kCustom, calls=%fused_computation.14 | custom fusion | flops 1048576 | bytes 20980736 | tf_op jit(solution)/shard_map/scatter-add | solution.py:229
  907.9 24.5 %copy.301 = f32[65536,64]{0,1:T(8,128)} copy(f32[65536,64]{1,0:T(8,128)} %scatter_custom_fusion.2) | data formatting | bytes 33554432 | tf_op jit(solution)/shard_map/scatter-add | solution.py:229
  932.4 15.6 %multiply_reduce_fusion = f32[]{:T(128)} fusion(f32[65536,64]{1,0:T(8,128)} %scatter_custom_fusion.2), kind=kLoop, calls=%fused_computation.7 | loop fusion | flops 8388607 | bytes 16777220 | tf_op jit(solution)/shard_map/reduce_sum | solution.py:233
  949.9 41.1 %all-reduce = (f32[16]{0:T(128)S(1)}, f32[]{:T(128)}, f32[5,256]{1,0:T(8,128)S(1)}, f32[9517]{0:T(1024)S(1)}) all-reduce(f32[16]{0:T(128)S(1)} %concatenate.6, f32[]{:T(128)S(6)} %add.323, f32[5,256]{1,0:T(8,128)S(1)} %bitcast.113, f32[9517]{0:T(1024)S(1)} %concatenate.7), channel_id=1, replica_groups=mesh['dp'=8,'mp'=4] {'dp','mp'}, use_global_device_ids=true, to_apply=%region_17.18 | all-reduce | flops 10814 | bytes 86512 | tf_op jit(solution)/shard_map/psum | solution.py:247
  1003.3 11.8 %copy.328 = f32[8,8,16,4096]{3,2,1,0:T(8,128)} copy(f32[8,8,16,4096]{3,1,2,0:T(8,128)S(1)} %bitcast.96) | data formatting | bytes 33554432
  1015.1 50.2 %multiply_subtract_fusion = (f32[16,4096,64]{1,0,2:T(8,128)}, f32[16,4096,64]{1,0,2:T(8,128)}, f32[16,4096,64]{1,0,2:T(8,128)}) fusion(f32[16,4096,64]{1,2,0:T(8,128)} %param.29, f32[8,8,16,4096]{3,2,1,0:T(8,128)} %copy.328, f32[16,4096,64]{1,2,0:T(8,128)} %param.30, f32[16,4096,64]{1,2,0:T(8,128)} %param.31), kind=kLoop, calls=%fused_computation.13 | loop fusion | flops 58720256 | bytes 117440512 | tf_op jit(solution)/shard_map/sub | solution.py:48
  1065.3 19.6 %copy.309 = f32[16,4096,64]{1,2,0:T(8,128)} copy(f32[16,4096,64]{1,0,2:T(8,128)} %get-tuple-element.210) | data formatting | bytes 33554432
  1084.9 17.5 %copy.310 = f32[16,4096,64]{1,2,0:T(8,128)} copy(f32[16,4096,64]{1,0,2:T(8,128)S(1)} %copy-done) | data formatting | bytes 33554432
  1102.5 17.7 %copy.311 = f32[16,4096,64]{1,2,0:T(8,128)} copy(f32[16,4096,64]{1,0,2:T(8,128)S(1)} %bitcast.94) | data formatting | bytes 33554432
  (245 shorter events, 131.8 us)
Async XLA Ops:
  9.0 34.8 %copy-start.13 = (f32[128,8,128]{2,1,0:T(8,128)S(1)}, f32[128,8,128]{2,1,0:T(8,128)}, u32[]{:S(2)}) copy-start(f32[128,8,128]{2,1,0:T(8,128)} %param.32) | copy-start | bytes 1572868
  20.3 90.1 %copy-start.32 = (s32[4096,1]{0,1:T(1,128)}, s32[4096,1]{0,1:T(1,128)S(1)}, u32[]{:S(2)}) copy-start(s32[4096,1]{0,1:T(1,128)S(1)} %compare_select_fusion) | copy-start | bytes 49156
  36.5 27.5 %all-to-all-start = ((s32[32,1,256]{2,1,0:T(1,128)}), s32[32,1,256]{2,1,0:T(1,128)S(1)}, u32[]{:S(2)}, u32[]{:S(2)}) async-start(s32[32,1,256]{2,1,0:T(1,128)} %bitcast.3), calls=%async_computation | async-start | bytes 65536 | tf_op jit(solution)/shard_map/all_to_all | solution.py:104
  43.8 117.0 %all-gather.7.cloned.1.call-start = ((), (), s32[]{:S(2)}) async-start(), calls=%async_computation.8 | async-start | bytes 2359296 | tf_op jit(solution)/shard_map/all_gather | solution.py:130
  104.3 32.1 %all-to-all-start.1 = ((bf16[32,2,8192]{2,1,0:T(2,128)(2,1)}), bf16[32,2,8192]{2,1,0:T(2,128)(2,1)S(1)}, u32[]{:S(2)}, u32[]{:S(2)}) async-start(bf16[32,2,8192]{2,1,0:T(2,128)(2,1)} %reshape.384), calls=%async_computation.1 | async-start | bytes 2097152 | tf_op jit(solution)/shard_map/all_to_all | solution.py:111
  110.2 71.7 %all-gather.5.cloned.1.call-start = ((), (), s32[]{:S(2)}) async-start(), calls=%async_computation.7 | async-start | bytes 2621440 | tf_op jit(solution)/shard_map/all_gather | solution.py:133
  146.2 13.7 %copy-start.19 = (f32[64,8,128]{2,1,0:T(8,128)S(1)}, f32[64,8,128]{2,1,0:T(8,128)}, u32[]{:S(2)}) copy-start(f32[64,8,128]{2,1,0:T(8,128)} %param.35) | copy-start | bytes 786436
  158.3 30.1 %copy-start.5 = (bf16[4096,64]{1,0:T(8,128)(2,1)}, bf16[4096,64]{1,0:T(8,128)(2,1)S(1)}, u32[]{:S(2)}) copy-start(bf16[4096,64]{1,0:T(8,128)(2,1)S(1)} %gather_fusion.1) | copy-start | bytes 1572868
  159.9 65.0 %all-gather.9.cloned.1.call-start = ((), (), s32[]{:S(2)}) async-start(), calls=%async_computation.9 | async-start | bytes 1179648 | tf_op jit(solution)/shard_map/all_gather | solution.py:131
  160.6 200.3 %reduce-scatter.5.cloned.1.call-start = ((), (), s32[]{:S(2)}) async-start(), calls=%async_computation.10 | async-start | bytes 20971520 | tf_op jit(solution)/shard_map/reduce_scatter | solution.py:144
  160.8 64.1 %copy-start.40 = (f32[8,128]{1,0:T(8,128)}, f32[8,128]{1,0:T(8,128)S(1)}, u32[]{:S(2)}) copy-start(f32[8,128]{1,0:T(8,128)S(1)} %constant_dynamic-slice_fusion) | copy-start | bytes 12292
  235.9 205.8 %all-gather.11.cloned.1.call-start = ((), (), s32[]{:S(2)}) async-start(), calls=%async_computation.11 | async-start | bytes 10485760 | tf_op jit(solution)/shard_map/all_gather | solution.py:195
  242.3 122.3 %copy-start.7 = (f32[256,5,8]{1,2,0:T(8,128)}, f32[256,5,8]{1,2,0:T(8,128)S(1)}, u32[]{:S(2)}) copy-start(f32[256,5,8]{1,2,0:T(8,128)S(1)} %copy.287) | copy-start | bytes 122884
  383.3 119.7 %reduce-scatter.7.cloned.1.call-start = ((), (), s32[]{:S(2)}) async-start(), calls=%async_computation.12 | async-start | bytes 5242880 | tf_op jit(solution)/shard_map/reduce_scatter | solution.py:206
  399.9 51.4 %copy-start.51 = (bf16[1024,8,128]{2,0,1:T(8,128)(2,1)S(1)}, bf16[1024,8,128]{2,0,1:T(8,128)(2,1)}, u32[]{:S(2)}) copy-start(bf16[1024,8,128]{2,0,1:T(8,128)(2,1)} %all-gather.7.cloned.1.call-done) | copy-start | bytes 6291460
  458.3 206.7 %all-reduce.4.cloned.1.call-start = ((), (), s32[]{:S(2)}) async-start(), calls=%async_computation.15 | async-start | bytes 5570560 | tf_op jit(solution)/shard_map/psum | solution.py:247
  465.2 271.4 %reduce-scatter.11.cloned.1.call-start = ((), (), s32[]{:S(2)}) async-start(), calls=%async_computation.14 | async-start | bytes 2359296 | tf_op jit(solution)/shard_map/reduce_scatter | solution.py:212
  479.1 348.9 %reduce-scatter.9.cloned.1.call-start = ((), (), s32[]{:S(2)}) async-start(), calls=%async_computation.13 | async-start | bytes 4718592 | tf_op jit(solution)/shard_map/reduce_scatter | solution.py:211
  523.0 7.9 copy-start.18
  523.0 7.9 copy-start.39
  523.0 306.8 %all-to-all-start.2 = ((f32[32,1,16384]{2,1,0:T(1,128)}), f32[32,1,16384]{2,1,0:T(1,128)}, u32[]{:S(2)}, u32[]{:S(2)}) async-start(f32[32,1,16384]{2,1,0:T(1,128)} %all_to_all.21), calls=%async_computation.4 | async-start | bytes 4194304 | tf_op jit(solution)/shard_map/all_to_all | solution.py:219
  530.9 140.0 %copy-start.49 = (f32[5]{0:T(128)S(1)}, f32[5]{0:T(128)}, u32[]{:S(2)}) copy-start(f32[5]{0:T(128)} %get-tuple-element.221) | copy-start | bytes 64
  1065.3 19.6 %copy-start = (f32[16,4096,64]{1,0,2:T(8,128)S(1)}, f32[16,4096,64]{1,0,2:T(8,128)}, u32[]{:S(2)}) copy-start(f32[16,4096,64]{1,0,2:T(8,128)} %get-tuple-element.211) | copy-start | bytes 50331652
  1065.3 37.1 %slice-start = ((s8[16777216]{0:T(1024)(128)(4,1)}), s8[4194304]{0:T(1024)(128)(4,1)S(1)}, s32[]{:S(2)}) async-start(s8[16777216]{0:T(1024)(128)(4,1)} %bitcast.93), calls=%async_computation.16 | async-start | bytes 8388608
  1065.3 37.1 %slice-start.1 = ((s8[16777216]{0:T(1024)(128)(4,1)}), s8[4194304]{0:T(1024)(128)(4,1)S(1)}, s32[]{:S(2)}) async-start(s8[16777216]{0:T(1024)(128)(4,1)} %bitcast.93), calls=%async_computation.17 | async-start | bytes 8388608
  1084.9 17.5 %slice-start.2 = ((s8[16777216]{0:T(1024)(128)(4,1)}), s8[4194304]{0:T(1024)(128)(4,1)S(1)}, s32[]{:S(2)}) async-start(s8[16777216]{0:T(1024)(128)(4,1)} %bitcast.93), calls=%async_computation.18 | async-start | bytes 8388608
  1084.9 17.5 %slice-start.3 = ((s8[16777216]{0:T(1024)(128)(4,1)}), s8[4194304]{0:T(1024)(128)(4,1)S(1)}, s32[]{:S(2)}) async-start(s8[16777216]{0:T(1024)(128)(4,1)} %bitcast.93), calls=%async_computation.19 | async-start | bytes 8388608
  1102.4 17.7 %copy-start.14 = (f32[128,8,128]{2,1,0:T(8,128)S(1)}, f32[128,8,128]{2,1,0:T(8,128)}, u32[]{:S(2)}) copy-start(f32[128,8,128]{2,1,0:T(8,128)} %param.32) | copy-start | bytes 1572868
  1102.5 17.7 %copy-start.15 = (f32[128,8,128]{2,0,1:T(8,128)S(1)}, f32[128,8,128]{2,0,1:T(8,128)}, u32[]{:S(2)}) copy-start(f32[128,8,128]{2,0,1:T(8,128)} %reduce-scatter.9.cloned.1.call-done) | copy-start | bytes 1572868
  1102.5 17.7 %copy-start.23 = (f32[128,8,128]{2,1,0:T(8,128)S(1)}, f32[128,8,128]{2,1,0:T(8,128)}, u32[]{:S(2)}) copy-start(f32[128,8,128]{2,1,0:T(8,128)} %param.33) | copy-start | bytes 1572868
  1102.5 17.7 %copy-start.24 = (f32[128,8,128]{2,1,0:T(8,128)S(1)}, f32[128,8,128]{2,1,0:T(8,128)}, u32[]{:S(2)}) copy-start(f32[128,8,128]{2,1,0:T(8,128)} %param.34) | copy-start | bytes 1572868
  1102.5 25.2 %copy-start.12 = (f32[512,1280]{1,0:T(8,128)S(1)}, f32[512,1280]{1,0:T(8,128)}, u32[]{:S(2)}) copy-start(f32[512,1280]{1,0:T(8,128)} %param.43) | copy-start | bytes 7864324
  (40 other events, 189.6 us)
Sparse Core Ops, SparseCore 0:
  47.4 50.4 all-gather.6
  160.0 21.8 all-gather.4
  184.6 40.1 all-gather.8
  236.0 124.8 reduce-scatter.4
  383.4 58.2 all-gather.10
  458.4 44.5 reduce-scatter.6
  509.8 155.1 all-reduce.3
  669.1 67.5 reduce-scatter.10
  740.9 87.1 reduce-scatter.8
where the time goes:
time: 1150 us; the launch traced here: 1140 us
  waiting for transfers between devices  548 us (48%)
  local copies, waits for them, and re-layouts  226 us (20%)
  other arithmetic  196 us (17%)
  matrix products  89.4 us (8%)
  blocking collectives  41.1 us (4%)
  between operations  24.2 us (2%)
  starting transfers between devices  19.1 us (2%)
    psum x1, waiting for transfers between devices, body(): lax.psum((gating_grad, towers_grad, heads_grad, bias_grad, sums_here, lar...  131 us
    reduce_scatter x1, waiting for transfers between devices, body(): lax.psum_scatter(jnp.einsum('seh,oeh->seo', hidden, out_full, preferred_e...  119 us
    unnamed x136, local copies, waits for them, and re-layouts  98.7 us
    reduce_scatter x1, waiting for transfers between devices, body(): lax.psum_scatter(in_grad, 'dp', scatter_dimension=0, tiled=True)  89.7 us
    scatter-add x1, other arithmetic, body(): table_grad = jnp.zeros_like(flat_table).at[safe_code].add(jnp.where(fille...  68.3 us
    reduce_scatter x1, waiting for transfers between devices, body(): lax.psum_scatter(out_grad, 'dp', scatter_dimension=0, tiled=True)  65.7 us
    sub x5, other arithmetic, adamw(): weight - rate * (corrected / (scaled + adam_eps) + decay * weight)  57.1 us
    all_gather x1, waiting for transfers between devices, body(): output_rows = lax.all_gather(output_grad, 'mp', axis=0, tiled=True)  41.8 us
  transfers between devices with their start and end apart: 12, of which 9 were waited for; matrix products, arithmetic and copies ran while one was open for 15% of the time, Pallas kernels for 0%

commit v1 on v0

v1 whole, which is shorter than its diff:
```python
import functools
import math

import jax
import jax.numpy as jnp
from jax import lax
from jax.experimental import pallas as pl
from jax.experimental.pallas import tpu as pltpu
from jax.sharding import PartitionSpec as P

EXPERTS = 8
TASKS = 5
STEP = 3

HIGH = lax.Precision.HIGHEST
beta_one = 0.5
beta_two = 0.5
adam_eps = 1e-08
decay = 0.01
clip_max = 0.002
rate_table = 0.5
rate_dense = 0.02
stat_eps = 1e-06

LOW = jnp.bfloat16
F32 = jnp.float32
I32 = jnp.int32
MIB = 1024 * 1024
AXES = ("dp", "mp")


def params(mib):
    return pltpu.CompilerParams(vmem_limit_bytes=mib * MIB)


VMEM = pl.BlockSpec(memory_space=pltpu.VMEM)
SMEM = pl.BlockSpec(memory_space=pltpu.SMEM)


def adamw(weight, first, second, gradient, rate):
    first_next = beta_one * first + (1.0 - beta_one) * gradient
    second_next = beta_two * second + (1.0 - beta_two) * gradient * gradient
    corrected = first_next / (1.0 - beta_one**STEP)
    scaled = jnp.sqrt(second_next / (1.0 - beta_two**STEP))
    return (
        weight - rate * (corrected / (scaled + adam_eps) + decay * weight),
        first_next,
        second_next,
    )


def gelu_pair(value):
    result, back = jax.vjp(jax.nn.gelu, value)
    return (result, back(jnp.ones_like(value))[0])


def route_kernel(row_bits, ids_ref, out_ref, place_ref, slot_ref):
    devices, capacity = out_ref.shape
    tables, samples = ids_ref.shape
    rows_dev = 1 << row_bits
    halves = devices * capacity // 2
    width = 256
    upper = (
        lax.broadcasted_iota(I32, (width, width), 0) <= lax.broadcasted_iota(I32, (width, width), 1)
    ).astype(LOW)
    owners = lax.broadcasted_iota(I32, (devices, width), 0)
    slots = lax.broadcasted_iota(I32, (capacity, width), 0)
    carry = jnp.zeros((devices, 1), F32)
    total = jnp.zeros((2 * devices, capacity), F32)
    for table in range(tables):
        parity = table % 2
        for part in range(samples // width):
            cols = pl.ds(part * width, width)
            ids = ids_ref[pl.ds(table, 1), cols]
            owner = ids >> row_bits
            code = (parity * (tables // 2) + table // 2) * rows_dev + (ids & (rows_dev - 1)) + 1
            onehot = (owner == owners).astype(F32)
            counted = jnp.dot(onehot.astype(LOW), upper, preferred_element_type=F32) + carry
            rank = jnp.sum(onehot * counted, axis=0, keepdims=True).astype(I32) - 1
            carry = counted[:, width - 1 :]
            at_slot = (rank == slots).astype(LOW)
            high = (code >> 7).astype(F32)
            low = (code & 127).astype(F32)
            pieces = jnp.concatenate([onehot * high, onehot * low], axis=0).astype(LOW)
            total += lax.dot_general(
                pieces, at_slot, (((1,), (1,)), ((), ())), preferred_element_type=F32
            )
            row = owner * (capacity // 2) + (rank >> 1)
            half = rank & 1
            place_ref[pl.ds(table, 1), cols] = (half ^ parity) * halves + row
            slot_ref[pl.ds(table, 1), cols] = half * halves + row
    codes = (total[:devices] * 128.0 + total[devices:]).astype(I32)
    first = lax.broadcasted_iota(I32, (devices, capacity), 1) == 0
    counted = jnp.where(first, carry * 65536.0, 0.0).astype(I32)
    out_ref[...] = codes + counted


def turn_kernel(table_ref, out_ref):
    pair, width, rows = table_ref.shape
    out_ref[0] = table_ref[...].reshape(pair * width, rows).T


def left_lanes(shape):
    return lax.broadcasted_iota(I32, shape, len(shape) - 1) < 64


def find_kernel(groups, code_bits, codes_ref, table_ref, out_ref, rows_ref):
    group = pl.program_id(0)
    blocks, _, height, lanes = out_ref.shape
    mask = (1 << code_bits) - 1
    left = left_lanes((1, lanes))

    def fetch(code, side):
        at = jnp.maximum((code & 65535) - 1, 0)
        row = table_ref[pl.ds(at & mask, 1), :]
        return pltpu.roll(row, ((at >> code_bits) ^ side) * 64, 1)

    def block_step(block, _):
        source = block * groups + group
        count = codes_ref[source, 0] >> 16

        def step(outer, _):
            for inner in range(8):
                at = outer * 8 + inner
                even = fetch(codes_ref[source, 2 * at], 0)
                odd = fetch(codes_ref[source, 2 * at + 1], 1)
                rows_ref[pl.ds(at, 1), :] = jnp.where(left, even, odd)
            return 0

        lax.fori_loop(0, (count + 15) // 16, step, 0)
        out_ref[block, 0] = rows_ref[...].astype(LOW)
        return 0

    lax.fori_loop(0, blocks, block_step, 0)


def place_kernel(place_ref, rows_ref, out_ref, both_ref, flat_ref):
    count, lanes = rows_ref.shape
    tables, samples = place_ref.shape
    rows = rows_ref[...].astype(F32)
    both_ref[pl.ds(0, count), :] = rows
    both_ref[pl.ds(count, count), :] = pltpu.roll(rows, 64, 1)
    left = left_lanes((1, lanes))

    def step(outer, _):
        for inner in range(8):
            sample = outer * 8 + inner
            for pair in range(tables // 2):
                even = both_ref[pl.ds(place_ref[2 * pair, sample], 1), :]
                odd = both_ref[pl.ds(place_ref[2 * pair + 1, sample], 1), :]
                flat_ref[pair, pl.ds(sample, 1), :] = jnp.where(left, even, odd)
        return 0

    lax.fori_loop(0, samples // 8, step, 0)
    for pair in range(tables // 2):
        out_ref[:, pair * lanes : (pair + 1) * lanes] = flat_ref[pair].astype(LOW)


def send_kernel(slot_ref, grad_ref, out_ref, both_ref, rows_ref):
    count, lanes = out_ref.shape
    tables, samples = slot_ref.shape
    for pair in range(tables // 2):
        rows = grad_ref[:, pair * lanes : (pair + 1) * lanes]
        both_ref[pair, pl.ds(0, samples), :] = rows
        both_ref[pair, pl.ds(samples, samples), :] = pltpu.roll(rows, 64, 1)
    bits = count.bit_length() - 1

    def step(outer, _):
        for inner in range(8):
            sample = outer * 8 + inner
            for table in range(tables):
                slot = slot_ref[table, sample]
                turned = (slot >> bits) ^ (table % 2)
                rows_ref[pl.ds(slot, 1), :] = both_ref[
                    table // 2, pl.ds(turned * samples + sample, 1), :
                ]
        return 0

    lax.fori_loop(0, samples // 8, step, 0)
    left = left_lanes((count, lanes))
    out_ref[...] = jnp.where(
        left, rows_ref[pl.ds(0, count), :], rows_ref[pl.ds(count, count), :]
    ).astype(LOW)


def add_kernel(groups, code_bits, codes_ref, rows_ref, out_ref, square_ref, parts_ref, sems, *sums):
    count, lanes = rows_ref.shape
    sources = codes_ref.shape[0]
    height = count // sources
    mask = (1 << code_bits) - 1
    table_rows = sums[0].shape[0]
    left = left_lanes((count, lanes))
    rows = rows_ref[...].astype(F32)
    turned = pltpu.roll(rows, 64, 1)
    parts_ref[pl.ds(0, count), :] = jnp.where(left, rows, 0.0)
    parts_ref[pl.ds(count, count), :] = jnp.where(left, 0.0, turned)
    parts_ref[pl.ds(2 * count, count), :] = jnp.where(left, turned, 0.0)
    parts_ref[pl.ds(3 * count, count), :] = jnp.where(left, 0.0, rows)
    parts_ref[pl.ds(4 * count, 8), :] = jnp.zeros((8, lanes), F32)

    def clear(at, _):
        for table in sums:
            table[pl.ds(pl.multiple_of(at * 64, 64), 64), :] = jnp.zeros((64, lanes), F32)
        return 0

    lax.fori_loop(0, table_rows // 64, clear, 0)

    def block_step(block, _):
        most = codes_ref[block * groups, 0] >> 16
        for group in range(1, groups):
            most = jnp.maximum(most, codes_ref[block * groups + group, 0] >> 16)

        def step(outer, _):
            for inner in range(4):
                for group in range(groups):
                    source = block * groups + group
                    code = codes_ref[source, outer * 4 + inner] & 65535
                    at = jnp.maximum(code - 1, 0)
                    parity = at >> code_bits
                    part = ((inner % 2) * 2 + parity) * count + source * height
                    part = part + outer * 2 + inner // 2
                    part = jnp.where(code > 0, part, 4 * count)
                    here = pl.ds(at & mask, 1)
                    sums[group][here, :] = sums[group][here, :] + parts_ref[pl.ds(part, 1), :]
            return 0

        lax.fori_loop(0, (most + 3) // 4, step, 0)
        return 0

    lax.fori_loop(0, sources // groups, block_step, 0)
    copies = [
        pltpu.make_async_copy(
            sums[group], out_ref.at[pl.ds(group * table_rows, table_rows)], sems.at[group]
        )
        for group in range(groups)
    ]
    for copy in copies:
        copy.start()

    def square(at, total):
        for table in sums:
            rows = table[pl.ds(pl.multiple_of(at * 64, 64), 64), :]
            total = total + jnp.sum((rows * rows).reshape(8, 8, lanes), axis=0)
        return total

    square_ref[...] = lax.fori_loop(0, table_rows // 64, square, jnp.zeros((8, lanes), F32))
    for copy in copies:
        copy.wait()


def table_kernel(factor_ref, weight_ref, first_ref, second_ref, grad_ref, *outs):
    pair, width, rows = weight_ref.shape
    gradient = grad_ref[0].T.reshape(pair, width, rows) * factor_ref[0]
    results = adamw(weight_ref[...], first_ref[...], second_ref[...], gradient, rate_table)
    for out, result in zip(outs, results):
        out[...] = result


def body(
    row_ids,
    counts,
    labels,
    label_mask,
    embeddings,
    embed_first,
    embed_second,
    expert_in,
    in_first,
    in_second,
    expert_out,
    out_first,
    out_second,
    gating,
    gating_first,
    gating_second,
    towers,
    towers_first,
    towers_second,
    heads,
    heads_first,
    heads_second,
    biases,
    biases_first,
    biases_second,
):
    devices = lax.axis_size(AXES)
    mp_count = lax.axis_size("mp")
    dp_count = lax.axis_size("dp")
    mp_index = lax.axis_index("mp")
    samples, tables_here = row_ids.shape
    tables, rows_dev, d_emb = embeddings.shape
    own = samples // mp_count
    requests = samples * tables_here
    capacity = 2 * requests // devices
    height = capacity // 2
    slots = devices * height
    row_bits = rows_dev.bit_length() - 1
    code_bits = row_bits + (tables_here // 2).bit_length() - 1
    pairs = tables // 2
    lanes = 2 * d_emb
    group_rows = tables_here // 2 * rows_dev
    in_rows, out_rows = expert_in.shape[0], expert_out.shape[0]
    experts_here = EXPERTS // mp_count
    hid = expert_in.shape[2] * mp_count
    features = tables * d_emb
    width_out = out_rows * dp_count
    tower_hid = towers.shape[1] // TASKS

    outgoing, place, slot = pl.pallas_call(
        functools.partial(route_kernel, row_bits),
        out_shape=(
            jax.ShapeDtypeStruct((devices, capacity), I32),
            jax.ShapeDtypeStruct((tables_here, samples), I32),
            jax.ShapeDtypeStruct((tables_here, samples), I32),
        ),
        in_specs=[VMEM],
        out_specs=(VMEM, VMEM, VMEM),
        compiler_params=params(32),
        name="route",
    )(row_ids.T)
    codes = lax.all_to_all(
        outgoing.reshape(devices, 1, capacity), AXES, split_axis=0, concat_axis=0, tiled=True
    ).reshape(devices, capacity)

    shard = jnp.concatenate([expert_in, expert_out], axis=0).astype(LOW)
    shard = lax.all_to_all(shard, "mp", split_axis=1, concat_axis=2, tiled=True)
    gathered = lax.all_gather(shard, "dp", axis=0, tiled=False)
    w_in = gathered[:, :in_rows].reshape(in_rows * dp_count, experts_here, hid)
    w_out = gathered[:, in_rows:].reshape(width_out, experts_here, hid)

    table_view = jnp.transpose(embeddings, (0, 2, 1))
    turned = pl.pallas_call(
        turn_kernel,
        grid=(pairs,),
        out_shape=jax.ShapeDtypeStruct((pairs, rows_dev, lanes), F32),
        in_specs=[pl.BlockSpec((2, d_emb, rows_dev), lambda p: (p, 0, 0))],
        out_specs=pl.BlockSpec((1, rows_dev, lanes), lambda p: (p, 0, 0)),
        compiler_params=params(32),
        name="turn",
    )(table_view)
    found = pl.pallas_call(
        functools.partial(find_kernel, mp_count, code_bits),
        grid=(mp_count,),
        out_shape=jax.ShapeDtypeStruct((dp_count, mp_count, height, lanes), LOW),
        in_specs=[SMEM, pl.BlockSpec((group_rows, lanes), lambda m: (m, 0))],
        out_specs=pl.BlockSpec((dp_count, 1, height, lanes), lambda m: (0, m, 0, 0)),
        scratch_shapes=[pltpu.VMEM((height, lanes), F32)],
        compiler_params=params(32),
        name="find",
    )(codes, turned.reshape(pairs * rows_dev, lanes))
    returned = lax.all_to_all(
        found.reshape(devices, height, lanes), AXES, split_axis=0, concat_axis=0, tiled=True
    )
    embedded = pl.pallas_call(
        place_kernel,
        out_shape=jax.ShapeDtypeStruct((samples, tables_here * d_emb), LOW),
        in_specs=[SMEM, VMEM],
        out_specs=VMEM,
        scratch_shapes=[
            pltpu.VMEM((2 * slots, lanes), F32),
            pltpu.VMEM((tables_here // 2, samples, lanes), F32),
        ],
        compiler_params=params(32),
        name="place",
    )(place, returned.reshape(slots, lanes))

    valid_all = (jnp.arange(samples, dtype=I32) < counts[lax.axis_index("dp")]).astype(F32)
    own_start = mp_index * own
    valid_own = lax.dynamic_slice_in_dim(valid_all, own_start, own, 0)
    embed_float = embedded.astype(F32)
    input_sq = jnp.sum(valid_all[:, None] * embed_float * embed_float)
    first = EXPERTS * hid
    second = first + EXPERTS * width_out
    third = second + TASKS * EXPERTS
    fourth = third + TASKS * tower_hid
    inner_bias = biases[:first].reshape(mp_count, experts_here, hid)
    outer_bias = biases[first:second].reshape(mp_count, experts_here, width_out)
    gate_bias = biases[second:third]
    tower_bias = biases[third:fourth].reshape(TASKS, tower_hid)
    head_bias = biases[fourth:]
    inner_here = lax.dynamic_index_in_dim(inner_bias, mp_index, 0, keepdims=False)
    outer_here = lax.dynamic_index_in_dim(outer_bias, mp_index, 0, keepdims=False)

    def exchange(parts):
        return lax.all_to_all(parts, "mp", split_axis=0, concat_axis=0, tiled=True)

    blocks = exchange(jnp.broadcast_to(embedded[None], (mp_count,) + embedded.shape))
    inputs = jnp.transpose(blocks, (1, 0, 2)).reshape(samples, features)
    own_inputs = lax.dynamic_slice_in_dim(inputs, own_start, own, 0)
    preact = jnp.einsum("si,ieh->seh", inputs, w_in, preferred_element_type=F32) + inner_here
    hidden_float, hidden_slope = gelu_pair(preact)
    hidden = hidden_float.astype(LOW)
    partial_y = jnp.einsum("seh,oeh->eso", hidden, w_out, preferred_element_type=F32)
    partial_y = (partial_y + outer_here[:, None, :]).astype(LOW)
    partial_y = partial_y.reshape(experts_here, mp_count, own, width_out).transpose(1, 0, 2, 3)
    expert_y = exchange(partial_y).reshape(EXPERTS, own, width_out).astype(F32)

    gating_low = gating.astype(LOW)
    gate_logit = jnp.dot(own_inputs, gating_low, preferred_element_type=F32) + gate_bias
    gates = jax.nn.softmax(gate_logit.reshape(own, TASKS, EXPERTS), axis=-1)
    mixed = jnp.einsum("ske,eso->sko", gates, expert_y, precision=HIGH)
    mixed_low = mixed.astype(LOW)
    tower_low = towers.astype(LOW).reshape(width_out, TASKS, tower_hid)
    tower_pre = (
        jnp.einsum("sko,okj->skj", mixed_low, tower_low, preferred_element_type=F32) + tower_bias
    )
    tower_act, tower_slope = gelu_pair(tower_pre)
    logits = jnp.sum(tower_act * heads, axis=-1) + head_bias
    target_float = labels.astype(F32)
    weights = valid_own[:, None] * label_mask.astype(F32)
    loss_here = jnp.sum(weights * (jax.nn.softplus(logits) - target_float * logits))
    expert_sq = jnp.sum(valid_own[None, :, None] * expert_y * expert_y, axis=(1, 2))
    mixed_sq = jnp.sum(valid_own[:, None, None] * mixed * mixed, axis=(0, 2))
    logit_grad = weights * (jax.nn.sigmoid(logits) - target_float)
    heads_grad = jnp.einsum("sk,skj->kj", logit_grad, tower_act, precision=HIGH)
    head_bias_grad = jnp.sum(logit_grad, axis=0)
    tower_grad = (logit_grad[:, :, None] * heads * tower_slope).astype(LOW)
    towers_grad = jnp.einsum(
        "sko,skj->okj", mixed_low, tower_grad, preferred_element_type=F32
    ).reshape(width_out, TASKS * tower_hid)
    tower_bias_grad = jnp.sum(tower_grad.astype(F32), axis=0)
    mixed_grad = jnp.einsum("skj,okj->sko", tower_grad, tower_low, preferred_element_type=F32)
    gate_grad = jnp.einsum("sko,eso->ske", mixed_grad, expert_y, precision=HIGH)
    gate_logit_grad = gates * (gate_grad - jnp.sum(gates * gate_grad, axis=-1, keepdims=True))
    gate_logit_grad = gate_logit_grad.reshape(own, TASKS * EXPERTS).astype(LOW)
    output_grad = jnp.einsum("ske,sko->eso", gates, mixed_grad, precision=HIGH).astype(LOW)
    gating_grad = jnp.einsum("si,sk->ki", own_inputs, gate_logit_grad, preferred_element_type=F32)
    gate_bias_grad = jnp.sum(gate_logit_grad.astype(F32), axis=0)
    outer_bias_grad = jnp.sum(output_grad.astype(F32), axis=1)
    input_gate_grad = jnp.einsum(
        "sk,ik->si", gate_logit_grad, gating_low, preferred_element_type=F32
    )
    output_rows = exchange(output_grad.reshape(mp_count, experts_here, own, width_out))
    output_rows = output_rows.transpose(1, 0, 2, 3).reshape(experts_here, samples, width_out)

    hidden_grad = jnp.einsum("eso,oeh->seh", output_rows, w_out, preferred_element_type=F32)
    preact_grad = (hidden_grad * hidden_slope).astype(LOW)
    out_grad = jnp.einsum("eso,seh->oeh", output_rows, hidden, preferred_element_type=F32)
    in_grad = jnp.einsum("si,seh->ieh", inputs, preact_grad, preferred_element_type=F32)
    inner_bias_part = jnp.sum(preact_grad.astype(F32), axis=0)
    input_grad = jnp.einsum("seh,ieh->si", preact_grad, w_in, preferred_element_type=F32)
    own_part = lax.dynamic_slice_in_dim(input_grad, own_start, own, 0) + input_gate_grad
    input_grad = lax.dynamic_update_slice_in_dim(input_grad, own_part, own_start, 0)
    input_parts = input_grad.astype(LOW).reshape(samples, mp_count, tables_here * d_emb)
    embed_grad = jnp.sum(exchange(input_parts.transpose(1, 0, 2)).astype(F32), axis=0)

    back_rows = pl.pallas_call(
        send_kernel,
        out_shape=jax.ShapeDtypeStruct((slots, lanes), LOW),
        in_specs=[SMEM, VMEM],
        out_specs=VMEM,
        scratch_shapes=[
            pltpu.VMEM((tables_here // 2, 2 * samples, lanes), F32),
            pltpu.VMEM((2 * slots, lanes), F32),
        ],
        compiler_params=params(32),
        name="send",
    )(slot, embed_grad)
    arrived = lax.all_to_all(
        back_rows.reshape(devices, height, lanes), AXES, split_axis=0, concat_axis=0, tiled=True
    )
    table_grad, table_sq = pl.pallas_call(
        functools.partial(add_kernel, mp_count, code_bits),
        out_shape=(
            jax.ShapeDtypeStruct((pairs * rows_dev, lanes), F32),
            jax.ShapeDtypeStruct((8, lanes), F32),
        ),
        in_specs=[SMEM, VMEM],
        out_specs=(pl.BlockSpec(memory_space=pl.ANY), VMEM),
        scratch_shapes=[
            pltpu.VMEM((4 * slots + 8, lanes), F32),
            pltpu.SemaphoreType.DMA((mp_count,)),
        ]
        + [pltpu.VMEM((group_rows, lanes), F32)] * mp_count,
        compiler_params=params(60),
        name="add",
    )(codes, arrived.reshape(slots, lanes))

    def scatter_grad(grad, rows):
        parts = grad.astype(LOW).reshape(dp_count, rows, experts_here, mp_count, hid // mp_count)
        return parts.transpose(0, 3, 1, 2, 4).reshape(devices, rows * experts_here, hid // mp_count)

    grad_parts = jnp.concatenate([scatter_grad(in_grad, in_rows), scatter_grad(out_grad, out_rows)], 1)
    grad_parts = lax.all_to_all(grad_parts, AXES, split_axis=0, concat_axis=0, tiled=True)
    grad_sum = jnp.sum(
        grad_parts.reshape(dp_count, mp_count, in_rows + out_rows, experts_here, -1).astype(F32), 0
    )
    grad_sum = grad_sum.transpose(1, 0, 2, 3).reshape(in_rows + out_rows, EXPERTS, -1)
    in_sum, out_sum = grad_sum[:in_rows], grad_sum[in_rows:]

    inner_bias_grad = lax.dynamic_update_slice_in_dim(
        jnp.zeros((mp_count, experts_here, hid), F32), inner_bias_part[None], mp_index, 0
    )
    bias_grad = jnp.concatenate(
        [
            inner_bias_grad.reshape(-1),
            outer_bias_grad.reshape(-1),
            gate_bias_grad,
            tower_bias_grad.reshape(-1),
            head_bias_grad,
        ]
    )

    def sum_over_all(value):
        size = value.size
        unit = devices * 1024
        padded = jnp.pad(value.reshape(-1), (0, -size % unit)).reshape(devices, -1, 128)
        parts = lax.all_to_all(padded.astype(LOW), AXES, split_axis=0, concat_axis=0, tiled=True)
        share = jnp.sum(parts.astype(F32), axis=0)
        share_sq = jnp.sum(share * share)
        spread = jnp.broadcast_to(share.astype(LOW)[None], padded.shape)
        whole = lax.all_to_all(spread, AXES, split_axis=0, concat_axis=0, tiled=True)
        return whole.astype(F32).reshape(-1)[:size].reshape(value.shape), share_sq

    towers_sum, towers_sq = sum_over_all(towers_grad)
    rest, rest_sq = sum_over_all(
        jnp.concatenate([gating_grad.reshape(-1), heads_grad.reshape(-1), bias_grad])
    )
    gating_sum = rest[: gating_grad.size].reshape(gating_grad.shape).T
    heads_sum = rest[gating_grad.size : gating_grad.size + heads_grad.size].reshape(heads.shape)
    bias_sum = rest[gating_grad.size + heads_grad.size :]
    squares = (
        jnp.sum(table_sq) + jnp.sum(in_sum * in_sum) + jnp.sum(out_sum * out_sum) + towers_sq + rest_sq
    )
    sums_here = jnp.concatenate(
        [loss_here[None], input_sq[None], expert_sq, mixed_sq, jnp.sum(weights)[None], squares[None]]
    )
    sums_here = jnp.pad(sums_here, (0, 128 - sums_here.size))
    sums = jnp.sum(
        lax.all_to_all(
            jnp.broadcast_to(sums_here, (devices, 1, 128)),
            AXES,
            split_axis=0,
            concat_axis=0,
            tiled=True,
        ),
        axis=(0, 1),
    )
    stat_end = 2 + EXPERTS + TASKS
    weight_total = sums[stat_end]
    grad_norm = jnp.sqrt(sums[stat_end + 1]) / weight_total
    factor = jnp.minimum(1.0, clip_max / grad_norm) / weight_total

    table_spec = pl.BlockSpec((2, d_emb, rows_dev // 2), lambda p, c: (p, 0, c))
    embed_out = pl.pallas_call(
        table_kernel,
        grid=(pairs, 2),
        out_shape=(jax.ShapeDtypeStruct(table_view.shape, F32),) * 3,
        in_specs=[
            SMEM,
            table_spec,
            table_spec,
            table_spec,
            pl.BlockSpec((1, rows_dev // 2, lanes), lambda p, c: (p, c, 0)),
        ],
        out_specs=(table_spec,) * 3,
        compiler_params=params(48),
        name="tables",
    )(
        factor.reshape(1),
        table_view,
        jnp.transpose(embed_first, (0, 2, 1)),
        jnp.transpose(embed_second, (0, 2, 1)),
        table_grad.reshape(pairs, rows_dev, lanes),
    )
    embed_out = [jnp.transpose(value, (0, 2, 1)) for value in embed_out]
    in_out = adamw(expert_in, in_first, in_second, in_sum * factor, rate_dense)
    out_out = adamw(expert_out, out_first, out_second, out_sum * factor, rate_dense)
    gating_out = adamw(gating, gating_first, gating_second, gating_sum * factor, rate_dense)
    towers_out = adamw(towers, towers_first, towers_second, towers_sum * factor, rate_dense)
    heads_out = adamw(heads, heads_first, heads_second, heads_sum * factor, rate_dense)
    biases_out = adamw(biases, biases_first, biases_second, bias_sum * factor, rate_dense)
    n_valid = jnp.sum(counts).astype(F32)
    widths = jnp.concatenate(
        [jnp.full((1,), features, F32), jnp.full((EXPERTS + TASKS,), width_out, F32)]
    )
    stats = jnp.sqrt(sums[1:stat_end] / (n_valid * widths) + stat_eps)
    loss = jnp.stack([sums[0], weight_total])
    return (
        *embed_out,
        *in_out,
        in_out[0].astype(LOW),
        *out_out,
        out_out[0].astype(LOW),
        *gating_out,
        *towers_out,
        *heads_out,
        *biases_out,
        grad_norm.reshape(1),
        loss,
        stats,
    )


def solution(mesh):
    rows = P(None, AXES, None)
    expert = P("dp", None, "mp")
    sample = P(AXES, None)
    placed = (P("dp", "mp"), P(), sample, sample) + (rows,) * 3 + (expert,) * 6 + (P(),) * 12
    results = (rows,) * 3 + (expert,) * 8 + (P(),) * 15
    return jax.shard_map(body, mesh=mesh, in_specs=placed, out_specs=results, check_vma=False)
```

time: 1150 us -> 611 us (0.53)
  waiting for transfers between devices: 548 us -> 116 us
  Pallas kernels: 0 us -> 153 us
  other arithmetic: 196 us -> 55.3 us
  local copies, waits for them, and re-layouts: 226 us -> 88.1 us
  matrix products: 89.4 us -> 54.4 us
  blocking collectives: 41.1 us -> 68.7 us
  starting transfers between devices: 19.1 us -> 44.1 us
    reduce_scatter x4 -> x0, waiting for transfers between devices: 291 us -> none  [the longest x1 119 us: body(): lax.psum_scatter(jnp.einsum('seh,oeh->seo', hidden, out_full, preferred_e...]
    pallas_call x0 -> x7, Pallas kernels: none -> 153 us  [the longest x1 46.1 us: body(): pl.pallas_call(functools.partial(add_kernel, mp_count, code_bits), out_sh...]
    psum x1 -> x0, waiting for transfers between devices: 131 us -> none  [body(): lax.psum((gating_grad, towers_grad, heads_grad, bias_grad, sums_here, lar...]
    all_gather x4 -> x1, waiting for transfers between devices: 99.3 us -> 0.01 us  [body(): gathered = lax.all_gather(shard, 'dp', axis=0, tiled=False)]
    all_to_all x3 -> x11, waiting for transfers between devices: 26 us -> 116 us  [the longest x4 61.5 us: exchange(): return lax.all_to_all(parts, 'mp', split_axis=0, concat_axis=0, tiled=True)]
    unnamed x136 -> x117, local copies, waits for them, and re-layouts: 98.7 us -> 27.1 us
    all_to_all x0 -> x3, blocking collectives: none -> 68.7 us  [the longest x1 44.3 us: body(): lax.all_to_all(found.reshape(devices, height, lanes), AXES, split_axis=0,...]
    scatter-add x1 -> x0, other arithmetic: 68.3 us -> none  [body(): table_grad = jnp.zeros_like(flat_table).at[safe_code].add(jnp.where(fille...]
  transfers between devices with their start and end apart: 12 -> 12, of which waited for: 9 -> 9; matrix products, arithmetic and copies ran while one was open for 15% -> 18% of each run, Pallas kernels for 0% -> 16%
where the time goes in v1:
time: 611 us; the launch traced here: 603 us
  Pallas kernels  153 us (25%)
  waiting for transfers between devices  116 us (19%)
  local copies, waits for them, and re-layouts  88.1 us (14%)
  blocking collectives  68.7 us (11%)
  other arithmetic  55.3 us (9%)
  matrix products  54.4 us (9%)
  starting transfers between devices  44.1 us (7%)
  between operations  23.1 us (4%)
    all_to_all x4, waiting for transfers between devices, exchange(): return lax.all_to_all(parts, 'mp', split_axis=0, concat_axis=0, tiled=True)  61.5 us
    pallas_call x1, Pallas kernels, body(): pl.pallas_call(functools.partial(add_kernel, mp_count, code_bits), out_sh...  46.1 us
    all_to_all x1, blocking collectives, body(): lax.all_to_all(found.reshape(devices, height, lanes), AXES, split_axis=0,...  44.3 us
    pallas_call x1, Pallas kernels, body(): pl.pallas_call(table_kernel, grid=(pairs, 2), out_shape=(jax.ShapeDtypeSt...  43.1 us
    pallas_call x1, Pallas kernels, body(): pl.pallas_call(functools.partial(find_kernel, mp_count, code_bits), grid=...  32 us
    unnamed x117, local copies, waits for them, and re-layouts  27.1 us
    all_to_all x1, waiting for transfers between devices, body(): lax.all_to_all(grad_parts, AXES, split_axis=0, concat_axis=0, tiled=True)  18.1 us
    all_to_all x4, starting transfers between devices, exchange(): return lax.all_to_all(parts, 'mp', split_axis=0, concat_axis=0, tiled=True)  18 us
  transfers between devices with their start and end apart: 12, of which 9 were waited for; matrix products, arithmetic and copies ran while one was open for 18% of the time, Pallas kernels for 16%

profile of v1, /device:TPU:0, one launch (start us, length us, event | category | flops | bytes accessed | tf_op | source)
XLA Modules:
  0.0 603.4 jit_solution(11767443656543416974)
XLA Ops:
  9.5 11.5 %all_to_all.80 = bf16[192,8,128]{2,0,1:T(8,128)(2,1)S(1)} all-to-all(bf16[192,8,128]{2,0,1:T(8,128)(2,1)S(1)} %pad_maximum_fusion.1), channel_id=1, replica_groups=mesh['dp'=8,'mp'=4] {'mp'}, dimensions={1} | all-to-all | bytes 786432 | tf_op jit(solution)/shard_map/all_to_all | solution.py:326
  24.8 4.9 all-to-all-start
  29.7 10.2 %turn.1 = f32[8,4096,128]{2,1,0:T(8,128)S(1)} custom-call(f32[16,64,4096]{2,1,0:T(8,128)} %bitcast.148), custom_call_target="tpu_custom_call" | custom-call | tf_op jit(solution)/shard_map/turn/pallas_call | solution.py:332
  39.9 6.2 %copy-done = f32[8,4096,128]{2,1,0:T(8,128)} copy-done((f32[8,4096,128]{2,1,0:T(8,128)}, f32[8,4096,128]{2,1,0:T(8,128)S(1)}, u32[]{:S(2)}) %copy-start) | copy-done | bytes 16777240
  46.1 5.8 copy-done.1
  51.9 32.0 %find.1 = bf16[8,4,128,128]{3,2,1,0:T(8,128)(2,1)S(1)} custom-call(s32[32,256]{1,0:T(8,128)S(1)} %bitcast.144, f32[32768,128]{1,0:T(8,128)S(1)} %bitcast.141), custom_call_target="tpu_custom_call" | custom-call | tf_op jit(solution)/shard_map/find/pallas_call | solution.py:341
  83.9 44.3 %all_to_all.81 = bf16[32,128,128]{2,1,0:T(8,128)(2,1)S(1)} all-to-all(bf16[32,128,128]{2,1,0:T(8,128)(2,1)S(1)} %bitcast.142), channel_id=1, replica_groups=mesh['dp'=8,'mp'=4] {'dp','mp'}, dimensions={0} | all-to-all | bytes 2097152 | tf_op jit(solution)/shard_map/all_to_all | solution.py:351
  128.2 7.0 %place.1 = bf16[1024,256]{1,0:T(8,128)(2,1)S(1)} custom-call(s32[4,1024]{1,0:T(4,128)S(1)} %get-tuple-element.34.place_ref, bf16[4096,128]{1,0:T(8,128)(2,1)S(1)} %bitcast.143), custom_call_target="tpu_custom_call" | custom-call | tf_op jit(solution)/shard_map/place/pallas_call | solution.py:354
  136.7 4.6 all-to-all-start.2
  141.3 25.7 %all-to-all-done.2 = bf16[4,1024,256]{2,1,0:T(8,128)(2,1)} async-done(((bf16[4,1024,256]{2,1,0:T(8,128)(2,1)}), bf16[4,1024,256]{2,1,0:T(8,128)(2,1)}, u32[]{:S(2)}, u32[]{:S(2)}) %all-to-all-start.2) | async-done | bytes 2097184 | tf_op jit(solution)/shard_map/all_to_all | solution.py:385
  182.9 4.9 all-to-all-start.4
  195.7 17.9 %all-to-all-done.4 = bf16[4,2,256,512]{3,2,1,0:T(8,128)(2,1)} async-done(((bf16[4,2,256,512]{3,2,1,0:T(8,128)(2,1)}), bf16[4,2,256,512]{3,2,1,0:T(8,128)(2,1)}, u32[]{:S(2)}, u32[]{:S(2)}) %all-to-all-start.4) | async-done | bytes 2097184 | tf_op jit(solution)/shard_map/all_to_all | solution.py:385
  213.6 5.4 fusion.14
  224.4 7.4 %fusion.90 = (bf16[8,512]{1,0:T(8,128)(2,1)S(1)}, bf16[8,256,512]{2,0,1:T(8,128)(2,1)}) fusion(f32[256,5,8]{2,1,0:T(8,128)S(1)} %copy-done.11, f32[256,5]{1,0:T(8,128)S(1)} %copy-done.37, f32[256,5]{1,0:T(8,128)S(1)} %copy.280, f32[256,5,512]{2,0,1:T(8,128)S(1)} %convolution_bitcast_fusion.1), kind=kOutput, calls=%fused_computation.155 | convolution fusion | flops 65028096 | bytes 4777984 | tf_op jit(solution)/shard_map/ske,sko->eso/dot_general | solution.py:426
  235.9 4.3 copy.295
  240.2 4.9 all-to-all-start.5
  245.2 7.5 %fusion.1 = f32[256,5,8]{2,1,0:T(8,128)S(1)} fusion(f32[256,5,512]{2,0,1:T(8,128)S(1)} %convolution_bitcast_fusion.1, bf16[8,256,512]{2,1,0:T(8,128)(2,1)} %bitcast.17), kind=kOutput, calls=%fused_computation.6 | convolution fusion | flops 62914560 | bytes 4759552 | tf_op jit(solution)/shard_map/sko,eso->ske/dot_general | solution.py:423
  252.7 11.4 %fusion.91 = (bf16[5,8]{1,0:T(8,128)(2,1)S(1)}, bf16[256,5,8]{2,1,0:T(8,128)(2,1)S(1)}) fusion(f32[256,5,8]{2,1,0:T(8,128)S(1)} %fusion.1, f32[256,5]{1,0:T(8,128)S(1)} %copy-done.38, f32[256,5,8]{2,1,0:T(8,128)S(1)} %copy-done.12, f32[256,5]{1,0:T(8,128)S(1)} %copy.280), kind=kOutput, calls=%fused_computation.156 | output fusion | flops 93407 | bytes 112720 | tf_op jit(solution)/shard_map/sub | solution.py:424
  273.0 6.2 %convert_reduce_fusion.1 = (bf16[2,512]{1,0:T(2,128)(2,1)S(1)}, bf16[1024,2,512]{2,0,1:T(8,128)(2,1)S(1)}) fusion(f32[1024,2,512]{2,0,1:T(8,128)} %copy-done.48, f32[2,512]{1,0:T(2,128)S(1)} %get-tuple-element.196, bf16[2,1024,512]{2,1,0:T(8,128)(2,1)S(1)} %bitcast.168, bf16[512,2,512]{2,0,1:T(8,128)(2,1)S(1)} %bitcast.173), kind=kOutput, calls=%fused_computation.20 | convolution fusion | flops 1096809472 | bytes 9443328 | tf_op jit(solution)/shard_map/eso,oeh->seh/dot_general | solution.py:436
  279.2 4.4 convolution_bitcast_fusion
  312.5 13.9 %all-to-all-done.6 = bf16[4,1024,256]{1,2,0:T(8,128)(2,1)S(1)} async-done(((bf16[4,1024,256]{1,2,0:T(8,128)(2,1)}), bf16[4,1024,256]{1,2,0:T(8,128)(2,1)S(1)}, u32[]{:S(2)}, u32[]{:S(2)}) %all-to-all-start.6) | async-done | bytes 2097184 | tf_op jit(solution)/shard_map/all_to_all | solution.py:385
  332.7 12.9 %send.1 = bf16[4096,128]{1,0:T(8,128)(2,1)} custom-call(s32[4,1024]{1,0:T(4,128)S(1)} %get-tuple-element.36.slot_ref, f32[1024,256]{1,0:T(8,128)S(1)} %copy.302.grad_ref), custom_call_target="tpu_custom_call" | custom-call | tf_op jit(solution)/shard_map/send/pallas_call | solution.py:447
  345.6 16.0 %all-to-all-done.9 = bf16[32,160,128]{2,1,0:T(8,128)(2,1)} async-done(((bf16[32,160,128]{2,1,0:T(8,128)(2,1)}), bf16[32,160,128]{2,1,0:T(8,128)(2,1)}, u32[]{:S(2)}, u32[]{:S(2)}) %all-to-all-start.9) | async-done | bytes 1310752 | tf_op jit(solution)/shard_map/all_to_all | solution.py:508
  365.3 5.0 fusion.28
  401.5 46.1 %add.375 = (f32[32768,128]{1,0:T(8,128)}, f32[8,128]{1,0:T(8,128)}) custom-call(s32[32,256]{1,0:T(8,128)} %bitcast.145, bf16[4096,128]{1,0:T(8,128)(2,1)} %bitcast.33.rows_ref), custom_call_target="tpu_custom_call" | custom-call | tf_op jit(solution)/shard_map/add/pallas_call | solution.py:462
  448.9 18.1 %all-to-all-done.8 = bf16[32,384,128]{2,1,0:T(8,128)(2,1)} async-done(((bf16[32,384,128]{2,1,0:T(8,128)(2,1)}), bf16[32,384,128]{2,1,0:T(8,128)(2,1)}, u32[]{:S(2)}, u32[]{:S(2)}) %all-to-all-start.8) | async-done | bytes 3145760 | tf_op jit(solution)/shard_map/all_to_all | solution.py:484
  467.6 4.7 all-to-all-start.12
  472.4 5.4 convert_reduce_fusion
  484.5 12.9 %all_to_all.82 = f32[32,1,128]{2,1,0:T(1,128)S(1)} all-to-all(f32[32,1,128]{2,1,0:T(1,128)S(1)} %broadcast_in_dim.27), channel_id=1, replica_groups=mesh['dp'=8,'mp'=4] {'dp','mp'}, dimensions={0} | all-to-all | bytes 32768 | tf_op jit(solution)/shard_map/all_to_all | solution.py:530
  517.3 16.1 %all-to-all-done.13 = bf16[32,160,128]{2,1,0:T(8,128)(2,1)S(1)} async-done(((bf16[32,160,128]{2,1,0:T(8,128)(2,1)}), bf16[32,160,128]{2,1,0:T(8,128)(2,1)S(1)}, u32[]{:S(2)}, u32[]{:S(2)}) %all-to-all-start.13) | async-done | bytes 1310752 | tf_op jit(solution)/shard_map/all_to_all | solution.py:512
  541.2 8.0 %multiply_subtract_fusion = (f32[512,1280]{1,0:T(8,128)}, f32[512,1280]{1,0:T(8,128)}, f32[512,1280]{1,0:T(8,128)}) fusion(f32[512,1280]{1,0:T(8,128)} %param.41, f32[512,1280]{1,0:T(8,128)S(1)} %mul.473, f32[512,1280]{1,0:T(8,128)} %param.42, f32[512,1280]{1,0:T(8,128)} %param.43), kind=kLoop, calls=%fused_computation.29 | loop fusion | flops 9175040 | bytes 18350080 | tf_op jit(solution)/shard_map/sub | solution.py:46
  551.9 43.1 %tables.1 = (f32[16,64,4096]{2,1,0:T(8,128)}, f32[16,64,4096]{2,1,0:T(8,128)}, f32[16,64,4096]{2,1,0:T(8,128)}) custom-call(f32[1]{0:T(128)} %bitcast.51.factor_ref, f32[16,64,4096]{2,1,0:T(8,128)} %bitcast.149, f32[16,64,4096]{2,1,0:T(8,128)} %bitcast.150, f32[16,64,4096]{2,1,0:T(8,128)} %bitcast.151, f32[8,4096,128]{2,1,0:T(8,128)} %bitcast.152), custom_call_target="tpu_custom_call" | custom-call | tf_op jit(solution)/shard_map/tables/pallas_call | solution.py:545
  (224 shorter events, 151.7 us)
Async XLA Ops:
  7.2 165.7 %all-gather.2.cloned.1.call-start = ((), (), s32[]{:S(2)}) async-start(), calls=%async_computation.14 | async-start | bytes 3538944 | tf_op jit(solution)/shard_map/all_gather | solution.py:327
  8.3 13.9 %copy-start.3 = (s32[1024,4]{0,1:T(4,128)S(1)}, s32[1024,4]{0,1:T(4,128)}, u32[]{:S(2)}) copy-start(s32[1024,4]{0,1:T(4,128)} %param.25) | copy-start | bytes 49156
  24.8 21.2 %all-to-all-start = ((s32[32,1,256]{2,1,0:T(1,128)}), s32[32,1,256]{2,1,0:T(1,128)S(1)}, u32[]{:S(2)}, u32[]{:S(2)}) async-start(s32[32,1,256]{2,1,0:T(1,128)} %copy.278), calls=%async_computation | async-start | bytes 65536 | tf_op jit(solution)/shard_map/all_to_all | solution.py:321
  39.9 6.2 %copy-start = (f32[8,4096,128]{2,1,0:T(8,128)}, f32[8,4096,128]{2,1,0:T(8,128)S(1)}, u32[]{:S(2)}) copy-start(f32[8,4096,128]{2,1,0:T(8,128)S(1)} %turn.1) | copy-start | bytes 50331652
  46.1 37.8 %copy-start.2 = (s32[32,1,256]{2,0,1:T(8,128)}, s32[32,1,256]{2,0,1:T(8,128)S(1)}, u32[]{:S(2)}) copy-start(s32[32,1,256]{2,0,1:T(8,128)S(1)} %copy.403) | copy-start | bytes 98308
  46.1 5.8 copy-start.1
  136.7 30.3 %all-to-all-start.2 = ((bf16[4,1024,256]{2,1,0:T(8,128)(2,1)}), bf16[4,1024,256]{2,1,0:T(8,128)(2,1)}, u32[]{:S(2)}, u32[]{:S(2)}) async-start(bf16[4,1024,256]{2,1,0:T(8,128)(2,1)} %broadcast_in_dim.20), calls=%async_computation.2 | async-start | bytes 4194304 | tf_op jit(solution)/shard_map/all_to_all | solution.py:385
  182.9 30.7 %all-to-all-start.4 = ((bf16[4,2,256,512]{3,2,1,0:T(8,128)(2,1)}), bf16[4,2,256,512]{3,2,1,0:T(8,128)(2,1)}, u32[]{:S(2)}, u32[]{:S(2)}) async-start(bf16[4,2,256,512]{3,2,1,0:T(8,128)(2,1)} %bitcast.154), calls=%async_computation.4 | async-start | bytes 4194304 | tf_op jit(solution)/shard_map/all_to_all | solution.py:385
  194.8 24.2 %copy-start.10 = (f32[256,5,8]{2,1,0:T(8,128)}, f32[256,5,8]{2,1,0:T(8,128)S(1)}, u32[]{:S(2)}) copy-start(f32[256,5,8]{2,1,0:T(8,128)S(1)} %copy.281) | copy-start | bytes 122884
  195.7 23.4 %copy-start.36 = (f32[256,5]{1,0:T(8,128)}, f32[256,5]{1,0:T(8,128)S(1)}, u32[]{:S(2)}) copy-start(f32[256,5]{1,0:T(8,128)S(1)} %fusion.46) | copy-start | bytes 15364
  213.6 5.5 copy-start.41
  240.2 30.7 %all-to-all-start.5 = ((bf16[4,2,256,512]{3,1,2,0:T(2,128)(2,1)}), bf16[4,2,256,512]{3,1,2,0:T(2,128)(2,1)}, u32[]{:S(2)}, u32[]{:S(2)}) async-start(bf16[4,2,256,512]{3,1,2,0:T(2,128)(2,1)} %copy.295), calls=%async_computation.5 | async-start | bytes 4194304 | tf_op jit(solution)/shard_map/all_to_all | solution.py:385
  245.2 7.5 %copy-start.12 = (f32[256,5,8]{2,1,0:T(8,128)S(1)}, f32[256,5,8]{2,1,0:T(8,128)}, u32[]{:S(2)}) copy-start(f32[256,5,8]{2,1,0:T(8,128)} %copy-done.10) | copy-start | bytes 122884
  245.2 7.5 %copy-start.38 = (f32[256,5]{1,0:T(8,128)S(1)}, f32[256,5]{1,0:T(8,128)}, u32[]{:S(2)}) copy-start(f32[256,5]{1,0:T(8,128)} %copy-done.36) | copy-start | bytes 15364
  252.7 13.0 %copy-start.22 = (f32[256,5,256]{2,0,1:T(8,128)S(1)}, f32[256,5,256]{2,0,1:T(8,128)}, u32[]{:S(2)}) copy-start(f32[256,5,256]{2,0,1:T(8,128)} %copy-done.21) | copy-start | bytes 3932164
  273.0 6.3 %copy-start.17 = (bf16[2,4,256,512]{3,2,1,0:T(8,128)(2,1)}, bf16[2,4,256,512]{3,2,1,0:T(8,128)(2,1)S(1)}, u32[]{:S(2)}) copy-start(bf16[2,4,256,512]{3,2,1,0:T(8,128)(2,1)S(1)} %copy.296) | copy-start | bytes 6291460
  273.0 6.3 %copy-start.16 = (bf16[8,128,2,512]{3,1,0,2:T(8,128)(2,1)S(1)}, bf16[8,128,2,512]{3,1,0,2:T(8,128)(2,1)}, u32[]{:S(2)}) copy-start(bf16[8,128,2,512]{3,1,0,2:T(8,128)(2,1)} %copy-done.15) | copy-start | bytes 6291460
  285.3 11.1 %all-to-all-start.10 = ((bf16[32,16,128]{2,1,0:T(8,128)(2,1)}), bf16[32,16,128]{2,1,0:T(8,128)(2,1)S(1)}, u32[]{:S(2)}, u32[]{:S(2)}) async-start(bf16[32,16,128]{2,1,0:T(8,128)(2,1)} %bitcast.46), calls=%async_computation.10 | async-start | bytes 262144 | tf_op jit(solution)/shard_map/all_to_all | solution.py:508
  297.1 29.3 %all-to-all-start.6 = ((bf16[4,1024,256]{1,2,0:T(8,128)(2,1)}), bf16[4,1024,256]{1,2,0:T(8,128)(2,1)S(1)}, u32[]{:S(2)}, u32[]{:S(2)}) async-start(bf16[4,1024,256]{1,2,0:T(8,128)(2,1)} %bitcast.31), calls=%async_computation.6 | async-start | bytes 4194304 | tf_op jit(solution)/shard_map/all_to_all | solution.py:385
  326.4 35.3 %all-to-all-start.9 = ((bf16[32,160,128]{2,1,0:T(8,128)(2,1)}), bf16[32,160,128]{2,1,0:T(8,128)(2,1)}, u32[]{:S(2)}, u32[]{:S(2)}) async-start(bf16[32,160,128]{2,1,0:T(8,128)(2,1)} %convert_element_type.166), calls=%async_computation.9 | async-start | bytes 2621440 | tf_op jit(solution)/shard_map/all_to_all | solution.py:508
  345.6 19.7 %copy-start.18 = (bf16[2,4,256,512]{3,2,1,0:T(8,128)(2,1)S(1)}, bf16[2,4,256,512]{3,2,1,0:T(8,128)(2,1)}, u32[]{:S(2)}) copy-start(bf16[2,4,256,512]{3,2,1,0:T(8,128)(2,1)} %copy-done.17) | copy-start | bytes 6291460
  361.7 29.8 %all-to-all-start.7 = ((bf16[32,128,128]{2,1,0:T(8,128)(2,1)}), bf16[32,128,128]{2,1,0:T(8,128)(2,1)}, u32[]{:S(2)}, u32[]{:S(2)}) async-start(bf16[32,128,128]{2,1,0:T(8,128)(2,1)} %bitcast.32), calls=%async_computation.7 | async-start | bytes 2097152 | tf_op jit(solution)/shard_map/all_to_all | solution.py:459
  372.5 5.7 copy-start.9
  391.5 75.5 %all-to-all-start.8 = ((bf16[32,384,128]{2,1,0:T(8,128)(2,1)}), bf16[32,384,128]{2,1,0:T(8,128)(2,1)}, u32[]{:S(2)}, u32[]{:S(2)}) async-start(bf16[32,384,128]{2,1,0:T(8,128)(2,1)} %pad_maximum_fusion), calls=%async_computation.8 | async-start | bytes 6291456 | tf_op jit(solution)/shard_map/all_to_all | solution.py:484
  467.6 16.9 %all-to-all-start.12 = ((bf16[32,16,128]{2,1,0:T(8,128)(2,1)}), bf16[32,16,128]{2,1,0:T(8,128)(2,1)S(1)}, u32[]{:S(2)}, u32[]{:S(2)}) async-start(bf16[32,16,128]{2,1,0:T(8,128)(2,1)} %broadcast_in_dim.28), calls=%async_computation.12 | async-start | bytes 262144 | tf_op jit(solution)/shard_map/all_to_all | solution.py:512
  498.7 9.0 %copy-start.14 = (f32[128,8,128]{2,1,0:T(8,128)S(1)}, f32[128,8,128]{2,1,0:T(8,128)}, u32[]{:S(2)}) copy-start(f32[128,8,128]{2,1,0:T(8,128)} %param.32) | copy-start | bytes 1572868
  498.7 34.7 %all-to-all-start.13 = ((bf16[32,160,128]{2,1,0:T(8,128)(2,1)}), bf16[32,160,128]{2,1,0:T(8,128)(2,1)S(1)}, u32[]{:S(2)}, u32[]{:S(2)}) async-start(bf16[32,160,128]{2,1,0:T(8,128)(2,1)} %broadcast_in_dim.29), calls=%async_computation.13 | async-start | bytes 2621440 | tf_op jit(solution)/shard_map/all_to_all | solution.py:512
  541.1 8.0 %copy-start.42 = (f32[5,256]{1,0:T(8,128)S(1)}, f32[5,256]{1,0:T(8,128)}, u32[]{:S(2)}) copy-start(f32[5,256]{1,0:T(8,128)} %param.45) | copy-start | bytes 15364
  541.1 8.0 %copy-start.43 = (f32[5,256]{1,0:T(8,128)S(1)}, f32[5,256]{1,0:T(8,128)}, u32[]{:S(2)}) copy-start(f32[5,256]{1,0:T(8,128)} %param.46) | copy-start | bytes 15364
  541.1 9.3 %copy-start.35 = (f32[9517]{0:T(1024)S(1)}, f32[9517]{0:T(1024)}, u32[]{:S(2)}) copy-start(f32[9517]{0:T(1024)} %param.47) | copy-start | bytes 114208
  541.2 9.3 %copy-start.39 = (f32[9517]{0:T(1024)S(1)}, f32[9517]{0:T(1024)}, u32[]{:S(2)}) copy-start(f32[9517]{0:T(1024)} %param.48) | copy-start | bytes 114208
  541.2 9.3 %copy-start.40 = (f32[9517]{0:T(1024)S(1)}, f32[9517]{0:T(1024)}, u32[]{:S(2)}) copy-start(f32[9517]{0:T(1024)} %param.49) | copy-start | bytes 114208
  (32 other events, 96.4 us)
Sparse Core Ops, SparseCore 0:
  22.3 60.8 all-gather.1

commit v2 on v1

--- a/solution.py
+++ b/solution.py
@@ -47,11 +47,6 @@
         first_next,
         second_next,
     )
-
-
-def gelu_pair(value):
-    result, back = jax.vjp(jax.nn.gelu, value)
-    return (result, back(jnp.ones_like(value))[0])
 
 
 def route_kernel(row_bits, ids_ref, out_ref, place_ref, slot_ref):
@@ -104,34 +99,41 @@
     return lax.broadcasted_iota(I32, shape, len(shape) - 1) < 64
 
 
-def find_kernel(groups, code_bits, codes_ref, table_ref, out_ref, rows_ref):
-    group = pl.program_id(0)
+def find_kernel(groups, group_rows, code_bits, codes_ref, table_ref, out_ref, rows_ref):
     blocks, _, height, lanes = out_ref.shape
     mask = (1 << code_bits) - 1
     left = left_lanes((1, lanes))
 
-    def fetch(code, side):
+    def fetch(code, base, side):
         at = jnp.maximum((code & 65535) - 1, 0)
-        row = table_ref[pl.ds(at & mask, 1), :]
-        return pltpu.roll(row, ((at >> code_bits) ^ side) * 64, 1)
-
-    def block_step(block, _):
-        source = block * groups + group
+        row = table_ref[pl.ds((at & mask) + base, 1), :]
+        return row, ((at >> code_bits) ^ side) * 64
+
+    def source_step(source, _):
         count = codes_ref[source, 0] >> 16
+        group = lax.rem(source, groups)
+        base = group * group_rows
 
         def step(outer, _):
+            got = []
             for inner in range(8):
                 at = outer * 8 + inner
-                even = fetch(codes_ref[source, 2 * at], 0)
-                odd = fetch(codes_ref[source, 2 * at + 1], 1)
-                rows_ref[pl.ds(at, 1), :] = jnp.where(left, even, odd)
+                even = fetch(codes_ref[source, 2 * at], base, 0)
+                odd = fetch(codes_ref[source, 2 * at + 1], base, 1)
+                got.append((at, even, odd))
+            got = [
+                (at, jnp.where(left, pltpu.roll(*even, 1), pltpu.roll(*odd, 1)))
+                for at, even, odd in got
+            ]
+            for at, row in got:
+                rows_ref[pl.ds(at, 1), :] = row
             return 0
 
         lax.fori_loop(0, (count + 15) // 16, step, 0)
-        out_ref[block, 0] = rows_ref[...].astype(LOW)
+        out_ref[lax.div(source, groups), group] = rows_ref[...].astype(LOW)
         return 0
 
-    lax.fori_loop(0, blocks, block_step, 0)
+    lax.fori_loop(0, blocks * groups, source_step, 0)
 
 
 def place_kernel(place_ref, rows_ref, out_ref, both_ref, flat_ref):
@@ -143,12 +145,15 @@
     left = left_lanes((1, lanes))
 
     def step(outer, _):
+        got = []
         for inner in range(8):
             sample = outer * 8 + inner
             for pair in range(tables // 2):
                 even = both_ref[pl.ds(place_ref[2 * pair, sample], 1), :]
                 odd = both_ref[pl.ds(place_ref[2 * pair + 1, sample], 1), :]
-                flat_ref[pair, pl.ds(sample, 1), :] = jnp.where(left, even, odd)
+                got.append((pair, sample, jnp.where(left, even, odd)))
+        for pair, sample, row in got:
+            flat_ref[pair, pl.ds(sample, 1), :] = row
         return 0
 
     lax.fori_loop(0, samples // 8, step, 0)
@@ -166,14 +171,17 @@
     bits = count.bit_length() - 1
 
     def step(outer, _):
+        got = []
         for inner in range(8):
             sample = outer * 8 + inner
             for table in range(tables):
                 slot = slot_ref[table, sample]
                 turned = (slot >> bits) ^ (table % 2)
-                rows_ref[pl.ds(slot, 1), :] = both_ref[
-                    table // 2, pl.ds(turned * samples + sample, 1), :
-                ]
+                got.append(
+                    (slot, both_ref[table // 2, pl.ds(turned * samples + sample, 1), :])
+                )
+        for slot, row in got:
+            rows_ref[pl.ds(slot, 1), :] = row
         return 0
 
     lax.fori_loop(0, samples // 8, step, 0)
@@ -212,6 +220,7 @@
 
         def step(outer, _):
             for inner in range(4):
+                got = []
                 for group in range(groups):
                     source = block * groups + group
                     code = codes_ref[source, outer * 4 + inner] & 65535
@@ -221,7 +230,9 @@
                     part = part + outer * 2 + inner // 2
                     part = jnp.where(code > 0, part, 4 * count)
                     here = pl.ds(at & mask, 1)
-                    sums[group][here, :] = sums[group][here, :] + parts_ref[pl.ds(part, 1), :]
+                    got.append((here, sums[group][here, :] + parts_ref[pl.ds(part, 1), :]))
+                for group, (here, row) in enumerate(got):
+                    sums[group][here, :] = row
             return 0
 
         lax.fori_loop(0, (most + 3) // 4, step, 0)
@@ -246,6 +257,415 @@
     square_ref[...] = lax.fori_loop(0, table_rows // 64, square, jnp.zeros((8, lanes), F32))
     for copy in copies:
         copy.wait()
+
+
+def gelu_parts(value):
+    scale = math.sqrt(2.0 / math.pi)
+    square = value * value
+    bend = jnp.tanh(scale * value * (1.0 + 0.044715 * square))
+    half = 0.5 * (1.0 + bend)
+    slope = half + 0.5 * value * (1.0 - bend * bend) * (scale * (1.0 + 3 * 0.044715 * square))
+    return value * half, slope
+
+
+def dot(a, b, axes=((1,), (0,)), precision=None):
+    return lax.dot_general(
+        a, b, (axes, ((), ())), preferred_element_type=F32, precision=precision
+    )
+
+
+NT = ((1,), (1,))
+TN = ((0,), (0,))
+MESH = pl.DeviceIdType.MESH
+
+
+def meet(peers):
+    me = lax.axis_index("mp")
+    barrier = pltpu.get_barrier_semaphore()
+    for step in range(1, peers):
+        pl.semaphore_signal(
+            barrier, inc=1, device_id={"mp": lax.rem(me + step, peers)}, device_id_type=MESH
+        )
+    pl.semaphore_wait(barrier, peers - 1)
+    return me
+
+
+def ahead_kernel(
+    count_ref,
+    x_ref,
+    w_ref,
+    b1_ref,
+    b2_ref,
+    wg_ref,
+    bg_ref,
+    w3_ref,
+    tb1_ref,
+    heads_ref,
+    tb2_ref,
+    labels_ref,
+    mask_ref,
+    blocks_ref,
+    hid_ref,
+    slope_ref,
+    dy_ref,
+    dgl_ref,
+    small_ref,
+    stats_ref,
+    y_send,
+    y_ref,
+    gates_ref,
+    mixb_ref,
+    dmix_ref,
+    dg_ref,
+    dy_send,
+    pack_ref,
+    act_ref,
+    x_out,
+    x_in,
+    y_out,
+    y_in,
+    d_out,
+    d_in,
+):
+    peers, samples, width = blocks_ref.shape
+    here = hid_ref.shape[0]
+    out_width = y_ref.shape[3]
+    own = y_ref.shape[2]
+    experts = peers * here
+    tasks, tower_hid = heads_ref.shape
+    shards, hid = w_ref.shape[1], w_ref.shape[3]
+    in_rows = peers * width // shards
+    me = meet(peers)
+
+    def other(step):
+        return lax.rem(me + step, peers)
+
+    def x_copy(turn, step):
+        target = other(step)
+        rows = pl.ds(pl.multiple_of(lax.rem(target + turn + 1, peers) * own, own), own)
+        return pltpu.make_async_remote_copy(
+            x_ref.at[rows],
+            blocks_ref.at[me, rows],
+            x_out.at[turn, step],
+            x_in.at[turn, step],
+            device_id={"mp": target},
+            device_id_type=MESH,
+        )
+
+    def y_copy(turn):
+        return pltpu.make_async_remote_copy(
+            y_send.at[turn],
+            y_ref.at[me],
+            y_out.at[turn],
+            y_in.at[turn],
+            device_id={"mp": other(turn + 1)},
+            device_id_type=MESH,
+        )
+
+    def d_copy(step):
+        target = other(step)
+        return pltpu.make_async_remote_copy(
+            dy_send.at[pl.ds(target * here, here)],
+            dy_ref.at[:, pl.ds(pl.multiple_of(me * own, own), own), :],
+            d_out.at[step],
+            d_in.at[step],
+            device_id={"mp": target},
+            device_id_type=MESH,
+        )
+
+    for turn in range(peers):
+        for step in range(1, peers):
+            x_copy(turn, step).start()
+    blocks_ref[me] = x_ref[...]
+    limit = count_ref[0]
+
+    def expert_step(turn, _):
+        for step in range(1, peers):
+            x_copy(turn, step).wait_recv()
+        chunk = lax.rem(me + turn + 1, peers)
+        rows = pl.ds(pl.multiple_of(chunk * own, own), own)
+        x = jnp.concatenate([blocks_ref[block, rows] for block in range(peers)], axis=1)
+        for e in range(here):
+            w_in = w_ref[e, :, :in_rows, :].reshape(peers * width, hid)
+            act_ref[...] = dot(x, w_in) + b1_ref[e]
+
+            def gelu_step(tile, _):
+                at = pl.multiple_of(tile * 32, 32)
+                value, slope = gelu_parts(act_ref[pl.ds(at, 32), :])
+                there = pl.ds(pl.multiple_of(chunk * own + at, 32), 32)
+                hid_ref[e, there, :] = value.astype(LOW)
+                slope_ref[e, there, :] = slope
+                return 0
+
+            lax.fori_loop(0, own // 32, gelu_step, 0)
+            w_out = w_ref[e, :, in_rows:, :].reshape(out_width, hid)
+            y_send[turn, e] = (dot(hid_ref[e, rows, :], w_out, NT) + b2_ref[e]).astype(LOW)
+
+        @pl.when(turn < peers - 1)
+        def _():
+            y_copy(turn).start()
+
+        return 0
+
+    lax.fori_loop(0, peers, expert_step, 0)
+    y_ref[me] = y_send[peers - 1]
+
+    own_rows = pl.ds(pl.multiple_of(me * own, own), own)
+    x_own = jnp.concatenate([blocks_ref[block, own_rows] for block in range(peers)], axis=1)
+    logits = dot(x_own, wg_ref[...], NT) + bg_ref[...]
+    for k in range(tasks):
+        part = logits[:, k * experts : (k + 1) * experts]
+        part = jnp.exp(part - jnp.max(part, axis=1, keepdims=True))
+        gates_ref[:, k * experts : (k + 1) * experts] = part / jnp.sum(part, axis=1, keepdims=True)
+
+    stats_ref[...] = jnp.zeros_like(stats_ref)
+
+    def square_step(tile, total):
+        at = pl.multiple_of(tile * 64, 64)
+        valid = (lax.broadcasted_iota(I32, (64, 1), 0) + at) < limit
+        part = jnp.where(valid, x_ref[pl.ds(at, 64), :].astype(F32), 0.0)
+        return total + jnp.sum((part * part).reshape(8, 8, width), axis=0)
+
+    x_square = lax.fori_loop(0, samples // 64, square_step, jnp.zeros((8, width), F32))
+    stats_ref[experts + tasks, :, :width] = x_square
+    for turn in range(peers - 1):
+        y_copy(turn).wait_recv()
+
+    tile_rows = 16
+
+    def tile_of(tile):
+        at = pl.multiple_of(tile * tile_rows, tile_rows)
+        return at, pl.ds(at, tile_rows)
+
+    def mix_step(tile, _):
+        at, rows = tile_of(tile)
+        valid = (lax.broadcasted_iota(I32, (tile_rows, 1), 0) + (at + me * own)) < limit
+        gates = gates_ref[rows, :]
+        mixed = [None] * tasks
+        for e in range(experts):
+            y = y_ref[e // here, e % here, rows, :].astype(F32)
+            square = jnp.where(valid, y * y, 0.0)
+            stats_ref[e] += square[:8] + square[8:]
+            for k in range(tasks):
+                term = gates[:, k * experts + e : k * experts + e + 1] * y
+                mixed[k] = term if e == 0 else mixed[k] + term
+        for k in range(tasks):
+            square = jnp.where(valid, mixed[k] * mixed[k], 0.0)
+            stats_ref[experts + k] += square[:8] + square[8:]
+            mixb_ref[k, rows, :] = mixed[k].astype(LOW)
+        return 0
+
+    lax.fori_loop(0, own // tile_rows, mix_step, 0)
+
+    pack_ref[...] = jnp.zeros_like(pack_ref)
+    blocks_x = peers * width // 128
+    heads_at = blocks_x * tasks * experts
+    tower_at = heads_at + tasks * tower_hid // 128
+    outer_at = tower_at + tasks * tower_hid // 128
+    rest_at = outer_at + experts * out_width // 128
+    loss = jnp.zeros((1, 1), F32)
+    weight_sum = jnp.zeros((1, 1), F32)
+    row_id = lax.broadcasted_iota(I32, (own, 1), 0) + me * own
+    for k in range(tasks):
+        cols = slice(k * tower_hid, (k + 1) * tower_hid)
+        z, slope = gelu_parts(dot(mixb_ref[k], w3_ref[:, cols]) + tb1_ref[k : k + 1, :])
+        head = heads_ref[k : k + 1, :]
+        logit = jnp.sum(z * head, axis=1, keepdims=True) + tb2_ref[0, k]
+        small = jnp.exp(-jnp.abs(logit))
+        label = labels_ref[:, k : k + 1].astype(F32)
+        weight = jnp.where(row_id < limit, mask_ref[:, k : k + 1].astype(F32), 0.0)
+        soft = jnp.maximum(logit, 0.0) + jnp.log1p(small)
+        loss += jnp.sum(weight * (soft - label * logit), axis=0, keepdims=True)
+        weight_sum += jnp.sum(weight, axis=0, keepdims=True)
+        chance = jnp.where(logit >= 0.0, 1.0, small) / (1.0 + small)
+        dl = weight * (chance - label)
+        g_head = jnp.sum(dl * z, axis=0, keepdims=True)
+        dz = (dl * head * slope).astype(LOW)
+        g_bias = jnp.sum(dz.astype(F32), axis=0, keepdims=True)
+        for part in range(tower_hid // 128):
+            lane = slice(part * 128, (part + 1) * 128)
+            at = k * (tower_hid // 128) + part
+            pack_ref[heads_at + at : heads_at + at + 1, :] = g_head[:, lane]
+            pack_ref[tower_at + at : tower_at + at + 1, :] = g_bias[:, lane]
+        pack_ref[rest_at + 1 : rest_at + 2, k : k + 1] = jnp.sum(dl, axis=0, keepdims=True)
+        dmix_ref[k] = dot(dz, w3_ref[:, cols], NT)
+        small_ref[:, cols] = dot(mixb_ref[k], dz, TN).astype(LOW)
+    stats_ref[experts + tasks + 1, :1, :1] = loss
+    stats_ref[experts + tasks + 1, :1, 1:2] = weight_sum
+
+    def dy_step(tile, _):
+        at, rows = tile_of(tile)
+        gates = gates_ref[rows, :]
+        dmix = [dmix_ref[k, rows, :] for k in range(tasks)]
+        for e in range(experts):
+            total = None
+            for k in range(tasks):
+                term = gates[:, k * experts + e : k * experts + e + 1] * dmix[k]
+                total = term if k == 0 else total + term
+            dy_send[e, rows, :] = total.astype(LOW)
+        return 0
+
+    lax.fori_loop(0, own // tile_rows, dy_step, 0)
+    for step in range(1, peers):
+        d_copy(step).start()
+    dy_ref[:, own_rows, :] = dy_send[pl.ds(me * here, here)]
+    ones = jnp.ones((8, own), LOW)
+    for e in range(experts):
+        g_outer = dot(ones, dy_send[e])
+        for part in range(out_width // 128):
+            at = outer_at + e * (out_width // 128) + part
+            pack_ref[at : at + 1, :] = g_outer[:1, part * 128 : (part + 1) * 128]
+
+    lane = lax.broadcasted_iota(I32, (tile_rows, tasks * experts), 1)
+
+    def dg_step(tile, _):
+        at, rows = tile_of(tile)
+        dmix = [dmix_ref[k, rows, :] for k in range(tasks)]
+        found = jnp.zeros((tile_rows, tasks * experts), F32)
+        for e in range(experts):
+            y = y_ref[e // here, e % here, rows, :].astype(F32)
+            for k in range(tasks):
+                value = jnp.sum(dmix[k] * y, axis=1, keepdims=True)
+                found = jnp.where(lane == k * experts + e, value, found)
+        dg_ref[rows, :] = found
+        return 0
+
+    lax.fori_loop(0, own // tile_rows, dg_step, 0)
+    gates = gates_ref[...]
+    dg = dg_ref[...]
+    flat = (tasks * experts, tasks * experts)
+    same = lax.broadcasted_iota(I32, flat, 0) // experts == lax.broadcasted_iota(I32, flat, 1) // experts
+    mean = dot(gates * dg, same.astype(F32), precision=HIGH)
+    dgl = (gates * (dg - mean)).astype(LOW)
+    dgl_ref[...] = dgl
+    pack_ref[rest_at : rest_at + 1, : tasks * experts] = jnp.sum(
+        dgl.astype(F32), axis=0, keepdims=True
+    )
+    g_gating = dot(dgl, x_own, TN)
+    for part in range(blocks_x):
+        at = part * tasks * experts
+        pack_ref[at : at + tasks * experts, :] = g_gating[:, part * 128 : (part + 1) * 128]
+    small_ref[:, tasks * tower_hid :] = pack_ref[...].astype(LOW)
+
+    for turn in range(peers):
+        for step in range(1, peers):
+            x_copy(turn, step).wait_send()
+    for turn in range(peers - 1):
+        y_copy(turn).wait_send()
+    for step in range(1, peers):
+        d_copy(step).wait()
+
+
+def back_kernel(
+    dy_ref,
+    hid_ref,
+    slope_ref,
+    blocks_ref,
+    w_ref,
+    dgl_ref,
+    wg_ref,
+    dx_ref,
+    parts_ref,
+    b1_ref,
+    dpre_ref,
+    dx_send,
+    dx_recv,
+    x_out,
+    x_in,
+):
+    peers, samples, width = blocks_ref.shape
+    here, _, out_width = dy_ref.shape
+    own = samples // peers
+    hid = hid_ref.shape[2]
+    shards, rows_both = w_ref.shape[1], w_ref.shape[2]
+    in_rows = peers * width // shards
+    out_rows = rows_both - in_rows
+    features = peers * width
+    me = meet(peers)
+
+    def chunk_rows(turn):
+        return pl.ds(pl.multiple_of(lax.rem(me + turn, peers) * own, own), own)
+
+    def x_copy(turn, step):
+        target = lax.rem(me + step, peers)
+        rows = chunk_rows(turn)
+        return pltpu.make_async_remote_copy(
+            dx_send.at[target, rows],
+            dx_recv.at[me, rows],
+            x_out.at[turn, step],
+            x_in.at[turn, step],
+            device_id={"mp": target},
+            device_id_type=MESH,
+        )
+
+    b1_ref[...] = jnp.zeros_like(b1_ref)
+
+    def chunk_step(turn, _):
+        rows = chunk_rows(turn)
+        mine = jnp.where(turn == 0, 1.0, 0.0)
+        gate = (dgl_ref[...].astype(F32) * mine).astype(LOW)
+        total = dot(gate, wg_ref[...])
+        for e in range(here):
+            w_out = w_ref[e, :, in_rows:, :].reshape(out_width, hid)
+            dpre = (dot(dy_ref[e, rows, :], w_out) * slope_ref[e, rows, :]).astype(LOW)
+            dpre_ref[e, rows, :] = dpre
+            b1_ref[e] += dot(jnp.ones((8, own), LOW), dpre)
+            w_in = w_ref[e, :, :in_rows, :].reshape(features, hid)
+            total += dot(dpre, w_in, NT)
+        for target in range(peers):
+            dx_send[target, rows] = total[:, target * width : (target + 1) * width].astype(LOW)
+        for step in range(1, peers):
+            x_copy(turn, step).start()
+        return 0
+
+    lax.fori_loop(0, peers, chunk_step, 0)
+
+    lanes = parts_ref.shape[3]
+    blocks_in = width // 128
+    per_in = 128 // in_rows
+    per_out = 128 // out_rows
+    for e in range(here):
+
+        def in_step(block, _):
+            cols = pl.ds(pl.multiple_of(lax.rem(block, blocks_in) * 128, 128), 128)
+            x = blocks_ref[lax.div(block, blocks_in), :, cols]
+            value = dot(x, dpre_ref[e], TN).astype(LOW)
+            for shard in range(per_in):
+                for target in range(peers):
+                    parts_ref[
+                        block * per_in + shard, target, e * rows_both : e * rows_both + in_rows, :
+                    ] = value[
+                        shard * in_rows : (shard + 1) * in_rows, target * lanes : (target + 1) * lanes
+                    ]
+            return 0
+
+        lax.fori_loop(0, features // 128, in_step, 0)
+
+        def out_step(block, _):
+            cols = pl.ds(pl.multiple_of(block * 128, 128), 128)
+            value = dot(dy_ref[e, :, cols], hid_ref[e], TN).astype(LOW)
+            for shard in range(per_out):
+                for target in range(peers):
+                    parts_ref[
+                        block * per_out + shard,
+                        target,
+                        e * rows_both + in_rows : (e + 1) * rows_both,
+                        :,
+                    ] = value[
+                        shard * out_rows : (shard + 1) * out_rows,
+                        target * lanes : (target + 1) * lanes,
+                    ]
+            return 0
+
+        lax.fori_loop(0, out_width // 128, out_step, 0)
+
+    for turn in range(peers):
+        for step in range(1, peers):
+            x_copy(turn, step).wait()
+    total = dx_send[me].astype(F32)
+    for step in range(1, peers):
+        total = total + dx_recv[lax.rem(me + step, peers)].astype(F32)
+    dx_ref[...] = total
 
 
 def table_kernel(factor_ref, weight_ref, first_ref, second_ref, grad_ref, *outs):
@@ -325,8 +745,7 @@
     shard = jnp.concatenate([expert_in, expert_out], axis=0).astype(LOW)
     shard = lax.all_to_all(shard, "mp", split_axis=1, concat_axis=2, tiled=True)
     gathered = lax.all_gather(shard, "dp", axis=0, tiled=False)
-    w_in = gathered[:, :in_rows].reshape(in_rows * dp_count, experts_here, hid)
-    w_out = gathered[:, in_rows:].reshape(width_out, experts_here, hid)
+    expert_w = jnp.transpose(gathered, (2, 0, 1, 3))
 
     table_view = jnp.transpose(embeddings, (0, 2, 1))
     turned = pl.pallas_call(
@@ -339,11 +758,10 @@
         name="turn",
     )(table_view)
     found = pl.pallas_call(
-        functools.partial(find_kernel, mp_count, code_bits),
-        grid=(mp_count,),
+        functools.partial(find_kernel, mp_count, group_rows, code_bits),
         out_shape=jax.ShapeDtypeStruct((dp_count, mp_count, height, lanes), LOW),
-        in_specs=[SMEM, pl.BlockSpec((group_rows, lanes), lambda m: (m, 0))],
-        out_specs=pl.BlockSpec((dp_count, 1, height, lanes), lambda m: (0, m, 0, 0)),
+        in_specs=[SMEM, VMEM],
+        out_specs=VMEM,
         scratch_shapes=[pltpu.VMEM((height, lanes), F32)],
         compiler_params=params(32),
         name="find",
@@ -364,85 +782,102 @@
         name="place",
     )(place, returned.reshape(slots, lanes))
 
-    valid_all = (jnp.arange(samples, dtype=I32) < counts[lax.axis_index("dp")]).astype(F32)
-    own_start = mp_index * own
-    valid_own = lax.dynamic_slice_in_dim(valid_all, own_start, own, 0)
-    embed_float = embedded.astype(F32)
-    input_sq = jnp.sum(valid_all[:, None] * embed_float * embed_float)
     first = EXPERTS * hid
     second = first + EXPERTS * width_out
     third = second + TASKS * EXPERTS
     fourth = third + TASKS * tower_hid
-    inner_bias = biases[:first].reshape(mp_count, experts_here, hid)
-    outer_bias = biases[first:second].reshape(mp_count, experts_here, width_out)
-    gate_bias = biases[second:third]
-    tower_bias = biases[third:fourth].reshape(TASKS, tower_hid)
-    head_bias = biases[fourth:]
-    inner_here = lax.dynamic_index_in_dim(inner_bias, mp_index, 0, keepdims=False)
-    outer_here = lax.dynamic_index_in_dim(outer_bias, mp_index, 0, keepdims=False)
-
-    def exchange(parts):
-        return lax.all_to_all(parts, "mp", split_axis=0, concat_axis=0, tiled=True)
-
-    blocks = exchange(jnp.broadcast_to(embedded[None], (mp_count,) + embedded.shape))
-    inputs = jnp.transpose(blocks, (1, 0, 2)).reshape(samples, features)
-    own_inputs = lax.dynamic_slice_in_dim(inputs, own_start, own, 0)
-    preact = jnp.einsum("si,ieh->seh", inputs, w_in, preferred_element_type=F32) + inner_here
-    hidden_float, hidden_slope = gelu_pair(preact)
-    hidden = hidden_float.astype(LOW)
-    partial_y = jnp.einsum("seh,oeh->eso", hidden, w_out, preferred_element_type=F32)
-    partial_y = (partial_y + outer_here[:, None, :]).astype(LOW)
-    partial_y = partial_y.reshape(experts_here, mp_count, own, width_out).transpose(1, 0, 2, 3)
-    expert_y = exchange(partial_y).reshape(EXPERTS, own, width_out).astype(F32)
-
-    gating_low = gating.astype(LOW)
-    gate_logit = jnp.dot(own_inputs, gating_low, preferred_element_type=F32) + gate_bias
-    gates = jax.nn.softmax(gate_logit.reshape(own, TASKS, EXPERTS), axis=-1)
-    mixed = jnp.einsum("ske,eso->sko", gates, expert_y, precision=HIGH)
-    mixed_low = mixed.astype(LOW)
-    tower_low = towers.astype(LOW).reshape(width_out, TASKS, tower_hid)
-    tower_pre = (
-        jnp.einsum("sko,okj->skj", mixed_low, tower_low, preferred_element_type=F32) + tower_bias
-    )
-    tower_act, tower_slope = gelu_pair(tower_pre)
-    logits = jnp.sum(tower_act * heads, axis=-1) + head_bias
-    target_float = labels.astype(F32)
-    weights = valid_own[:, None] * label_mask.astype(F32)
-    loss_here = jnp.sum(weights * (jax.nn.softplus(logits) - target_float * logits))
-    expert_sq = jnp.sum(valid_own[None, :, None] * expert_y * expert_y, axis=(1, 2))
-    mixed_sq = jnp.sum(valid_own[:, None, None] * mixed * mixed, axis=(0, 2))
-    logit_grad = weights * (jax.nn.sigmoid(logits) - target_float)
-    heads_grad = jnp.einsum("sk,skj->kj", logit_grad, tower_act, precision=HIGH)
-    head_bias_grad = jnp.sum(logit_grad, axis=0)
-    tower_grad = (logit_grad[:, :, None] * heads * tower_slope).astype(LOW)
-    towers_grad = jnp.einsum(
-        "sko,skj->okj", mixed_low, tower_grad, preferred_element_type=F32
-    ).reshape(width_out, TASKS * tower_hid)
-    tower_bias_grad = jnp.sum(tower_grad.astype(F32), axis=0)
-    mixed_grad = jnp.einsum("skj,okj->sko", tower_grad, tower_low, preferred_element_type=F32)
-    gate_grad = jnp.einsum("sko,eso->ske", mixed_grad, expert_y, precision=HIGH)
-    gate_logit_grad = gates * (gate_grad - jnp.sum(gates * gate_grad, axis=-1, keepdims=True))
-    gate_logit_grad = gate_logit_grad.reshape(own, TASKS * EXPERTS).astype(LOW)
-    output_grad = jnp.einsum("ske,sko->eso", gates, mixed_grad, precision=HIGH).astype(LOW)
-    gating_grad = jnp.einsum("si,sk->ki", own_inputs, gate_logit_grad, preferred_element_type=F32)
-    gate_bias_grad = jnp.sum(gate_logit_grad.astype(F32), axis=0)
-    outer_bias_grad = jnp.sum(output_grad.astype(F32), axis=1)
-    input_gate_grad = jnp.einsum(
-        "sk,ik->si", gate_logit_grad, gating_low, preferred_element_type=F32
-    )
-    output_rows = exchange(output_grad.reshape(mp_count, experts_here, own, width_out))
-    output_rows = output_rows.transpose(1, 0, 2, 3).reshape(experts_here, samples, width_out)
-
-    hidden_grad = jnp.einsum("eso,oeh->seh", output_rows, w_out, preferred_element_type=F32)
-    preact_grad = (hidden_grad * hidden_slope).astype(LOW)
-    out_grad = jnp.einsum("eso,seh->oeh", output_rows, hidden, preferred_element_type=F32)
-    in_grad = jnp.einsum("si,seh->ieh", inputs, preact_grad, preferred_element_type=F32)
-    inner_bias_part = jnp.sum(preact_grad.astype(F32), axis=0)
-    input_grad = jnp.einsum("seh,ieh->si", preact_grad, w_in, preferred_element_type=F32)
-    own_part = lax.dynamic_slice_in_dim(input_grad, own_start, own, 0) + input_gate_grad
-    input_grad = lax.dynamic_update_slice_in_dim(input_grad, own_part, own_start, 0)
-    input_parts = input_grad.astype(LOW).reshape(samples, mp_count, tables_here * d_emb)
-    embed_grad = jnp.sum(exchange(input_parts.transpose(1, 0, 2)).astype(F32), axis=0)
+    inner_here = lax.dynamic_index_in_dim(
+        biases[:first].reshape(mp_count, experts_here, 1, hid), mp_index, 0, keepdims=False
+    )
+    outer_here = lax.dynamic_index_in_dim(
+        biases[first:second].reshape(mp_count, experts_here, 1, width_out),
+        mp_index,
+        0,
+        keepdims=False,
+    )
+    gating_low = gating.T.astype(LOW)
+    all_gates = TASKS * EXPERTS
+    pack_rows = width_out
+
+    def scratch(shape, kind=F32):
+        return pltpu.VMEM(shape, kind)
+
+    def sems(*shape):
+        return pltpu.SemaphoreType.DMA(shape)
+
+    blocks, hidden, slopes, output_rows, gate_logit_grad, small_grads, stat_parts = pl.pallas_call(
+        ahead_kernel,
+        out_shape=(
+            jax.ShapeDtypeStruct((mp_count, samples, tables_here * d_emb), LOW),
+            jax.ShapeDtypeStruct((experts_here, samples, hid), LOW),
+            jax.ShapeDtypeStruct((experts_here, samples, hid), F32),
+            jax.ShapeDtypeStruct((experts_here, samples, width_out), LOW),
+            jax.ShapeDtypeStruct((own, all_gates), LOW),
+            jax.ShapeDtypeStruct((pack_rows, TASKS * tower_hid + 128), LOW),
+            jax.ShapeDtypeStruct((EXPERTS + TASKS + 2, 8, width_out), F32),
+        ),
+        in_specs=[SMEM] + [VMEM] * 9 + [SMEM] + [VMEM] * 2,
+        out_specs=(VMEM,) * 7,
+        scratch_shapes=[
+            scratch((mp_count, experts_here, own, width_out), LOW),
+            scratch((mp_count, experts_here, own, width_out), LOW),
+            scratch((own, all_gates)),
+            scratch((TASKS, own, width_out), LOW),
+            scratch((TASKS, own, width_out)),
+            scratch((own, all_gates)),
+            scratch((EXPERTS, own, width_out), LOW),
+            scratch((pack_rows, 128)),
+            scratch((own, hid)),
+            sems(mp_count, mp_count),
+            sems(mp_count, mp_count),
+            sems(mp_count),
+            sems(mp_count),
+            sems(mp_count),
+            sems(mp_count),
+        ],
+        compiler_params=pltpu.CompilerParams(
+            vmem_limit_bytes=56 * MIB, collective_id=0, has_side_effects=True
+        ),
+        name="ahead",
+    )(
+        lax.dynamic_slice_in_dim(counts, lax.axis_index("dp"), 1, 0),
+        embedded,
+        expert_w,
+        inner_here,
+        outer_here,
+        gating_low,
+        biases[second:third].reshape(1, all_gates),
+        towers.astype(LOW),
+        biases[third:fourth].reshape(TASKS, tower_hid),
+        heads,
+        biases[fourth:].reshape(1, TASKS),
+        labels,
+        label_mask,
+    )
+    in_out_rows = in_rows + out_rows
+    embed_grad, grad_parts, inner_parts = pl.pallas_call(
+        back_kernel,
+        out_shape=(
+            jax.ShapeDtypeStruct((samples, tables_here * d_emb), F32),
+            jax.ShapeDtypeStruct(
+                (dp_count, mp_count, experts_here * in_out_rows, hid // mp_count), LOW
+            ),
+            jax.ShapeDtypeStruct((experts_here, 8, hid), F32),
+        ),
+        in_specs=[VMEM] * 7,
+        out_specs=(VMEM,) * 3,
+        scratch_shapes=[
+            scratch((experts_here, samples, hid), LOW),
+            scratch((mp_count, samples, tables_here * d_emb), LOW),
+            scratch((mp_count, samples, tables_here * d_emb), LOW),
+            sems(mp_count, mp_count),
+            sems(mp_count, mp_count),
+        ],
+        compiler_params=pltpu.CompilerParams(
+            vmem_limit_bytes=56 * MIB, collective_id=1, has_side_effects=True
+        ),
+        name="back",
+    )(output_rows, hidden, slopes, blocks, expert_w, gate_logit_grad, gating_low)
 
     back_rows = pl.pallas_call(
         send_kernel,
@@ -476,69 +911,58 @@
         name="add",
     )(codes, arrived.reshape(slots, lanes))
 
-    def scatter_grad(grad, rows):
-        parts = grad.astype(LOW).reshape(dp_count, rows, experts_here, mp_count, hid // mp_count)
-        return parts.transpose(0, 3, 1, 2, 4).reshape(devices, rows * experts_here, hid // mp_count)
-
-    grad_parts = jnp.concatenate([scatter_grad(in_grad, in_rows), scatter_grad(out_grad, out_rows)], 1)
-    grad_parts = lax.all_to_all(grad_parts, AXES, split_axis=0, concat_axis=0, tiled=True)
+    def exchange_all(parts):
+        return lax.all_to_all(parts, AXES, split_axis=0, concat_axis=0, tiled=True)
+
+    small_grads = small_grads.reshape(devices, pack_rows // devices, -1)
+    share = jnp.sum(exchange_all(small_grads).astype(F32), axis=0)
+    share_sq = jnp.sum(share * share)
+    whole = exchange_all(jnp.broadcast_to(share.astype(LOW)[None], small_grads.shape))
+    whole = whole.reshape(pack_rows, -1)
+    towers_sum = whole[:, : TASKS * tower_hid].astype(F32)
+    packed = whole[:, TASKS * tower_hid :].astype(F32)
+    blocks_x = features // 128
+    heads_at = blocks_x * all_gates
+    tower_at = heads_at + TASKS * tower_hid // 128
+    outer_at = tower_at + TASKS * tower_hid // 128
+    rest_at = outer_at + EXPERTS * width_out // 128
+    gating_sum = packed[:heads_at].reshape(blocks_x, all_gates, 128).transpose(1, 0, 2)
+    gating_sum = gating_sum.reshape(all_gates, features).T
+    heads_sum = packed[heads_at:tower_at].reshape(TASKS, tower_hid)
+
+    grad_parts = exchange_all(
+        grad_parts.reshape(devices, experts_here * in_out_rows, hid // mp_count)
+    )
     grad_sum = jnp.sum(
-        grad_parts.reshape(dp_count, mp_count, in_rows + out_rows, experts_here, -1).astype(F32), 0
-    )
-    grad_sum = grad_sum.transpose(1, 0, 2, 3).reshape(in_rows + out_rows, EXPERTS, -1)
+        grad_parts.reshape(dp_count, mp_count, experts_here, in_out_rows, -1).astype(F32), 0
+    )
+    grad_sum = grad_sum.reshape(EXPERTS, in_out_rows, -1).transpose(1, 0, 2)
     in_sum, out_sum = grad_sum[:in_rows], grad_sum[in_rows:]
 
-    inner_bias_grad = lax.dynamic_update_slice_in_dim(
-        jnp.zeros((mp_count, experts_here, hid), F32), inner_bias_part[None], mp_index, 0
-    )
-    bias_grad = jnp.concatenate(
+    squares = jnp.sum(table_sq) + jnp.sum(grad_sum * grad_sum) + share_sq
+    stat_end = EXPERTS + TASKS
+    stat_sums = jnp.sum(stat_parts[: stat_end + 1], axis=(1, 2))
+    scalars = jnp.concatenate(
+        [stat_parts[stat_end + 1, 0, :2], stat_sums, squares[None]]
+    )
+    scalars = jnp.pad(scalars, (0, 128 - scalars.size))[None]
+    final = jnp.concatenate(
+        [inner_parts[:, 0, :].reshape(-1, 128), scalars], axis=0
+    )
+    final = exchange_all(jnp.broadcast_to(final[None], (devices,) + final.shape))
+    sums = jnp.sum(final[:, -1, :], axis=0)
+    inner_sum = jnp.sum(final[:, :-1, :].reshape(dp_count, -1), axis=0)
+    bias_sum = jnp.concatenate(
         [
-            inner_bias_grad.reshape(-1),
-            outer_bias_grad.reshape(-1),
-            gate_bias_grad,
-            tower_bias_grad.reshape(-1),
-            head_bias_grad,
+            inner_sum,
+            packed[outer_at:rest_at].reshape(-1),
+            packed[rest_at, :all_gates],
+            packed[tower_at:outer_at].reshape(-1),
+            packed[rest_at + 1, :TASKS],
         ]
     )
-
-    def sum_over_all(value):
-        size = value.size
-        unit = devices * 1024
-        padded = jnp.pad(value.reshape(-1), (0, -size % unit)).reshape(devices, -1, 128)
-        parts = lax.all_to_all(padded.astype(LOW), AXES, split_axis=0, concat_axis=0, tiled=True)
-        share = jnp.sum(parts.astype(F32), axis=0)
-        share_sq = jnp.sum(share * share)
-        spread = jnp.broadcast_to(share.astype(LOW)[None], padded.shape)
-        whole = lax.all_to_all(spread, AXES, split_axis=0, concat_axis=0, tiled=True)
-        return whole.astype(F32).reshape(-1)[:size].reshape(value.shape), share_sq
-
-    towers_sum, towers_sq = sum_over_all(towers_grad)
-    rest, rest_sq = sum_over_all(
-        jnp.concatenate([gating_grad.reshape(-1), heads_grad.reshape(-1), bias_grad])
-    )
-    gating_sum = rest[: gating_grad.size].reshape(gating_grad.shape).T
-    heads_sum = rest[gating_grad.size : gating_grad.size + heads_grad.size].reshape(heads.shape)
-    bias_sum = rest[gating_grad.size + heads_grad.size :]
-    squares = (
-        jnp.sum(table_sq) + jnp.sum(in_sum * in_sum) + jnp.sum(out_sum * out_sum) + towers_sq + rest_sq
-    )
-    sums_here = jnp.concatenate(
-        [loss_here[None], input_sq[None], expert_sq, mixed_sq, jnp.sum(weights)[None], squares[None]]
-    )
-    sums_here = jnp.pad(sums_here, (0, 128 - sums_here.size))
-    sums = jnp.sum(
-        lax.all_to_all(
-            jnp.broadcast_to(sums_here, (devices, 1, 128)),
-            AXES,
-            split_axis=0,
-            concat_axis=0,
-            tiled=True,
-        ),
-        axis=(0, 1),
-    )
-    stat_end = 2 + EXPERTS + TASKS
-    weight_total = sums[stat_end]
-    grad_norm = jnp.sqrt(sums[stat_end + 1]) / weight_total
+    weight_total = sums[1]
+    grad_norm = jnp.sqrt(sums[stat_end + 3] + jnp.sum(inner_sum * inner_sum)) / weight_total
     factor = jnp.minimum(1.0, clip_max / grad_norm) / weight_total
 
     table_spec = pl.BlockSpec((2, d_emb, rows_dev // 2), lambda p, c: (p, 0, c))
@@ -574,7 +998,8 @@
     widths = jnp.concatenate(
         [jnp.full((1,), features, F32), jnp.full((EXPERTS + TASKS,), width_out, F32)]
     )
-    stats = jnp.sqrt(sums[1:stat_end] / (n_valid * widths) + stat_eps)
+    mean_sq = jnp.concatenate([sums[stat_end + 2][None], sums[2 : stat_end + 2]])
+    stats = jnp.sqrt(mean_sq / (n_valid * widths) + stat_eps)
     loss = jnp.stack([sums[0], weight_total])
     return (
         *embed_out,

time: 611 us -> 519 us (0.85)
  Pallas kernels: 153 us -> 281 us
  local copies, waits for them, and re-layouts: 88.1 us -> 32.1 us
  matrix products: 54.4 us -> 0 us
  waiting for transfers between devices: 116 us -> 68.5 us
  other arithmetic: 55.3 us -> 27.6 us
  blocking collectives: 68.7 us -> 50.7 us
  starting transfers between devices: 44.1 us -> 33.5 us
    pallas_call x1 -> x3, Pallas kernels: 32 us -> 157 us  [the longest x1 75.3 us: body(): pl.pallas_call(ahead_kernel, out_shape=(jax.ShapeDtypeStruct((mp_count, s...]
    all_to_all x9 -> x4, waiting for transfers between devices: 114 us -> 43.1 us  [the longest x3 25.1 us: exchange_all(): return lax.all_to_all(parts, AXES, split_axis=0, concat_axis=0, tiled=True)]
    dot_general x16 -> x0, matrix products: 54.4 us -> none  [the longest x1 7.49 us: body(): gate_grad = jnp.einsum('sko,eso->ske', mixed_grad, expert_y, precision=HIGH)]
    all_to_all x1, waiting for transfers between devices: 2.89 us -> 25.4 us  [body(): lax.all_to_all(back_rows.reshape(devices, height, lanes), AXES, split_axi...]
    all_to_all x2 -> x1, blocking collectives: 57.2 us -> 39.2 us  [exchange_all(): return lax.all_to_all(parts, AXES, split_axis=0, concat_axis=0, tiled=True)]
    reshape x13 -> x6, local copies, waits for them, and re-layouts: 22 us -> 4.98 us  [the longest x1 1.59 us: body(): grad_sum = grad_sum.reshape(EXPERTS, in_out_rows, -1).transpose(1, 0, 2)]
    reduce_sum x13 -> x8, other arithmetic: 17 us -> 3.87 us  [the longest x2 2.3 us: body(): squares = jnp.sum(table_sq) + jnp.sum(grad_sum * grad_sum) + share_sq]
    all_to_all x9 -> x4, starting transfers between devices: 35.6 us -> 22.6 us  [the longest x3 15.2 us: exchange_all(): return lax.all_to_all(parts, AXES, split_axis=0, concat_axis=0, tiled=True)]
  transfers between devices with their start and end apart: 12 -> 7, of which waited for: 9 -> 4; matrix products, arithmetic and copies ran while one was open for 18% -> 3% of each run, Pallas kernels for 16% -> 29%
where the time goes in v2:
time: 519 us; the launch traced here: 515 us
  Pallas kernels  281 us (54%)
  waiting for transfers between devices  68.5 us (13%)
  blocking collectives  50.7 us (10%)
  starting transfers between devices  33.5 us (6%)
  local copies, waits for them, and re-layouts  32.1 us (6%)
  other arithmetic  27.6 us (5%)
  between operations  21.6 us (4%)
    pallas_call x1, Pallas kernels, body(): pl.pallas_call(ahead_kernel, out_shape=(jax.ShapeDtypeStruct((mp_count, s...  75.3 us
    pallas_call x1, Pallas kernels, body(): pl.pallas_call(functools.partial(add_kernel, mp_count, code_bits), out_sh...  49.5 us
    pallas_call x1, Pallas kernels, body(): pl.pallas_call(table_kernel, grid=(pairs, 2), out_shape=(jax.ShapeDtypeSt...  43.1 us
    pallas_call x1, Pallas kernels, body(): pl.pallas_call(back_kernel, out_shape=(jax.ShapeDtypeStruct((samples, tab...  41.9 us
    pallas_call x1, Pallas kernels, body(): pl.pallas_call(functools.partial(find_kernel, mp_count, group_rows, code_...  39.5 us
    all_to_all x1, blocking collectives, exchange_all(): return lax.all_to_all(parts, AXES, split_axis=0, concat_axis=0, tiled=True)  39.2 us
    all_to_all x1, waiting for transfers between devices, body(): lax.all_to_all(back_rows.reshape(devices, height, lanes), AXES, split_axi...  25.4 us
    all_to_all x3, waiting for transfers between devices, exchange_all(): return lax.all_to_all(parts, AXES, split_axis=0, concat_axis=0, tiled=True)  25.1 us
  transfers between devices with their start and end apart: 7, of which 4 were waited for; matrix products, arithmetic and copies ran while one was open for 3% of the time, Pallas kernels for 29%

profile of v2, /device:TPU:0, one launch (start us, length us, event | category | flops | bytes accessed | tf_op | source)
XLA Modules:
  0.0 515.2 jit_solution(15657472703046803758)
XLA Ops:
  9.4 11.5 %all_to_all.50 = bf16[192,8,128]{2,0,1:T(8,128)(2,1)S(1)} all-to-all(bf16[192,8,128]{2,0,1:T(8,128)(2,1)S(1)} %pad_maximum_fusion), channel_id=1, replica_groups=mesh['dp'=8,'mp'=4] {'mp'}, dimensions={1} | all-to-all | bytes 786432 | tf_op jit(solution)/shard_map/all_to_all | solution.py:746
  22.2 2.0 route.1
  24.8 4.9 all-to-all-start
  29.7 10.2 %turn.1 = f32[8,4096,128]{2,1,0:T(8,128)S(1)} custom-call(f32[16,64,4096]{2,1,0:T(8,128)} %bitcast.93), custom_call_target="tpu_custom_call" | custom-call | tf_op jit(solution)/shard_map/turn/pallas_call | solution.py:751
  39.9 6.2 %copy-done = f32[8,4096,128]{2,1,0:T(8,128)} copy-done((f32[8,4096,128]{2,1,0:T(8,128)}, f32[8,4096,128]{2,1,0:T(8,128)S(1)}, u32[]{:S(2)}) %copy-start) | copy-done | bytes 16777240
  46.1 5.8 %copy-done.1 = f32[8,4096,128]{2,1,0:T(8,128)S(1)} copy-done((f32[8,4096,128]{2,1,0:T(8,128)S(1)}, f32[8,4096,128]{2,1,0:T(8,128)}, u32[]{:S(2)}) %copy-start.1) | copy-done | bytes 16777240
  51.9 39.5 %find.1 = bf16[8,4,128,128]{3,2,1,0:T(8,128)(2,1)} custom-call(s32[32,256]{1,0:T(8,128)S(1)} %bitcast.89, f32[32768,128]{1,0:T(8,128)S(1)} %bitcast.87), custom_call_target="tpu_custom_call" | custom-call | tf_op jit(solution)/shard_map/find/pallas_call | solution.py:760
  91.3 7.3 %all-to-all-start.1 = ((bf16[32,128,128]{2,1,0:T(8,128)(2,1)}), bf16[32,128,128]{2,1,0:T(8,128)(2,1)S(1)}, u32[]{:S(2)}, u32[]{:S(2)}) async-start(bf16[32,128,128]{2,1,0:T(8,128)(2,1)} %bitcast.4), calls=%async_computation.1 | async-start | bytes 2097152 | tf_op jit(solution)/shard_map/all_to_all | solution.py:769
  98.7 3.0 convert_element_type.44.w3_ref
  106.9 18.0 %all-to-all-done.1 = bf16[32,128,128]{2,1,0:T(8,128)(2,1)S(1)} async-done(((bf16[32,128,128]{2,1,0:T(8,128)(2,1)}), bf16[32,128,128]{2,1,0:T(8,128)(2,1)S(1)}, u32[]{:S(2)}, u32[]{:S(2)}) %all-to-all-start.1) | async-done | bytes 1048608 | tf_op jit(solution)/shard_map/all_to_all | solution.py:769
  124.9 7.0 %place.1.x_ref = bf16[1024,256]{1,0:T(8,128)(2,1)S(1)} custom-call(s32[4,1024]{1,0:T(4,128)S(1)} %get-tuple-element.44.place_ref, bf16[4096,128]{1,0:T(8,128)(2,1)S(1)} %bitcast.88), custom_call_target="tpu_custom_call" | custom-call | tf_op jit(solution)/shard_map/place/pallas_call | solution.py:772
  132.6 75.3 %ahead.1 = (bf16[4,1024,256]{2,1,0:T(8,128)(2,1)}, bf16[2,1024,512]{2,1,0:T(8,128)(2,1)}, f32[2,1024,512]{2,1,0:T(8,128)}, bf16[2,1024,512]{2,1,0:T(8,128)(2,1)}...) custom-call(s32[1]{0:T(128)} %dynamic_slice.10.count_ref, ...), custom_call_target="tpu_custom_call" | custom-call | tf_op jit(solution)/shard_map/ahead/pallas_call | solution.py:808
  207.9 8.0 %all-to-all-start.5 = ((bf16[32,16,1408]{2,1,0:T(8,128)(2,1)}), bf16[32,16,1408]{2,1,0:T(8,128)(2,1)S(1)}, u32[]{:S(2)}, u32[]{:S(2)}) async-start(bf16[32,16,1408]{2,1,0:T(8,128)(2,1)} %bitcast.111), calls=%async_computation.5 | async-start | bytes 2883584 | tf_op jit(solution)/shard_map/all_to_all | solution.py:915
  215.9 41.9 %back.1 = (f32[1024,256]{1,0:T(8,128)}, bf16[8,4,384,128]{3,2,1,0:T(8,128)(2,1)}, f32[2,8,512]{2,1,0:T(8,128)}) custom-call(bf16[2,1024,512]{2,1,0:T(8,128)(2,1)} %get-tuple-element.46.dy_ref, bf16[2,1024,512]{2,1,0:T(8,128)(2,1)} %get-tuple-element.47.hid_ref, f32[2,1024,512]{2,1,0:T(8,128)} %get-tuple-element.48.slope_ref, ...), custom_call_target="tpu_custom_call" | custom-call | tf_op jit(solution)/shard_map/back/pallas_call | solution.py:858
  257.8 1.2 copy-done.3
  259.0 12.8 %send.1 = bf16[4096,128]{1,0:T(8,128)(2,1)} custom-call(s32[4,1024]{1,0:T(4,128)S(1)} %get-tuple-element.53.slot_ref, f32[1024,256]{1,0:T(8,128)S(1)} %copy-done.3), custom_call_target="tpu_custom_call" | custom-call | tf_op jit(solution)/shard_map/send/pallas_call | solution.py:882
  271.8 6.0 %all-to-all-start.3 = ((bf16[32,128,128]{2,1,0:T(8,128)(2,1)}), bf16[32,128,128]{2,1,0:T(8,128)(2,1)S(1)}, u32[]{:S(2)}, u32[]{:S(2)}) async-start(bf16[32,128,128]{2,1,0:T(8,128)(2,1)} %bitcast.18), calls=%async_computation.3 | async-start | bytes 2097152 | tf_op jit(solution)/shard_map/all_to_all | solution.py:894
  278.6 25.4 %all-to-all-done.3 = bf16[32,128,128]{2,1,0:T(8,128)(2,1)S(1)} async-done(((bf16[32,128,128]{2,1,0:T(8,128)(2,1)}), bf16[32,128,128]{2,1,0:T(8,128)(2,1)S(1)}, u32[]{:S(2)}, u32[]{:S(2)}) %all-to-all-start.3) | async-done | bytes 1048608 | tf_op jit(solution)/shard_map/all_to_all | solution.py:894
  304.2 39.2 %all_to_all.51 = bf16[32,16,1408]{2,1,0:T(8,128)(2,1)} all-to-all(bf16[32,16,1408]{2,1,0:T(8,128)(2,1)S(1)} %broadcast_in_dim.21), channel_id=1, replica_groups=mesh['dp'=8,'mp'=4] {'dp','mp'}, dimensions={0} | all-to-all | bytes 2883584 | tf_op jit(solution)/shard_map/all_to_all | solution.py:915
  343.3 2.9 all-to-all-start.4
  348.5 49.5 %add.198 = (f32[32768,128]{1,0:T(8,128)}, f32[8,128]{1,0:T(8,128)}) custom-call(s32[32,256]{1,0:T(8,128)} %bitcast.90, bf16[4096,128]{1,0:T(8,128)(2,1)} %bitcast.105), custom_call_target="tpu_custom_call" | custom-call | tf_op jit(solution)/shard_map/add/pallas_call | solution.py:897
  398.1 1.3 reduce_sum.91
  400.9 17.2 %all-to-all-done.4 = bf16[32,384,128]{2,1,0:T(8,128)(2,1)S(1)} async-done(((bf16[32,384,128]{2,1,0:T(8,128)(2,1)}), bf16[32,384,128]{2,1,0:T(8,128)(2,1)S(1)}, u32[]{:S(2)}, u32[]{:S(2)}) %all-to-all-start.4) | async-done | bytes 3145760 | tf_op jit(solution)/shard_map/all_to_all | solution.py:915
  423.2 4.4 all-to-all-start.6
  428.8 1.6 copy.96
  430.3 7.9 %all-to-all-done.6 = f32[32,9,128]{2,1,0:T(8,128)S(1)} async-done(((f32[32,9,128]{2,1,0:T(8,128)}), f32[32,9,128]{2,1,0:T(8,128)S(1)}, u32[]{:S(2)}, u32[]{:S(2)}) %all-to-all-start.6) | async-done | bytes 147488 | tf_op jit(solution)/shard_map/all_to_all | solution.py:915
  444.0 1.6 slice_multiply_fusion.2
  448.3 3.0 fusion.13
  451.4 2.2 fusion.11
  453.7 6.9 %multiply_subtract_fusion = (f32[512,1280]{1,0:T(8,128)}, f32[512,1280]{1,0:T(8,128)}, f32[512,1280]{1,0:T(8,128)}) fusion(f32[512,1280]{1,0:T(8,128)S(1)} %copy-done.6, f32[]{:T(128)} %div.67, bf16[512,1408]{1,0:T(8,128)(2,1)S(1)} %bitcast.104, f32[512,1280]{1,0:T(8,128)S(1)} %copy-done.10, f32[512,1280]{1,0:T(8,128)} %param.43), kind=kLoop, calls=%fused_computation.5 | loop fusion | flops 10485760 | bytes 17039364 | tf_op jit(solution)/shard_map/sub | solution.py:46
  462.9 43.1 %tables.1 = (f32[16,64,4096]{2,1,0:T(8,128)}, f32[16,64,4096]{2,1,0:T(8,128)}, f32[16,64,4096]{2,1,0:T(8,128)}) custom-call(f32[1]{0:T(128)} %bitcast.30.factor_ref, f32[16,64,4096]{2,1,0:T(8,128)} %bitcast.94, f32[16,64,4096]{2,1,0:T(8,128)} %bitcast.95, f32[16,64,4096]{2,1,0:T(8,128)} %bitcast.96, f32[8,4096,128]{2,1,0:T(8,128)} %bitcast.97), custom_call_target="tpu_custom_call" | custom-call | tf_op jit(solution)/shard_map/tables/pallas_call | solution.py:969
  506.0 1.3 add_sqrt_fusion
  (117 shorter events, 25.9 us)
Async XLA Ops:
  7.2 15.0 %copy-start.5 = (s32[1024,4]{0,1:T(4,128)S(1)}, s32[1024,4]{0,1:T(4,128)}, u32[]{:S(2)}) copy-start(s32[1024,4]{0,1:T(4,128)} %param.25) | copy-start | bytes 49156
  7.2 125.4 %all-gather.2.cloned.1.call-start = ((), (), s32[]{:S(2)}) async-start(), calls=%async_computation.8 | async-start | bytes 3538944 | tf_op jit(solution)/shard_map/all_gather | solution.py:747
  24.8 21.2 %all-to-all-start = ((s32[32,1,256]{2,1,0:T(1,128)}), s32[32,1,256]{2,1,0:T(1,128)S(1)}, u32[]{:S(2)}, u32[]{:S(2)}) async-start(s32[32,1,256]{2,1,0:T(1,128)} %copy.72), calls=%async_computation | async-start | bytes 65536 | tf_op jit(solution)/shard_map/all_to_all | solution.py:741
  39.9 6.2 %copy-start = (f32[8,4096,128]{2,1,0:T(8,128)}, f32[8,4096,128]{2,1,0:T(8,128)S(1)}, u32[]{:S(2)}) copy-start(f32[8,4096,128]{2,1,0:T(8,128)S(1)} %turn.1) | copy-start | bytes 50331652
  46.1 45.2 %copy-start.4 = (s32[32,1,256]{2,0,1:T(8,128)}, s32[32,1,256]{2,0,1:T(8,128)S(1)}, u32[]{:S(2)}) copy-start(s32[32,1,256]{2,0,1:T(8,128)S(1)} %copy.98) | copy-start | bytes 98308
  91.3 10.3 %copy-start.18 = (f32[9517]{0:T(1024)S(1)}, f32[9517]{0:T(1024)}, u32[]{:S(2)}) copy-start(f32[9517]{0:T(1024)} %param.47) | copy-start | bytes 114208
  91.3 11.0 %copy-start.24 = (s32[256,5]{0,1:T(8,128)S(1)}, s32[256,5]{0,1:T(8,128)}, u32[]{:S(2)}) copy-start(s32[256,5]{0,1:T(8,128)} %param.27) | copy-start | bytes 15364
  91.3 11.8 %copy-start.25 = (s32[256,5]{0,1:T(8,128)S(1)}, s32[256,5]{0,1:T(8,128)}, u32[]{:S(2)}) copy-start(s32[256,5]{0,1:T(8,128)} %param.28) | copy-start | bytes 15364
  91.3 33.6 %all-to-all-start.1 = ((bf16[32,128,128]{2,1,0:T(8,128)(2,1)}), bf16[32,128,128]{2,1,0:T(8,128)(2,1)S(1)}, u32[]{:S(2)}, u32[]{:S(2)}) async-start(bf16[32,128,128]{2,1,0:T(8,128)(2,1)} %bitcast.4), calls=%async_computation.1 | async-start | bytes 2097152 | tf_op jit(solution)/shard_map/all_to_all | solution.py:769
  98.7 7.6 %copy-start.13 = (f32[1024,40]{0,1:T(8,128)S(1)}, f32[1024,40]{0,1:T(8,128)}, u32[]{:S(2)}) copy-start(f32[1024,40]{0,1:T(8,128)} %param.38) | copy-start | bytes 491524
  207.9 63.8 %all-to-all-start.5 = ((bf16[32,16,1408]{2,1,0:T(8,128)(2,1)}), bf16[32,16,1408]{2,1,0:T(8,128)(2,1)S(1)}, u32[]{:S(2)}, u32[]{:S(2)}) async-start(bf16[32,16,1408]{2,1,0:T(8,128)(2,1)} %bitcast.111), calls=%async_computation.5 | async-start | bytes 2883584 | tf_op jit(solution)/shard_map/all_to_all | solution.py:915
  271.8 32.3 %all-to-all-start.3 = ((bf16[32,128,128]{2,1,0:T(8,128)(2,1)}), bf16[32,128,128]{2,1,0:T(8,128)(2,1)S(1)}, u32[]{:S(2)}, u32[]{:S(2)}) async-start(bf16[32,128,128]{2,1,0:T(8,128)(2,1)} %bitcast.18), calls=%async_computation.3 | async-start | bytes 2097152 | tf_op jit(solution)/shard_map/all_to_all | solution.py:894
  304.1 39.3 %copy-start.9 = (bf16[32,128,128]{2,1,0:T(8,128)(2,1)}, bf16[32,128,128]{2,1,0:T(8,128)(2,1)S(1)}, u32[]{:S(2)}) copy-start(bf16[32,128,128]{2,1,0:T(8,128)(2,1)S(1)} %all-to-all-done.3) | copy-start | bytes 3145732
  343.3 74.7 %all-to-all-start.4 = ((bf16[32,384,128]{2,1,0:T(8,128)(2,1)}), bf16[32,384,128]{2,1,0:T(8,128)(2,1)S(1)}, u32[]{:S(2)}, u32[]{:S(2)}) async-start(bf16[32,384,128]{2,1,0:T(8,128)(2,1)} %bitcast.108), calls=%async_computation.4 | async-start | bytes 6291456 | tf_op jit(solution)/shard_map/all_to_all | solution.py:915
  400.3 27.9 %copy-start.11 = (f32[512,128]{1,0:T(8,128)}, f32[512,128]{1,0:T(8,128)S(1)}, u32[]{:S(2)}) copy-start(f32[512,128]{1,0:T(8,128)S(1)} %slice_convert_fusion) | copy-start | bytes 786436
  423.2 15.0 %all-to-all-start.6 = ((f32[32,9,128]{2,1,0:T(8,128)}), f32[32,9,128]{2,1,0:T(8,128)S(1)}, u32[]{:S(2)}, u32[]{:S(2)}) async-start(f32[32,9,128]{2,1,0:T(8,128)} %broadcast_in_dim.20), calls=%async_computation.6 | async-start | bytes 524288 | tf_op jit(solution)/shard_map/all_to_all | solution.py:915
  439.6 13.9 %copy-start.10 = (f32[512,1280]{1,0:T(8,128)S(1)}, f32[512,1280]{1,0:T(8,128)}, u32[]{:S(2)}) copy-start(f32[512,1280]{1,0:T(8,128)} %param.42) | copy-start | bytes 7864324
  453.5 7.0 %copy-start.12 = (f32[320,128]{1,0:T(8,128)S(1)}, f32[320,128]{1,0:T(8,128)}, u32[]{:S(2)}) copy-start(f32[320,128]{1,0:T(8,128)} %slice_multiply_fusion.2) | copy-start | bytes 491524
  453.5 7.0 %copy-start.14 = (f32[1024,40]{0,1:T(8,128)S(1)}, f32[1024,40]{0,1:T(8,128)}, u32[]{:S(2)}) copy-start(f32[1024,40]{0,1:T(8,128)} %param.38) | copy-start | bytes 491524
  453.6 7.0 %copy-start.16 = (f32[1024,40]{0,1:T(8,128)S(1)}, f32[1024,40]{0,1:T(8,128)}, u32[]{:S(2)}) copy-start(f32[1024,40]{0,1:T(8,128)} %param.39) | copy-start | bytes 491524
  453.6 7.0 %copy-start.17 = (f32[1024,40]{0,1:T(8,128)S(1)}, f32[1024,40]{0,1:T(8,128)}, u32[]{:S(2)}) copy-start(f32[1024,40]{0,1:T(8,128)} %param.40) | copy-start | bytes 491524
  453.6 7.9 %copy-start.23 = (f32[5,256]{1,0:T(8,128)S(1)}, f32[5,256]{1,0:T(8,128)}, u32[]{:S(2)}) copy-start(f32[5,256]{1,0:T(8,128)} %heads_ref.1) | copy-start | bytes 15364
  453.6 7.9 %copy-start.26 = (f32[5,256]{1,0:T(8,128)S(1)}, f32[5,256]{1,0:T(8,128)}, u32[]{:S(2)}) copy-start(f32[5,256]{1,0:T(8,128)} %param.45) | copy-start | bytes 15364
  453.6 7.9 %copy-start.27 = (f32[5,256]{1,0:T(8,128)S(1)}, f32[5,256]{1,0:T(8,128)}, u32[]{:S(2)}) copy-start(f32[5,256]{1,0:T(8,128)} %param.46) | copy-start | bytes 15364
  453.6 8.5 %copy-start.20 = (f32[4096]{0:T(1024)S(1)}, f32[4096]{0:T(1024)}, u32[]{:S(2)}) copy-start(f32[4096]{0:T(1024)} %slice_bitcast_fusion) | copy-start | bytes 49156
  453.6 8.5 %copy-start.31 = (f32[40]{0:T(128)S(1)}, f32[40]{0:T(128)}, u32[]{:S(2)}) copy-start(f32[40]{0:T(128)} %slice_bitcast_fusion.3) | copy-start | bytes 484
  453.6 8.5 %copy-start.32 = (f32[5]{0:T(128)S(1)}, f32[5]{0:T(128)}, u32[]{:S(2)}) copy-start(f32[5]{0:T(128)} %slice_bitcast_fusion.2) | copy-start | bytes 64
  453.7 8.5 %copy-start.19 = (f32[9517]{0:T(1024)S(1)}, f32[9517]{0:T(1024)}, u32[]{:S(2)}) copy-start(f32[9517]{0:T(1024)} %param.47) | copy-start | bytes 114208
  453.7 8.5 %copy-start.21 = (f32[9517]{0:T(1024)S(1)}, f32[9517]{0:T(1024)}, u32[]{:S(2)}) copy-start(f32[9517]{0:T(1024)} %param.48) | copy-start | bytes 114208
  453.7 8.5 %copy-start.22 = (f32[9517]{0:T(1024)S(1)}, f32[9517]{0:T(1024)}, u32[]{:S(2)}) copy-start(f32[9517]{0:T(1024)} %param.49) | copy-start | bytes 114208
  462.9 43.1 %copy-start.29 = (f32[14]{0:T(128)S(1)}, f32[14]{0:T(128)}, u32[]{:S(2)}) copy-start(f32[14]{0:T(128)} %constant.34.clone.1) | copy-start | bytes 172
  462.9 43.1 %copy-start.30 = (f32[13]{0:T(128)S(1)}, f32[13]{0:T(128)}, u32[]{:S(2)}) copy-start(f32[13]{0:T(128)} %slice.97) | copy-start | bytes 160
  (9 other events, 30.0 us)
Sparse Core Ops, SparseCore 0:
  22.3 60.8 all-gather.1

commit v3 on v2

--- a/solution.py
+++ b/solution.py
@@ -49,8 +49,8 @@
     )
 
 
-def route_kernel(row_bits, ids_ref, out_ref, place_ref, slot_ref):
-    devices, capacity = out_ref.shape
+def route_kernel(row_bits, ids_ref, out_ref, place_ref, slot_ref, from_ref):
+    devices, _, capacity = out_ref.shape
     tables, samples = ids_ref.shape
     rows_dev = 1 << row_bits
     halves = devices * capacity // 2
@@ -68,7 +68,7 @@
             cols = pl.ds(part * width, width)
             ids = ids_ref[pl.ds(table, 1), cols]
             owner = ids >> row_bits
-            code = (parity * (tables // 2) + table // 2) * rows_dev + (ids & (rows_dev - 1)) + 1
+            code = table * rows_dev + (ids & (rows_dev - 1)) + 1
             onehot = (owner == owners).astype(F32)
             counted = jnp.dot(onehot.astype(LOW), upper, preferred_element_type=F32) + carry
             rank = jnp.sum(onehot * counted, axis=0, keepdims=True).astype(I32) - 1
@@ -84,61 +84,61 @@
             half = rank & 1
             place_ref[pl.ds(table, 1), cols] = (half ^ parity) * halves + row
             slot_ref[pl.ds(table, 1), cols] = half * halves + row
+            sample = lax.broadcasted_iota(I32, (1, width), 1) + part * width
+            from_ref[pl.ds(table, 1), cols] = (half ^ parity) * samples + sample
     codes = (total[:devices] * 128.0 + total[devices:]).astype(I32)
     first = lax.broadcasted_iota(I32, (devices, capacity), 1) == 0
     counted = jnp.where(first, carry * 65536.0, 0.0).astype(I32)
-    out_ref[...] = codes + counted
-
-
-def turn_kernel(table_ref, out_ref):
-    pair, width, rows = table_ref.shape
-    out_ref[0] = table_ref[...].reshape(pair * width, rows).T
+    out_ref[...] = (codes + counted).reshape(devices, 1, capacity)
 
 
 def left_lanes(shape):
     return lax.broadcasted_iota(I32, shape, len(shape) - 1) < 64
 
 
-def find_kernel(groups, group_rows, code_bits, codes_ref, table_ref, out_ref, rows_ref):
+def find_kernel(groups, at_ref, counts_ref, table_ref, out_ref, turned_ref, rows_ref):
     blocks, _, height, lanes = out_ref.shape
-    mask = (1 << code_bits) - 1
+    tables, width, rows_dev = table_ref.shape
+    group = pl.program_id(0)
     left = left_lanes((1, lanes))
-
-    def fetch(code, base, side):
-        at = jnp.maximum((code & 65535) - 1, 0)
-        row = table_ref[pl.ds((at & mask) + base, 1), :]
-        return row, ((at >> code_bits) ^ side) * 64
-
-    def source_step(source, _):
-        count = codes_ref[source, 0] >> 16
-        group = lax.rem(source, groups)
-        base = group * group_rows
+    part = 512
+
+    def turn_step(step, _):
+        table = lax.div(step, rows_dev // part)
+        first = pl.multiple_of(lax.rem(step, rows_dev // part) * part, part)
+        columns = table_ref[table, :, pl.ds(first, part)]
+        there = pl.ds(pl.multiple_of(step * part, part), part)
+        turned_ref[there, :] = jnp.concatenate([columns, columns], axis=0).T
+        return 0
+
+    lax.fori_loop(0, tables * (rows_dev // part), turn_step, 0)
+
+    def block_step(block, _):
+        source = block * groups + group
+        base = source * 2 * height
 
         def step(outer, _):
             got = []
             for inner in range(8):
                 at = outer * 8 + inner
-                even = fetch(codes_ref[source, 2 * at], base, 0)
-                odd = fetch(codes_ref[source, 2 * at + 1], base, 1)
-                got.append((at, even, odd))
-            got = [
-                (at, jnp.where(left, pltpu.roll(*even, 1), pltpu.roll(*odd, 1)))
-                for at, even, odd in got
-            ]
+                even = turned_ref[pl.ds(at_ref[base + 2 * at], 1), :]
+                odd = turned_ref[pl.ds(at_ref[base + 2 * at + 1], 1), :]
+                got.append((at, jnp.where(left, even, odd)))
             for at, row in got:
                 rows_ref[pl.ds(at, 1), :] = row
             return 0
 
-        lax.fori_loop(0, (count + 15) // 16, step, 0)
-        out_ref[lax.div(source, groups), group] = rows_ref[...].astype(LOW)
-        return 0
-
-    lax.fori_loop(0, blocks * groups, source_step, 0)
+        lax.fori_loop(0, (counts_ref[source] + 15) // 16, step, 0)
+        out_ref[block, 0] = rows_ref[...].astype(LOW)
+        return 0
+
+    lax.fori_loop(0, blocks, block_step, 0)
 
 
 def place_kernel(place_ref, rows_ref, out_ref, both_ref, flat_ref):
     count, lanes = rows_ref.shape
-    tables, samples = place_ref.shape
+    samples = out_ref.shape[0]
+    tables = place_ref.shape[0] // samples
     rows = rows_ref[...].astype(F32)
     both_ref[pl.ds(0, count), :] = rows
     both_ref[pl.ds(count, count), :] = pltpu.roll(rows, 64, 1)
@@ -149,8 +149,8 @@
         for inner in range(8):
             sample = outer * 8 + inner
             for pair in range(tables // 2):
-                even = both_ref[pl.ds(place_ref[2 * pair, sample], 1), :]
-                odd = both_ref[pl.ds(place_ref[2 * pair + 1, sample], 1), :]
+                even = both_ref[pl.ds(place_ref[2 * pair * samples + sample], 1), :]
+                odd = both_ref[pl.ds(place_ref[(2 * pair + 1) * samples + sample], 1), :]
                 got.append((pair, sample, jnp.where(left, even, odd)))
         for pair, sample, row in got:
             flat_ref[pair, pl.ds(sample, 1), :] = row
@@ -161,25 +161,22 @@
         out_ref[:, pair * lanes : (pair + 1) * lanes] = flat_ref[pair].astype(LOW)
 
 
-def send_kernel(slot_ref, grad_ref, out_ref, both_ref, rows_ref):
+def send_kernel(slot_ref, from_ref, grad_ref, out_ref, both_ref, rows_ref):
     count, lanes = out_ref.shape
-    tables, samples = slot_ref.shape
+    samples = grad_ref.shape[0]
+    tables = slot_ref.shape[0] // samples
     for pair in range(tables // 2):
         rows = grad_ref[:, pair * lanes : (pair + 1) * lanes]
         both_ref[pair, pl.ds(0, samples), :] = rows
         both_ref[pair, pl.ds(samples, samples), :] = pltpu.roll(rows, 64, 1)
-    bits = count.bit_length() - 1
 
     def step(outer, _):
         got = []
         for inner in range(8):
             sample = outer * 8 + inner
             for table in range(tables):
-                slot = slot_ref[table, sample]
-                turned = (slot >> bits) ^ (table % 2)
-                got.append(
-                    (slot, both_ref[table // 2, pl.ds(turned * samples + sample, 1), :])
-                )
+                row = both_ref[table // 2, pl.ds(from_ref[table * samples + sample], 1), :]
+                got.append((slot_ref[table * samples + sample], row))
         for slot, row in got:
             rows_ref[pl.ds(slot, 1), :] = row
         return 0
@@ -191,11 +188,71 @@
     ).astype(LOW)
 
 
-def add_kernel(groups, code_bits, codes_ref, rows_ref, out_ref, square_ref, parts_ref, sems, *sums):
+def swap_kernel(rows_ref, share_ref, out_ref, shares_ref, r_out, r_in, s_out, s_in):
+    devices = rows_ref.shape[0]
+    groups = share_ref.shape[0]
+    peers = lax.axis_size("mp")
+    dp, mp = lax.axis_index("dp"), lax.axis_index("mp")
+    mine = lax.div(dp, 2) * (peers // 2) + lax.div(mp, 2)
+    me = dp * peers + mp
+    barrier = pltpu.get_barrier_semaphore()
+
+    def place_of(device):
+        return {"dp": lax.div(device, peers), "mp": lax.rem(device, peers)}
+
+    def greet(step, _):
+        target = lax.rem(me + step, devices)
+        pl.semaphore_signal(barrier, inc=1, device_id=place_of(target), device_id_type=MESH)
+        return 0
+
+    lax.fori_loop(1, devices, greet, 0)
+    pl.semaphore_wait(barrier, devices - 1)
+
+    def r_copy(step):
+        target = lax.rem(me + step, devices)
+        return pltpu.make_async_remote_copy(
+            rows_ref.at[target],
+            out_ref.at[me],
+            r_out.at[step],
+            r_in.at[step],
+            device_id=place_of(target),
+            device_id_type=MESH,
+        )
+
+    def s_copy(step):
+        target = lax.rem(mine + step, groups)
+        to_dp = lax.div(target, peers // 2) * 2 + lax.rem(dp, 2)
+        to_mp = lax.rem(target, peers // 2) * 2 + lax.rem(mp, 2)
+        return pltpu.make_async_remote_copy(
+            share_ref.at[target],
+            shares_ref.at[mine],
+            s_out.at[step],
+            s_in.at[step],
+            device_id={"dp": to_dp, "mp": to_mp},
+            device_id_type=MESH,
+        )
+
+    def loop(first, copies, act):
+        def step(at, _):
+            act(copies(at))
+            return 0
+
+        lax.fori_loop(1, first, step, 0)
+
+    loop(devices, r_copy, lambda copy: copy.start())
+    loop(groups, s_copy, lambda copy: copy.start())
+    out_ref[me] = rows_ref[me]
+    shares_ref[mine] = share_ref[mine]
+    loop(groups, s_copy, lambda copy: copy.wait())
+    loop(devices, r_copy, lambda copy: copy.wait())
+
+
+def add_kernel(
+    groups, at_ref, part_at_ref, counts_ref, rows_ref, out_ref, square_ref, parts_ref, sems, *sums
+):
     count, lanes = rows_ref.shape
-    sources = codes_ref.shape[0]
+    sources = counts_ref.shape[0]
     height = count // sources
-    mask = (1 << code_bits) - 1
     table_rows = sums[0].shape[0]
     left = left_lanes((count, lanes))
     rows = rows_ref[...].astype(F32)
@@ -214,23 +271,18 @@
     lax.fori_loop(0, table_rows // 64, clear, 0)
 
     def block_step(block, _):
-        most = codes_ref[block * groups, 0] >> 16
+        most = counts_ref[block * groups]
         for group in range(1, groups):
-            most = jnp.maximum(most, codes_ref[block * groups + group, 0] >> 16)
+            most = jnp.maximum(most, counts_ref[block * groups + group])
 
         def step(outer, _):
             for inner in range(4):
                 got = []
                 for group in range(groups):
-                    source = block * groups + group
-                    code = codes_ref[source, outer * 4 + inner] & 65535
-                    at = jnp.maximum(code - 1, 0)
-                    parity = at >> code_bits
-                    part = ((inner % 2) * 2 + parity) * count + source * height
-                    part = part + outer * 2 + inner // 2
-                    part = jnp.where(code > 0, part, 4 * count)
-                    here = pl.ds(at & mask, 1)
-                    got.append((here, sums[group][here, :] + parts_ref[pl.ds(part, 1), :]))
+                    at = (block * groups + group) * 2 * height + outer * 4 + inner
+                    here = pl.ds(at_ref[at], 1)
+                    part = pl.ds(part_at_ref[at], 1)
+                    got.append((here, sums[group][here, :] + parts_ref[part, :]))
                 for group, (here, row) in enumerate(got):
                     sums[group][here, :] = row
             return 0
@@ -279,15 +331,80 @@
 MESH = pl.DeviceIdType.MESH
 
 
-def meet(peers):
+def meet(peers, partner=None):
     me = lax.axis_index("mp")
     barrier = pltpu.get_barrier_semaphore()
+    if partner is not None:
+        pl.semaphore_signal(
+            barrier, inc=1, device_id={"dp": partner, "mp": me}, device_id_type=MESH
+        )
     for step in range(1, peers):
         pl.semaphore_signal(
             barrier, inc=1, device_id={"mp": lax.rem(me + step, peers)}, device_id_type=MESH
         )
-    pl.semaphore_wait(barrier, peers - 1)
+    pl.semaphore_wait(barrier, peers - 1 + (partner is not None))
     return me
+
+
+def ask_kernel(codes_ref, shard_ref, out_ref, full_ref, c_out, c_in, w_out, w_in):
+    devices = codes_ref.shape[0]
+    here, _, full = full_ref.shape
+    width = shard_ref.shape[2]
+    peers = full // width
+    mp = lax.axis_index("mp")
+    me = lax.axis_index("dp") * peers + mp
+    barrier = pltpu.get_barrier_semaphore()
+
+    def place_of(device):
+        return {"dp": lax.div(device, peers), "mp": lax.rem(device, peers)}
+
+    def greet(step, _):
+        target = lax.rem(me + step, devices)
+        pl.semaphore_signal(barrier, inc=1, device_id=place_of(target), device_id_type=MESH)
+        return 0
+
+    lax.fori_loop(1, devices, greet, 0)
+    columns = pl.ds(pl.multiple_of(mp * width, width), width)
+    full_ref[:, :, columns] = shard_ref[pl.ds(mp * here, here)]
+    out_ref[me] = codes_ref[me]
+    pl.semaphore_wait(barrier, devices - 1)
+
+    def c_copy(step):
+        target = lax.rem(me + step, devices)
+        return pltpu.make_async_remote_copy(
+            codes_ref.at[target],
+            out_ref.at[me],
+            c_out.at[step],
+            c_in.at[step],
+            device_id=place_of(target),
+            device_id_type=MESH,
+        )
+
+    def w_copy(step):
+        target = lax.rem(mp + step, peers)
+        return pltpu.make_async_remote_copy(
+            shard_ref.at[pl.ds(target * here, here)],
+            full_ref.at[:, :, columns],
+            w_out.at[step],
+            w_in.at[step],
+            device_id={"mp": target},
+            device_id_type=MESH,
+        )
+
+    def start(step, _):
+        c_copy(step).start()
+        return 0
+
+    def finish(step, _):
+        c_copy(step).wait()
+        return 0
+
+    lax.fori_loop(1, devices, start, 0)
+    for step in range(1, peers):
+        w_copy(step).start()
+    lax.fori_loop(1, devices, finish, 0)
+    for step in range(1, peers):
+        w_copy(step).wait()
 
 
 def ahead_kernel(
@@ -333,7 +450,7 @@
     own = y_ref.shape[2]
     experts = peers * here
     tasks, tower_hid = heads_ref.shape
-    shards, hid = w_ref.shape[1], w_ref.shape[3]
+    shards, hid = w_ref.shape[0], w_ref.shape[3]
     in_rows = peers * width // shards
     me = meet(peers)
 
@@ -386,7 +503,7 @@
         rows = pl.ds(pl.multiple_of(chunk * own, own), own)
         x = jnp.concatenate([blocks_ref[block, rows] for block in range(peers)], axis=1)
         for e in range(here):
-            w_in = w_ref[e, :, :in_rows, :].reshape(peers * width, hid)
+            w_in = w_ref[:, e, :in_rows, :].reshape(peers * width, hid)
             act_ref[...] = dot(x, w_in) + b1_ref[e]
 
             def gelu_step(tile, _):
@@ -398,7 +515,7 @@
                 return 0
 
             lax.fori_loop(0, own // 32, gelu_step, 0)
-            w_out = w_ref[e, :, in_rows:, :].reshape(out_width, hid)
+            w_out = w_ref[:, e, in_rows:, :].reshape(out_width, hid)
             y_send[turn, e] = (dot(hid_ref[e, rows, :], w_out, NT) + b2_ref[e]).astype(LOW)
 
         @pl.when(turn < peers - 1)
@@ -564,24 +681,36 @@
     w_ref,
     dgl_ref,
     wg_ref,
+    small_ref,
     dx_ref,
     parts_ref,
     b1_ref,
+    share_ref,
     dpre_ref,
     dx_send,
     dx_recv,
+    core_recv,
+    pair_send,
+    pair_recv,
     x_out,
     x_in,
+    s_out,
+    s_in,
 ):
     peers, samples, width = blocks_ref.shape
     here, _, out_width = dy_ref.shape
     own = samples // peers
     hid = hid_ref.shape[2]
-    shards, rows_both = w_ref.shape[1], w_ref.shape[2]
+    shards, rows_both = w_ref.shape[0], w_ref.shape[2]
     in_rows = peers * width // shards
     out_rows = rows_both - in_rows
     features = peers * width
-    me = meet(peers)
+    dp = lax.axis_index("dp")
+    dp_side = lax.rem(dp, 2)
+    pair = dp + 1 - 2 * dp_side
+    me = meet(peers, pair)
+    side = lax.rem(me, 2)
+    near = me + 1 - 2 * side
 
     def chunk_rows(turn):
         return pl.ds(pl.multiple_of(lax.rem(me + turn, peers) * own, own), own)
@@ -598,6 +727,36 @@
             device_id_type=MESH,
         )
 
+    share = share_ref.shape[0]
+
+    def share_rows(part):
+        return pl.ds(pl.multiple_of(part * share, share), share)
+
+    def core_copy():
+        return pltpu.make_async_remote_copy(
+            small_ref.at[pl.ds(pl.multiple_of((1 - side) * 2 * share, share), 2 * share)],
+            core_recv,
+            s_out.at[0],
+            s_in.at[0],
+            device_id={"dp": dp, "mp": near},
+            device_id_type=MESH,
+        )
+
+    def pair_copy():
+        return pltpu.make_async_remote_copy(
+            pair_send,
+            pair_recv,
+            s_out.at[1],
+            s_in.at[1],
+            device_id={"dp": pair, "mp": me},
+            device_id_type=MESH,
+        )
+
+    def core_sum(part):
+        mine = small_ref[share_rows(side * 2 + part), :].astype(F32)
+        return mine + core_recv[share_rows(part), :].astype(F32)
+
+    core_copy().start()
     b1_ref[...] = jnp.zeros_like(b1_ref)
 
     def chunk_step(turn, _):
@@ -606,11 +765,11 @@
         gate = (dgl_ref[...].astype(F32) * mine).astype(LOW)
         total = dot(gate, wg_ref[...])
         for e in range(here):
-            w_out = w_ref[e, :, in_rows:, :].reshape(out_width, hid)
+            w_out = w_ref[:, e, in_rows:, :].reshape(out_width, hid)
             dpre = (dot(dy_ref[e, rows, :], w_out) * slope_ref[e, rows, :]).astype(LOW)
             dpre_ref[e, rows, :] = dpre
             b1_ref[e] += dot(jnp.ones((8, own), LOW), dpre)
-            w_in = w_ref[e, :, :in_rows, :].reshape(features, hid)
+            w_in = w_ref[:, e, :in_rows, :].reshape(features, hid)
             total += dot(dpre, w_in, NT)
         for target in range(peers):
             dx_send[target, rows] = total[:, target * width : (target + 1) * width].astype(LOW)
@@ -620,7 +779,11 @@
 
     lax.fori_loop(0, peers, chunk_step, 0)
 
-    lanes = parts_ref.shape[3]
+    core_copy().wait()
+    pair_send[...] = core_sum(1 - dp_side).astype(LOW)
+    pair_copy().start()
+
+    lanes = parts_ref.shape[4]
     blocks_in = width // 128
     per_in = 128 // in_rows
     per_out = 128 // out_rows
@@ -632,8 +795,10 @@
             value = dot(x, dpre_ref[e], TN).astype(LOW)
             for shard in range(per_in):
                 for target in range(peers):
+                    to = block * per_in + shard
+                    away = lax.rem(to + dp, 2)
                     parts_ref[
-                        block * per_in + shard, target, e * rows_both : e * rows_both + in_rows, :
+                        away, lax.div(to, 2), target, e * rows_both : e * rows_both + in_rows, :
                     ] = value[
                         shard * in_rows : (shard + 1) * in_rows, target * lanes : (target + 1) * lanes
                     ]
@@ -646,8 +811,11 @@
             value = dot(dy_ref[e, :, cols], hid_ref[e], TN).astype(LOW)
             for shard in range(per_out):
                 for target in range(peers):
+                    to = block * per_out + shard
+                    away = lax.rem(to + dp, 2)
                     parts_ref[
-                        block * per_out + shard,
+                        away,
+                        lax.div(to, 2),
                         target,
                         e * rows_both + in_rows : (e + 1) * rows_both,
                         :,
@@ -662,15 +830,122 @@
     for turn in range(peers):
         for step in range(1, peers):
             x_copy(turn, step).wait()
+    pair_copy().wait()
+    share_ref[...] = (core_sum(dp_side) + pair_recv[...].astype(F32)).astype(LOW)
     total = dx_send[me].astype(F32)
     for step in range(1, peers):
         total = total + dx_recv[lax.rem(me + step, peers)].astype(F32)
     dx_ref[...] = total
 
 
+def total_kernel(
+    features,
+    width_out,
+    valid_ref,
+    inner_ref,
+    stats_ref,
+    tables_ref,
+    shares_ref,
+    grads_ref,
+    inner_out,
+    result_ref,
+    pay_ref,
+    got_ref,
+    t_out,
+    t_in,
+):
+    devices = got_ref.shape[0]
+    peers = inner_out.shape[0]
+    here, _, hid = inner_ref.shape
+    inner_rows = inner_out.shape[1]
+    number = stats_ref.shape[0] - 2
+    me = lax.axis_index("dp") * peers + lax.axis_index("mp")
+    barrier = pltpu.get_barrier_semaphore()
+
+    def place_of(device):
+        return {"dp": lax.div(device, peers), "mp": lax.rem(device, peers)}
+
+    def greet(step, _):
+        target = lax.rem(me + step, devices)
+        pl.semaphore_signal(barrier, inc=1, device_id=place_of(target), device_id_type=MESH)
+        return 0
+
+    lax.fori_loop(1, devices, greet, 0)
+    lane = lax.broadcasted_iota(I32, (1, 128), 1)
+
+    def whole_sum(value):
+        return jnp.sum(jnp.sum(value, axis=0, keepdims=True), axis=1, keepdims=True)
+
+    def grad_step(at, total):
+        rows = grads_ref[pl.ds(pl.multiple_of(at * 64, 64), 64), :]
+        return total + jnp.sum((rows * rows).reshape(8, 8, 128), axis=0)
+
+    squares = lax.fori_loop(0, grads_ref.shape[0] // 64, grad_step, tables_ref[...])
+    share = shares_ref[...]
+    vector = jnp.where(lane == 0, stats_ref[number + 1, :1, :1], 0.0)
+    vector = jnp.where(lane == 1, stats_ref[number + 1, :1, 1:2], vector)
+    for at in range(number + 1):
+        vector = jnp.where(lane == at + 2, whole_sum(stats_ref[at]), vector)
+    vector = jnp.where(lane == number + 3, whole_sum(squares) + whole_sum(share * share), vector)
+    pay_ref[...] = jnp.zeros_like(pay_ref)
+    for e in range(here):
+        for part in range(hid // 128):
+            at = e * (hid // 128) + part
+            pay_ref[at : at + 1, :] = inner_ref[e, :1, part * 128 : (part + 1) * 128]
+    pay_ref[inner_rows : inner_rows + 1, :] = vector
+    got_ref[me] = pay_ref[...]
+    pl.semaphore_wait(barrier, devices - 1)
+
+    def t_copy(step):
+        target = lax.rem(me + step, devices)
+        return pltpu.make_async_remote_copy(
+            pay_ref,
+            got_ref.at[me],
+            t_out.at[step],
+            t_in.at[step],
+            device_id=place_of(target),
+            device_id_type=MESH,
+        )
+
+    def start(step, _):
+        t_copy(step).start()
+        return 0
+
+    def finish(step, _):
+        t_copy(step).wait()
+        return 0
+
+    lax.fori_loop(1, devices, start, 0)
+    lax.fori_loop(1, devices, finish, 0)
+    total = jnp.zeros((1, 128), F32)
+    inner_sq = jnp.zeros((inner_rows, 128), F32)
+    for group in range(peers):
+        part = jnp.zeros((inner_rows, 128), F32)
+        for block in range(devices // peers):
+            source = block * peers + group
+            part = part + got_ref[source, :inner_rows, :]
+            total = total + got_ref[source, inner_rows : inner_rows + 1, :]
+        inner_out[group] = part
+        inner_sq = inner_sq + part * part
+
+    def pick(at):
+        return jnp.sum(jnp.where(lane == at, total, 0.0), axis=1, keepdims=True)
+
+    weight = pick(1)
+    grad_norm = jnp.sqrt(pick(number + 3) + whole_sum(inner_sq)) / weight
+    factor = jnp.minimum(1.0, clip_max / grad_norm) / weight
+    count = valid_ref[0].astype(F32)
+    width = jnp.where(lane == number + 2, float(features), float(width_out))
+    result_ref[...] = jnp.zeros_like(result_ref)
+    result_ref[0:1, :] = jnp.broadcast_to(factor, (1, 128))
+    result_ref[1:2, :] = jnp.broadcast_to(grad_norm, (1, 128))
+    result_ref[2:3, :] = total
+    result_ref[3:4, :] = jnp.sqrt(total / (count * width) + stat_eps)
+
+
 def table_kernel(factor_ref, weight_ref, first_ref, second_ref, grad_ref, *outs):
     pair, width, rows = weight_ref.shape
-    gradient = grad_ref[0].T.reshape(pair, width, rows) * factor_ref[0]
+    gradient = grad_ref[0].T.reshape(pair, width, rows) * factor_ref[:1, :1].reshape(1, 1, 1)
     results = adamw(weight_ref[...], first_ref[...], second_ref[...], gradient, rate_table)
     for out, result in zip(outs, results):
         out[...] = result
@@ -715,7 +990,6 @@
     height = capacity // 2
     slots = devices * height
     row_bits = rows_dev.bit_length() - 1
-    code_bits = row_bits + (tables_here // 2).bit_length() - 1
     pairs = tables // 2
     lanes = 2 * d_emb
     group_rows = tables_here // 2 * rows_dev
@@ -726,46 +1000,70 @@
     width_out = out_rows * dp_count
     tower_hid = towers.shape[1] // TASKS
 
-    outgoing, place, slot = pl.pallas_call(
+    outgoing, place, slot, source = pl.pallas_call(
         functools.partial(route_kernel, row_bits),
         out_shape=(
-            jax.ShapeDtypeStruct((devices, capacity), I32),
+            jax.ShapeDtypeStruct((devices, 1, capacity), I32),
+            jax.ShapeDtypeStruct((tables_here, samples), I32),
             jax.ShapeDtypeStruct((tables_here, samples), I32),
             jax.ShapeDtypeStruct((tables_here, samples), I32),
         ),
         in_specs=[VMEM],
-        out_specs=(VMEM, VMEM, VMEM),
+        out_specs=(VMEM,) * 4,
         compiler_params=params(32),
         name="route",
     )(row_ids.T)
-    codes = lax.all_to_all(
-        outgoing.reshape(devices, 1, capacity), AXES, split_axis=0, concat_axis=0, tiled=True
-    ).reshape(devices, capacity)
-
-    shard = jnp.concatenate([expert_in, expert_out], axis=0).astype(LOW)
-    shard = lax.all_to_all(shard, "mp", split_axis=1, concat_axis=2, tiled=True)
-    gathered = lax.all_gather(shard, "dp", axis=0, tiled=False)
-    expert_w = jnp.transpose(gathered, (2, 0, 1, 3))
+    in_out_rows = in_rows + out_rows
+    hid_here = hid // mp_count
+    shard = jnp.concatenate([expert_in, expert_out], axis=0).astype(LOW).transpose(1, 0, 2)
+
+    def sems(*shape):
+        return pltpu.SemaphoreType.DMA(shape)
+
+    codes, shard = pl.pallas_call(
+        ask_kernel,
+        out_shape=(
+            jax.ShapeDtypeStruct((devices, 1, capacity), I32),
+            jax.ShapeDtypeStruct((experts_here, in_out_rows, hid), LOW),
+        ),
+        in_specs=[VMEM, VMEM],
+        out_specs=(VMEM, VMEM),
+        scratch_shapes=[sems(devices), sems(devices), sems(mp_count), sems(mp_count)],
+        compiler_params=pltpu.CompilerParams(
+            vmem_limit_bytes=16 * MIB, collective_id=2, has_side_effects=True
+        ),
+        name="ask",
+    )(outgoing, shard)
+    expert_w = lax.all_gather(shard, "dp", axis=0, tiled=False)
+    codes = codes.reshape(devices, capacity)
+    asked = codes[:, 0] >> 16
+    plain = codes & 65535
+    found_at = jnp.maximum(plain - 1, 0)
+    table_at = found_at >> row_bits
+    sum_at = (table_at >> 1) * rows_dev + (found_at & (rows_dev - 1))
+    number = jnp.arange(capacity, dtype=I32)[None, :]
+    part_at = ((number & 1) * 2 + (table_at & 1)) * slots + (number >> 1)
+    part_at = part_at + jnp.arange(devices, dtype=I32)[:, None] * height
+    part_at = jnp.where(plain > 0, part_at, 4 * slots)
 
     table_view = jnp.transpose(embeddings, (0, 2, 1))
-    turned = pl.pallas_call(
-        turn_kernel,
-        grid=(pairs,),
-        out_shape=jax.ShapeDtypeStruct((pairs, rows_dev, lanes), F32),
-        in_specs=[pl.BlockSpec((2, d_emb, rows_dev), lambda p: (p, 0, 0))],
-        out_specs=pl.BlockSpec((1, rows_dev, lanes), lambda p: (p, 0, 0)),
-        compiler_params=params(32),
-        name="turn",
-    )(table_view)
     found = pl.pallas_call(
-        functools.partial(find_kernel, mp_count, group_rows, code_bits),
+        functools.partial(find_kernel, mp_count),
+        grid=(mp_count,),
         out_shape=jax.ShapeDtypeStruct((dp_count, mp_count, height, lanes), LOW),
-        in_specs=[SMEM, VMEM],
-        out_specs=VMEM,
-        scratch_shapes=[pltpu.VMEM((height, lanes), F32)],
-        compiler_params=params(32),
+        in_specs=[
+            SMEM,
+            SMEM,
+            pl.BlockSpec((tables_here, d_emb, rows_dev), lambda m: (m, 0, 0)),
+        ],
+        out_specs=pl.BlockSpec((dp_count, 1, height, lanes), lambda m: (0, m, 0, 0)),
+        scratch_shapes=[
+            pltpu.VMEM((tables_here * rows_dev, lanes), F32),
+            pltpu.VMEM((height, lanes), F32),
+        ],
+        compiler_params=params(60),
         name="find",
-    )(codes, turned.reshape(pairs * rows_dev, lanes))
+    )(found_at.reshape(-1), asked, table_view)
     returned = lax.all_to_all(
         found.reshape(devices, height, lanes), AXES, split_axis=0, concat_axis=0, tiled=True
     )
@@ -780,7 +1078,7 @@
         ],
         compiler_params=params(32),
         name="place",
-    )(place, returned.reshape(slots, lanes))
+    )(place.reshape(-1), returned.reshape(slots, lanes))
 
     first = EXPERTS * hid
     second = first + EXPERTS * width_out
@@ -801,9 +1099,6 @@
 
     def scratch(shape, kind=F32):
         return pltpu.VMEM(shape, kind)
-
-    def sems(*shape):
-        return pltpu.SemaphoreType.DMA(shape)
 
     blocks, hidden, slopes, output_rows, gate_logit_grad, small_grads, stat_parts = pl.pallas_call(
         ahead_kernel,
@@ -854,35 +1149,41 @@
         labels,
         label_mask,
     )
-    in_out_rows = in_rows + out_rows
-    embed_grad, grad_parts, inner_parts = pl.pallas_call(
+    pack_shape = (pack_rows // 4, TASKS * tower_hid + 128)
+    embed_grad, grad_parts, inner_parts, share = pl.pallas_call(
         back_kernel,
         out_shape=(
             jax.ShapeDtypeStruct((samples, tables_here * d_emb), F32),
             jax.ShapeDtypeStruct(
-                (dp_count, mp_count, experts_here * in_out_rows, hid // mp_count), LOW
+                (2, dp_count // 2, mp_count, experts_here * in_out_rows, hid_here), LOW
             ),
             jax.ShapeDtypeStruct((experts_here, 8, hid), F32),
+            jax.ShapeDtypeStruct(pack_shape, LOW),
         ),
-        in_specs=[VMEM] * 7,
-        out_specs=(VMEM,) * 3,
+        in_specs=[VMEM] * 8,
+        out_specs=(VMEM,) * 4,
         scratch_shapes=[
             scratch((experts_here, samples, hid), LOW),
             scratch((mp_count, samples, tables_here * d_emb), LOW),
             scratch((mp_count, samples, tables_here * d_emb), LOW),
+            scratch((2 * pack_shape[0], pack_shape[1]), LOW),
+            scratch(pack_shape, LOW),
+            scratch(pack_shape, LOW),
             sems(mp_count, mp_count),
             sems(mp_count, mp_count),
+            sems(2),
+            sems(2),
         ],
         compiler_params=pltpu.CompilerParams(
             vmem_limit_bytes=56 * MIB, collective_id=1, has_side_effects=True
         ),
         name="back",
-    )(output_rows, hidden, slopes, blocks, expert_w, gate_logit_grad, gating_low)
+    )(output_rows, hidden, slopes, blocks, expert_w, gate_logit_grad, gating_low, small_grads)
 
     back_rows = pl.pallas_call(
         send_kernel,
         out_shape=jax.ShapeDtypeStruct((slots, lanes), LOW),
-        in_specs=[SMEM, VMEM],
+        in_specs=[SMEM, SMEM, VMEM],
         out_specs=VMEM,
         scratch_shapes=[
             pltpu.VMEM((tables_here // 2, 2 * samples, lanes), F32),
@@ -890,17 +1191,55 @@
         ],
         compiler_params=params(32),
         name="send",
-    )(slot, embed_grad)
-    arrived = lax.all_to_all(
-        back_rows.reshape(devices, height, lanes), AXES, split_axis=0, concat_axis=0, tiled=True
+    )(slot.reshape(-1), source.reshape(-1), embed_grad)
+    share = share.reshape(devices // 4, pack_rows // devices, -1)
+    arrived, shares = pl.pallas_call(
+        swap_kernel,
+        out_shape=(
+            jax.ShapeDtypeStruct((devices, height, lanes), LOW),
+            jax.ShapeDtypeStruct(share.shape, LOW),
+        ),
+        in_specs=[VMEM, VMEM],
+        out_specs=(VMEM, VMEM),
+        scratch_shapes=[sems(devices), sems(devices), sems(devices // 4), sems(devices // 4)],
+        compiler_params=pltpu.CompilerParams(
+            vmem_limit_bytes=16 * MIB, collective_id=3, has_side_effects=True
+        ),
+        name="swap",
+    )(back_rows.reshape(devices, height, lanes), share)
+    def exchange_all(parts):
+        return lax.all_to_all(parts, AXES, split_axis=0, concat_axis=0, tiled=True)
+
+    share = jnp.sum(shares.astype(F32), axis=0)
+    whole = lax.all_gather(share.astype(LOW), AXES, axis=0, tiled=False)
+
+    partner = lax.ppermute(grad_parts[1], "dp", [(d, d ^ 1) for d in range(dp_count)])
+    partner, arrived = lax.optimization_barrier((partner, arrived))
+    grad_parts = (grad_parts[0].astype(F32) + partner.astype(F32)).astype(LOW)
+    sides = [
+        [d * mp_count + m for d in range(x, dp_count, 2) for m in range(mp_count)] for x in range(2)
+    ]
+    grad_parts = lax.all_to_all(
+        grad_parts.reshape(devices // 2, experts_here * in_out_rows, hid_here),
+        AXES,
+        split_axis=0,
+        concat_axis=0,
+        axis_index_groups=sides,
+        tiled=True,
     )
+    grad_sum = jnp.sum(
+        grad_parts.reshape(dp_count // 2, mp_count, experts_here, in_out_rows, -1).astype(F32), 0
+    )
+    owned = grad_sum.reshape(EXPERTS, in_out_rows, -1).transpose(1, 0, 2)
+    in_sum, out_sum = owned[:in_rows], owned[in_rows:]
+
     table_grad, table_sq = pl.pallas_call(
-        functools.partial(add_kernel, mp_count, code_bits),
+        functools.partial(add_kernel, mp_count),
         out_shape=(
             jax.ShapeDtypeStruct((pairs * rows_dev, lanes), F32),
             jax.ShapeDtypeStruct((8, lanes), F32),
         ),
-        in_specs=[SMEM, VMEM],
+        in_specs=[SMEM, SMEM, SMEM, VMEM],
         out_specs=(pl.BlockSpec(memory_space=pl.ANY), VMEM),
         scratch_shapes=[
             pltpu.VMEM((4 * slots + 8, lanes), F32),
@@ -909,16 +1248,67 @@
         + [pltpu.VMEM((group_rows, lanes), F32)] * mp_count,
         compiler_params=params(60),
         name="add",
-    )(codes, arrived.reshape(slots, lanes))
-
-    def exchange_all(parts):
-        return lax.all_to_all(parts, AXES, split_axis=0, concat_axis=0, tiled=True)
-
-    small_grads = small_grads.reshape(devices, pack_rows // devices, -1)
-    share = jnp.sum(exchange_all(small_grads).astype(F32), axis=0)
-    share_sq = jnp.sum(share * share)
-    whole = exchange_all(jnp.broadcast_to(share.astype(LOW)[None], small_grads.shape))
-    whole = whole.reshape(pack_rows, -1)
+    )(sum_at.reshape(-1), part_at.reshape(-1), asked, arrived.reshape(slots, lanes))
+
+    stat_end = EXPERTS + TASKS
+    inner_rows = experts_here * hid // 128
+    pay_rows = inner_rows + 8
+    inner_sum, result = pl.pallas_call(
+        functools.partial(total_kernel, features, width_out),
+        out_shape=(
+            jax.ShapeDtypeStruct((mp_count, inner_rows, 128), F32),
+            jax.ShapeDtypeStruct((8, 128), F32),
+        ),
+        in_specs=[SMEM] + [VMEM] * 5,
+        out_specs=(VMEM,) * 2,
+        scratch_shapes=[
+            scratch((pay_rows, 128)),
+            scratch((devices, pay_rows, 128)),
+            sems(devices),
+            sems(devices),
+        ],
+        compiler_params=pltpu.CompilerParams(
+            vmem_limit_bytes=16 * MIB, collective_id=4, has_side_effects=True
+        ),
+        name="total",
+    )(
+        jnp.sum(counts).reshape(1),
+        inner_parts,
+        stat_parts,
+        table_sq,
+        share,
+        grad_sum.reshape(-1, 128),
+    )
+    factor = result[0, 0]
+
+    table_spec = pl.BlockSpec((2, d_emb, rows_dev), lambda p: (p, 0, 0))
+    embed_out = pl.pallas_call(
+        table_kernel,
+        grid=(pairs,),
+        out_shape=(jax.ShapeDtypeStruct(table_view.shape, F32),) * 3,
+        in_specs=[
+            pl.BlockSpec((8, 128), lambda p: (0, 0)),
+            table_spec,
+            table_spec,
+            table_spec,
+            pl.BlockSpec((1, rows_dev, lanes), lambda p: (p, 0, 0)),
+        ],
+        out_specs=(table_spec,) * 3,
+        compiler_params=params(58),
+        name="tables",
+    )(
+        result,
+        table_view,
+        jnp.transpose(embed_first, (0, 2, 1)),
+        jnp.transpose(embed_second, (0, 2, 1)),
+        table_grad.reshape(pairs, rows_dev, lanes),
+    )
+    embed_out = [jnp.transpose(value, (0, 2, 1)) for value in embed_out]
+    in_out = adamw(expert_in, in_first, in_second, in_sum * factor, rate_dense)
+    out_out = adamw(expert_out, out_first, out_second, out_sum * factor, rate_dense)
+    whole, embed_out = lax.optimization_barrier((whole, embed_out))
+    whole = whole.reshape(dp_count // 2, 2, mp_count // 2, 2, pack_rows // devices, -1)
+    whole = whole.transpose(3, 1, 0, 2, 4, 5).reshape(pack_rows, -1)
     towers_sum = whole[:, : TASKS * tower_hid].astype(F32)
     packed = whole[:, TASKS * tower_hid :].astype(F32)
     blocks_x = features // 128
@@ -929,78 +1319,21 @@
     gating_sum = packed[:heads_at].reshape(blocks_x, all_gates, 128).transpose(1, 0, 2)
     gating_sum = gating_sum.reshape(all_gates, features).T
     heads_sum = packed[heads_at:tower_at].reshape(TASKS, tower_hid)
-
-    grad_parts = exchange_all(
-        grad_parts.reshape(devices, experts_here * in_out_rows, hid // mp_count)
-    )
-    grad_sum = jnp.sum(
-        grad_parts.reshape(dp_count, mp_count, experts_here, in_out_rows, -1).astype(F32), 0
-    )
-    grad_sum = grad_sum.reshape(EXPERTS, in_out_rows, -1).transpose(1, 0, 2)
-    in_sum, out_sum = grad_sum[:in_rows], grad_sum[in_rows:]
-
-    squares = jnp.sum(table_sq) + jnp.sum(grad_sum * grad_sum) + share_sq
-    stat_end = EXPERTS + TASKS
-    stat_sums = jnp.sum(stat_parts[: stat_end + 1], axis=(1, 2))
-    scalars = jnp.concatenate(
-        [stat_parts[stat_end + 1, 0, :2], stat_sums, squares[None]]
-    )
-    scalars = jnp.pad(scalars, (0, 128 - scalars.size))[None]
-    final = jnp.concatenate(
-        [inner_parts[:, 0, :].reshape(-1, 128), scalars], axis=0
-    )
-    final = exchange_all(jnp.broadcast_to(final[None], (devices,) + final.shape))
-    sums = jnp.sum(final[:, -1, :], axis=0)
-    inner_sum = jnp.sum(final[:, :-1, :].reshape(dp_count, -1), axis=0)
     bias_sum = jnp.concatenate(
         [
-            inner_sum,
+            inner_sum.reshape(-1),
             packed[outer_at:rest_at].reshape(-1),
             packed[rest_at, :all_gates],
             packed[tower_at:outer_at].reshape(-1),
             packed[rest_at + 1, :TASKS],
         ]
     )
-    weight_total = sums[1]
-    grad_norm = jnp.sqrt(sums[stat_end + 3] + jnp.sum(inner_sum * inner_sum)) / weight_total
-    factor = jnp.minimum(1.0, clip_max / grad_norm) / weight_total
-
-    table_spec = pl.BlockSpec((2, d_emb, rows_dev // 2), lambda p, c: (p, 0, c))
-    embed_out = pl.pallas_call(
-        table_kernel,
-        grid=(pairs, 2),
-        out_shape=(jax.ShapeDtypeStruct(table_view.shape, F32),) * 3,
-        in_specs=[
-            SMEM,
-            table_spec,
-            table_spec,
-            table_spec,
-            pl.BlockSpec((1, rows_dev // 2, lanes), lambda p, c: (p, c, 0)),
-        ],
-        out_specs=(table_spec,) * 3,
-        compiler_params=params(48),
-        name="tables",
-    )(
-        factor.reshape(1),
-        table_view,
-        jnp.transpose(embed_first, (0, 2, 1)),
-        jnp.transpose(embed_second, (0, 2, 1)),
-        table_grad.reshape(pairs, rows_dev, lanes),
-    )
-    embed_out = [jnp.transpose(value, (0, 2, 1)) for value in embed_out]
-    in_out = adamw(expert_in, in_first, in_second, in_sum * factor, rate_dense)
-    out_out = adamw(expert_out, out_first, out_second, out_sum * factor, rate_dense)
     gating_out = adamw(gating, gating_first, gating_second, gating_sum * factor, rate_dense)
     towers_out = adamw(towers, towers_first, towers_second, towers_sum * factor, rate_dense)
     heads_out = adamw(heads, heads_first, heads_second, heads_sum * factor, rate_dense)
     biases_out = adamw(biases, biases_first, biases_second, bias_sum * factor, rate_dense)
-    n_valid = jnp.sum(counts).astype(F32)
-    widths = jnp.concatenate(
-        [jnp.full((1,), features, F32), jnp.full((EXPERTS + TASKS,), width_out, F32)]
-    )
-    mean_sq = jnp.concatenate([sums[stat_end + 2][None], sums[2 : stat_end + 2]])
-    stats = jnp.sqrt(mean_sq / (n_valid * widths) + stat_eps)
-    loss = jnp.stack([sums[0], weight_total])
+    stats = jnp.concatenate([result[3, stat_end + 2][None], result[3, 2 : stat_end + 2]])
+    loss = result[2, :2]
     return (
         *embed_out,
         *in_out,
@@ -1011,7 +1344,7 @@
         *towers_out,
         *heads_out,
         *biases_out,
-        grad_norm.reshape(1),
+        result[1, :1],
         loss,
         stats,
     )

time: 519 us -> 406 us (0.78)
  blocking collectives: 50.7 us -> 0 us
  starting transfers between devices: 33.5 us -> 8.89 us
  waiting for transfers between devices: 68.5 us -> 47.9 us
  local copies, waits for them, and re-layouts: 32.1 us -> 20.1 us
  between operations: 21.6 us -> 14.6 us
    all_to_all x2 -> x0, blocking collectives: 50.7 us -> none  [the longest x1 39.2 us: exchange_all(): return lax.all_to_all(parts, AXES, split_axis=0, concat_axis=0, tiled=True)]
    all_to_all x5 -> x1, waiting for transfers between devices: 50.5 us -> 8.31 us  [body(): lax.all_to_all(grad_parts.reshape(devices // 2, experts_here * in_out_row...]
    all_to_all x5 -> x1, starting transfers between devices: 26.2 us -> 4.3 us  [body(): lax.all_to_all(grad_parts.reshape(devices // 2, experts_here * in_out_row...]
    all_to_all x1, waiting for transfers between devices: 18 us -> 39.5 us  [body(): lax.all_to_all(found.reshape(devices, height, lanes), AXES, split_axis=0,...]
    pallas_call x4 -> x6, Pallas kernels: 142 us -> 157 us  [the longest x1 39.5 us: body(): pl.pallas_call(swap_kernel, out_shape=(jax.ShapeDtypeStruct((devices, hei...]
    unnamed x73 -> x86, local copies, waits for them, and re-layouts: 18.7 us -> 7.8 us
    pallas_call x1, Pallas kernels: 12.8 us -> 7.37 us  [body(): pl.pallas_call(send_kernel, out_shape=jax.ShapeDtypeStruct((slots, lanes)...]
  transfers between devices with their start and end apart: 7 -> 5, of which waited for: 4 -> 2; matrix products, arithmetic and copies ran while one was open for 3% -> 3% of each run, Pallas kernels for 29% -> 37%
where the time goes in v3:
time: 406 us; the launch traced here: 405 us
  Pallas kernels  285 us (70%)
  waiting for transfers between devices  47.9 us (12%)
  other arithmetic  28.4 us (7%)
  local copies, waits for them, and re-layouts  20.1 us (5%)
  between operations  14.6 us (4%)
  starting transfers between devices  8.89 us (2%)
    pallas_call x1, Pallas kernels, body(): pl.pallas_call(ahead_kernel, out_shape=(jax.ShapeDtypeStruct((mp_count, s...  75.3 us
    all_to_all x1, waiting for transfers between devices, body(): lax.all_to_all(found.reshape(devices, height, lanes), AXES, split_axis=0,...  39.5 us
    pallas_call x1, Pallas kernels, body(): pl.pallas_call(swap_kernel, out_shape=(jax.ShapeDtypeStruct((devices, hei...  39.5 us
    pallas_call x1, Pallas kernels, body(): pl.pallas_call(table_kernel, grid=(pairs,), out_shape=(jax.ShapeDtypeStru...  39.3 us
    pallas_call x1, Pallas kernels, body(): pl.pallas_call(back_kernel, out_shape=(jax.ShapeDtypeStruct((samples, tab...  38.3 us
    pallas_call x1, Pallas kernels, body(): pl.pallas_call(functools.partial(find_kernel, mp_count), grid=(mp_count,)...  26.5 us
    pallas_call x1, Pallas kernels, body(): pl.pallas_call(functools.partial(add_kernel, mp_count), out_shape=(jax.Sh...  22 us
    pallas_call x1, Pallas kernels, body(): pl.pallas_call(functools.partial(total_kernel, features, width_out), out_...  16.1 us
  transfers between devices with their start and end apart: 5, of which 2 were waited for; matrix products, arithmetic and copies ran while one was open for 3% of the time, Pallas kernels for 37%

profile of v3, /device:TPU:0, one launch (start us, length us, event | category | flops | bytes accessed | tf_op | source)
XLA Modules:
  0.0 405.0 jit_solution(144853716861281103)
XLA Ops:
  8.0 2.0 route.1
  10.0 1.1 copy.88
  11.1 1.0 copy.89
  12.2 13.6 %ask.1 = (s32[32,1,256]{2,1,0:T(1,128)S(1)}, bf16[2,192,512]{2,1,0:T(8,128)(2,1)}) custom-call(s32[32,1,256]{2,1,0:T(1,128)S(1)} %get-tuple-element.61.codes_ref, bf16[8,192,128]{2,1,0:T(8,128)(2,1)S(1)} %maximum_bitcast_fusion.shard_ref), custom_call_target="tpu_custom_call" | custom-call | tf_op jit(solution)/shard_map/ask/pallas_call | solution.py:1023
  27.1 26.5 %find.1 = bf16[8,4,128,128]{3,2,1,0:T(8,128)(2,1)} custom-call(s32[8192]{0:T(1024)} %bitcast.132, s32[32]{0:T(128)} %fusion.6.counts_ref, f32[16,64,4096]{2,1,0:T(8,128)} %bitcast.116), custom_call_target="tpu_custom_call" | custom-call | tf_op jit(solution)/shard_map/find/pallas_call | solution.py:1050
  53.7 3.0 all-to-all-start
  56.7 3.0 convert_element_type.57.w3_ref
  64.9 39.5 %all-to-all-done = bf16[32,128,128]{2,1,0:T(8,128)(2,1)S(1)} async-done(((bf16[32,128,128]{2,1,0:T(8,128)(2,1)}), bf16[32,128,128]{2,1,0:T(8,128)(2,1)S(1)}, u32[]{:S(2)}, u32[]{:S(2)}) %all-to-all-start) | async-done | bytes 1048608 | tf_op jit(solution)/shard_map/all_to_all | solution.py:1067
  104.4 5.0 %place.1.x_ref = bf16[1024,256]{1,0:T(8,128)(2,1)S(1)} custom-call(s32[4096]{0:T(1024)S(1)} %bitcast.110, bf16[4096,128]{1,0:T(8,128)(2,1)S(1)} %bitcast.106), custom_call_target="tpu_custom_call" | custom-call | tf_op jit(solution)/shard_map/place/pallas_call | solution.py:1070
  110.2 75.3 %ahead.1 = (bf16[4,1024,256]{2,1,0:T(8,128)(2,1)}, bf16[2,1024,512]{2,1,0:T(8,128)(2,1)}, f32[2,1024,512]{2,1,0:T(8,128)}, bf16[2,1024,512]{2,1,0:T(8,128)(2,1)}...) custom-call(s32[1]{0:T(128)} %dynamic_slice.10.count_ref, bf16[1024,256]{1,0:T(8,128)(2,1)} %copy-done, ...), custom_call_target="tpu_custom_call" | custom-call | tf_op jit(solution)/shard_map/ahead/pallas_call | solution.py:1103
  185.5 38.3 %back.1 = (f32[1024,256]{1,0:T(8,128)}, bf16[2,4,4,384,128]{4,3,2,1,0:T(8,128)(2,1)}, f32[2,8,512]{2,1,0:T(8,128)}, bf16[128,1408]{1,0:T(8,128)(2,1)}) custom-call(bf16[2,1024,512]{2,1,0:T(8,128)(2,1)} %get-tuple-element.64.dy_ref, bf16[2,1024,512]{2,1,0:T(8,128)(2,1)} %get-tuple-element.65.hid_ref, f32[2,1024,512]{2,1,0:T(8,128)} %get-tuple-element.66.slope_ref, ...), custom_call_target="tpu_custom_call" | custom-call | tf_op jit(solution)/shard_map/back/pallas_call | solution.py:1153
  223.9 1.7 slice_bitcast_fusion
  225.6 1.3 collective-permute-start
  226.9 7.4 %send.1 = bf16[4096,128]{1,0:T(8,128)(2,1)S(1)} custom-call(s32[4096]{0:T(1024)S(1)} %get-tuple-element.122.slot_ref, s32[4096]{0:T(1024)S(1)} %get-tuple-element.121.from_ref, f32[1024,256]{1,0:T(8,128)S(1)} %copy-done.2), custom_call_target="tpu_custom_call" | custom-call | tf_op jit(solution)/shard_map/send/pallas_call | solution.py:1183
  234.3 39.5 %swap.1 = (bf16[32,128,128]{2,1,0:T(8,128)(2,1)S(1)}, bf16[8,16,1408]{2,1,0:T(8,128)(2,1)S(1)}) custom-call(bf16[32,128,128]{2,1,0:T(8,128)(2,1)S(1)} %bitcast.107, bf16[8,16,1408]{2,1,0:T(8,128)(2,1)S(1)} %bitcast.109), custom_call_target="tpu_custom_call" | custom-call | tf_op jit(solution)/shard_map/swap/pallas_call | solution.py:1196
  274.8 1.6 fusion
  276.3 4.3 %all-to-all-start.1 = ((bf16[16,384,128]{2,1,0:T(8,128)(2,1)}), bf16[16,384,128]{2,1,0:T(8,128)(2,1)S(1)}, u32[]{:S(2)}, u32[]{:S(2)}) async-start(bf16[16,384,128]{2,1,0:T(8,128)(2,1)} %bitcast.124), calls=%async_computation.1 | async-start | bytes 3145728 | tf_op jit(solution)/shard_map/all_to_all | solution.py:1222
  283.3 22.0 %add.247 = (f32[32768,128]{1,0:T(8,128)}, f32[8,128]{1,0:T(8,128)}) custom-call(s32[8192]{0:T(1024)} %get-tuple-element.115.at_ref, s32[8192]{0:T(1024)} %get-tuple-element.114.part_at_ref, s32[32]{0:T(128)} %fusion.6.counts_ref, bf16[4096,128]{1,0:T(8,128)(2,1)} %bitcast.108), custom_call_target="tpu_custom_call" | custom-call | tf_op jit(solution)/shard_map/add/pallas_call | solution.py:1236
  305.2 8.3 %all-to-all-done.1 = bf16[16,384,128]{2,1,0:T(8,128)(2,1)S(1)} async-done(((bf16[16,384,128]{2,1,0:T(8,128)(2,1)}), bf16[16,384,128]{2,1,0:T(8,128)(2,1)S(1)}, u32[]{:S(2)}, u32[]{:S(2)}) %all-to-all-start.1) | async-done | bytes 1572896 | tf_op jit(solution)/shard_map/all_to_all | solution.py:1222
  314.5 16.1 %total.1 = (f32[4,8,128]{2,1,0:T(8,128)S(1)}, f32[8,128]{1,0:T(8,128)S(1)}) custom-call(s32[1]{0:T(128)} %bitcast.17.valid_ref, f32[2,8,512]{2,1,0:T(8,128)S(1)} %copy-done.5, f32[15,8,512]{2,1,0:T(8,128)S(1)} %copy-done.4, f32[8,128]{1,0:T(8,128)S(1)} %copy-done.8, f32[16,1408]{1,0:T(8,128)S(1)} %convert_reduce_fusion.1.shares_ref, f32[1536,128]{1,0:T(8,128)S(1)} %bitcast.105), custom_call_target="tpu_custom_call" | custom-call | tf_op jit(solution)/shard_map/total/pallas_call | solution.py:1256
  331.2 39.3 %tables.1 = (f32[16,64,4096]{2,1,0:T(8,128)}, f32[16,64,4096]{2,1,0:T(8,128)}, f32[16,64,4096]{2,1,0:T(8,128)}) custom-call(f32[8,128]{1,0:T(8,128)} %copy-done.7, f32[16,64,4096]{2,1,0:T(8,128)} %bitcast.117, f32[16,64,4096]{2,1,0:T(8,128)} %bitcast.118, f32[16,64,4096]{2,1,0:T(8,128)} %bitcast.119, f32[8,4096,128]{2,1,0:T(8,128)} %bitcast.120), custom_call_target="tpu_custom_call" | custom-call | tf_op jit(solution)/shard_map/tables/pallas_call | solution.py:1285
  370.5 1.4 fusion.17
  371.9 1.5 copy.70
  375.1 1.2 slice_bitcast_fusion.2
  376.3 1.3 slice_multiply_fusion.2
  378.3 1.3 slice_bitcast_fusion.5
  379.5 1.2 slice_bitcast_fusion.6
  380.7 8.9 %multiply_subtract_fusion = (f32[512,1280]{1,0:T(8,128)}, f32[512,1280]{1,0:T(8,128)}, f32[512,1280]{1,0:T(8,128)}) fusion(f32[512,1280]{1,0:T(8,128)} %param.41, f32[]{:T(128)} %bitcast.32, bf16[512,1408]{1,0:T(8,128)(2,1)S(1)} %bitcast.126, f32[512,1280]{1,0:T(8,128)} %param.42, f32[512,1280]{1,0:T(8,128)} %param.43), kind=kLoop, calls=%fused_computation.6 | loop fusion | flops 10485760 | bytes 17039364 | tf_op jit(solution)/shard_map/sub | solution.py:46
  389.9 2.4 fusion.14
  392.2 1.7 fusion.12
  394.0 1.2 pad_maximum_fusion
  395.3 1.3 multiply_subtract_fusion.4
  (122 shorter events, 17.1 us)
Async XLA Ops:
  7.2 103.0 %all-gather.5.cloned.1.call-start = ((), (), s32[]{:S(2)}) async-start(), calls=%async_computation.2 | async-start | bytes 3538944 | tf_op jit(solution)/shard_map/all_gather | solution.py:1037
  53.7 6.0 %copy-start.29 = (s32[256,5]{0,1:T(8,128)S(1)}, s32[256,5]{0,1:T(8,128)}, u32[]{:S(2)}) copy-start(s32[256,5]{0,1:T(8,128)} %param.27) | copy-start | bytes 15364
  53.7 6.8 %copy-start.30 = (s32[256,5]{0,1:T(8,128)S(1)}, s32[256,5]{0,1:T(8,128)}, u32[]{:S(2)}) copy-start(s32[256,5]{0,1:T(8,128)} %param.28) | copy-start | bytes 15364
  53.7 50.7 %all-to-all-start = ((bf16[32,128,128]{2,1,0:T(8,128)(2,1)}), bf16[32,128,128]{2,1,0:T(8,128)(2,1)S(1)}, u32[]{:S(2)}, u32[]{:S(2)}) async-start(bf16[32,128,128]{2,1,0:T(8,128)(2,1)} %bitcast.127), calls=%async_computation | async-start | bytes 2097152 | tf_op jit(solution)/shard_map/all_to_all | solution.py:1067
  56.6 4.6 %copy-start.22 = (f32[9517]{0:T(1024)S(1)}, f32[9517]{0:T(1024)}, u32[]{:S(2)}) copy-start(f32[9517]{0:T(1024)} %param.47) | copy-start | bytes 114208
  56.7 5.3 %copy-start.35 = (s32[8]{0:T(128)S(1)}, s32[8]{0:T(128)}, u32[]{:S(2)}) copy-start(s32[8]{0:T(128)} %param.26) | copy-start | bytes 100
  56.7 7.6 %copy-start.13 = (f32[1024,40]{0,1:T(8,128)S(1)}, f32[1024,40]{0,1:T(8,128)}, u32[]{:S(2)}) copy-start(f32[1024,40]{0,1:T(8,128)} %param.38) | copy-start | bytes 491524
  223.8 10.4 %copy-start.3 = (bf16[128,1408]{1,0:T(8,128)(2,1)S(1)}, bf16[128,1408]{1,0:T(8,128)(2,1)}, u32[]{:S(2)}) copy-start(bf16[128,1408]{1,0:T(8,128)(2,1)} %get-tuple-element.71) | copy-start | bytes 1081348
  223.9 50.9 %copy-start.9 = (bf16[2,4,4,384,128]{4,3,2,1,0:T(8,128)(2,1)S(1)}, bf16[2,4,4,384,128]{4,3,2,1,0:T(8,128)(2,1)}, u32[]{:S(2)}) copy-start(bf16[2,4,4,384,128]{4,3,2,1,0:T(8,128)(2,1)} %get-tuple-element.75) | copy-start | bytes 9437188
  225.6 49.2 %collective-permute-start = (bf16[4,4,384,128]{3,2,1,0:T(8,128)(2,1)S(1)}, bf16[4,4,384,128]{3,2,1,0:T(8,128)(2,1)S(1)}, u32[]{:S(2)}, u32[]{:S(2)}) collective-permute-start(bf16[4,4,384,128]{3,2,1,0:T(8,128)(2,1)S(1)} %slice_bitcast_fusion), channel_id=1, source_target_pairs={{0,4},{4,0},{8,12},{12,8},{16,20},{20,16},{24,28},{28,24},{1,5},{5... | collective-permute-start | bytes 4718600 | tf_op jit(solution)/shard_map/ppermute | solution.py:1216
  276.3 6.3 %copy-start.17 = (s32[32,1,256]{2,1,0:T(1,128)S(1)}, s32[32,1,256]{2,1,0:T(1,128)}, u32[]{:S(2)}) copy-start(s32[32,1,256]{2,1,0:T(1,128)} %add_maximum_fusion) | copy-start | bytes 98308
  276.3 37.2 %all-to-all-start.1 = ((bf16[16,384,128]{2,1,0:T(8,128)(2,1)}), bf16[16,384,128]{2,1,0:T(8,128)(2,1)S(1)}, u32[]{:S(2)}, u32[]{:S(2)}) async-start(bf16[16,384,128]{2,1,0:T(8,128)(2,1)} %bitcast.124), calls=%async_computation.1 | async-start | bytes 3145728 | tf_op jit(solution)/shard_map/all_to_all | solution.py:1222
  280.6 33.2 %copy-start.4 = (f32[15,8,512]{2,1,0:T(8,128)S(1)}, f32[15,8,512]{2,1,0:T(8,128)}, u32[]{:S(2)}) copy-start(f32[15,8,512]{2,1,0:T(8,128)} %get-tuple-element.74.stats_ref) | copy-start | bytes 737284
  280.7 33.2 %copy-start.5 = (f32[2,8,512]{2,1,0:T(8,128)S(1)}, f32[2,8,512]{2,1,0:T(8,128)}, u32[]{:S(2)}) copy-start(f32[2,8,512]{2,1,0:T(8,128)} %get-tuple-element.73.inner_ref) | copy-start | bytes 98308
  280.7 91.3 %all-gather.7.cloned.1.call-start = ((), (), s32[]{:S(2)}) async-start(), calls=%async_computation.3 | async-start | bytes 1486848 | tf_op jit(solution)/shard_map/all_gather | solution.py:1214
  380.7 8.9 %copy-start.10 = (f32[128,8,128]{2,1,0:T(8,128)S(1)}, f32[128,8,128]{2,1,0:T(8,128)}, u32[]{:S(2)}) copy-start(f32[128,8,128]{2,1,0:T(8,128)} %param.32) | copy-start | bytes 1572868
  380.7 8.9 %copy-start.15 = (f32[128,8,128]{2,1,0:T(8,128)S(1)}, f32[128,8,128]{2,1,0:T(8,128)}, u32[]{:S(2)}) copy-start(f32[128,8,128]{2,1,0:T(8,128)} %param.33) | copy-start | bytes 1572868
  380.7 8.9 %copy-start.16 = (f32[128,8,128]{2,1,0:T(8,128)S(1)}, f32[128,8,128]{2,1,0:T(8,128)}, u32[]{:S(2)}) copy-start(f32[128,8,128]{2,1,0:T(8,128)} %param.34) | copy-start | bytes 1572868
  389.7 5.5 %copy-start.24 = (f32[4096]{0:T(1024)S(1)}, f32[4096]{0:T(1024)}, u32[]{:S(2)}) copy-start(f32[4096]{0:T(1024)} %slice_bitcast_fusion.1) | copy-start | bytes 49156
  389.7 5.5 %copy-start.28 = (f32[1280]{0:T(1024)S(1)}, f32[1280]{0:T(1024)}, u32[]{:S(2)}) copy-start(f32[1280]{0:T(1024)} %get-tuple-element.110) | copy-start | bytes 15364
  389.7 5.5 %copy-start.33 = (f32[5]{0:T(128)S(1)}, f32[5]{0:T(128)}, u32[]{:S(2)}) copy-start(f32[5]{0:T(128)} %slice_bitcast_fusion.3) | copy-start | bytes 64
  389.7 5.5 %copy-start.34 = (f32[40]{0:T(128)S(1)}, f32[40]{0:T(128)}, u32[]{:S(2)}) copy-start(f32[40]{0:T(128)} %slice_bitcast_fusion.4) | copy-start | bytes 484
  389.7 5.5 %copy-start.23 = (f32[9517]{0:T(1024)S(1)}, f32[9517]{0:T(1024)}, u32[]{:S(2)}) copy-start(f32[9517]{0:T(1024)} %param.47) | copy-start | bytes 114208
  389.8 5.5 %copy-start.25 = (f32[9517]{0:T(1024)S(1)}, f32[9517]{0:T(1024)}, u32[]{:S(2)}) copy-start(f32[9517]{0:T(1024)} %param.48) | copy-start | bytes 114208
  389.8 5.5 %copy-start.26 = (f32[9517]{0:T(1024)S(1)}, f32[9517]{0:T(1024)}, u32[]{:S(2)}) copy-start(f32[9517]{0:T(1024)} %param.49) | copy-start | bytes 114208
  389.8 6.8 %copy-start.27 = (f32[5,256]{1,0:T(8,128)S(1)}, f32[5,256]{1,0:T(8,128)}, u32[]{:S(2)}) copy-start(f32[5,256]{1,0:T(8,128)} %heads_ref.1) | copy-start | bytes 15364
  389.8 6.8 %copy-start.31 = (f32[5,256]{1,0:T(8,128)S(1)}, f32[5,256]{1,0:T(8,128)}, u32[]{:S(2)}) copy-start(f32[5,256]{1,0:T(8,128)} %param.45) | copy-start | bytes 15364
  389.8 6.8 %copy-start.32 = (f32[5,256]{1,0:T(8,128)S(1)}, f32[5,256]{1,0:T(8,128)}, u32[]{:S(2)}) copy-start(f32[5,256]{1,0:T(8,128)} %param.46) | copy-start | bytes 15364
  389.8 7.4 %copy-start.12 = (f32[320,128]{1,0:T(8,128)S(1)}, f32[320,128]{1,0:T(8,128)}, u32[]{:S(2)}) copy-start(f32[320,128]{1,0:T(8,128)} %slice_multiply_fusion.2) | copy-start | bytes 491524
  389.8 7.4 %copy-start.14 = (f32[1024,40]{0,1:T(8,128)S(1)}, f32[1024,40]{0,1:T(8,128)}, u32[]{:S(2)}) copy-start(f32[1024,40]{0,1:T(8,128)} %param.38) | copy-start | bytes 491524
  389.8 7.4 %copy-start.20 = (f32[1024,40]{0,1:T(8,128)S(1)}, f32[1024,40]{0,1:T(8,128)}, u32[]{:S(2)}) copy-start(f32[1024,40]{0,1:T(8,128)} %param.39) | copy-start | bytes 491524
  389.9 7.4 %copy-start.21 = (f32[1024,40]{0,1:T(8,128)S(1)}, f32[1024,40]{0,1:T(8,128)}, u32[]{:S(2)}) copy-start(f32[1024,40]{0,1:T(8,128)} %param.40) | copy-start | bytes 491524
  (10 other events, 18.9 us)
Sparse Core Ops, SparseCore 0:
  26.0 78.4 all-gather.4
  285.0 65.4 all-gather.6

commit v4 on v3

--- a/solution.py
+++ b/solution.py
@@ -407,7 +407,7 @@
         w_copy(step).wait()
 
 
-def ahead_kernel(
+def dense_kernel(
     count_ref,
     x_ref,
     w_ref,
@@ -421,13 +421,15 @@
     tb2_ref,
     labels_ref,
     mask_ref,
+    stats_ref,
+    dx_ref,
+    parts_ref,
+    g_b1_ref,
+    share_ref,
     blocks_ref,
     hid_ref,
     slope_ref,
     dy_ref,
-    dgl_ref,
-    small_ref,
-    stats_ref,
     y_send,
     y_ref,
     gates_ref,
@@ -435,14 +437,29 @@
     dmix_ref,
     dg_ref,
     dy_send,
+    small_ref,
     pack_ref,
     act_ref,
+    gate_ref,
+    dpre_ref,
+    dx_send,
+    dx_near,
+    dx_help,
+    dx_sum,
+    dx_far,
+    core_recv,
+    pair_send,
+    pair_recv,
     x_out,
     x_in,
     y_out,
     y_in,
     d_out,
     d_in,
+    g_out,
+    g_in,
+    s_out,
+    s_in,
 ):
     peers, samples, width = blocks_ref.shape
     here = hid_ref.shape[0]
@@ -452,55 +469,102 @@
     tasks, tower_hid = heads_ref.shape
     shards, hid = w_ref.shape[0], w_ref.shape[3]
     in_rows = peers * width // shards
-    me = meet(peers)
-
-    def other(step):
-        return lax.rem(me + step, peers)
-
-    def x_copy(turn, step):
-        target = other(step)
-        rows = pl.ds(pl.multiple_of(lax.rem(target + turn + 1, peers) * own, own), own)
+    rows_both = w_ref.shape[2]
+    out_rows = rows_both - in_rows
+    features = peers * width
+    dp = lax.axis_index("dp")
+    dp_side = lax.rem(dp, 2)
+    pair = dp + 1 - 2 * dp_side
+    me = meet(peers, pair)
+    side = lax.rem(me, 2)
+    chip = lax.div(me, 2)
+    near = me + 1 - 2 * side
+    far = lax.rem(me + 2, peers)
+    across = lax.rem(near + 2, peers)
+
+    def rows_of(chunk):
+        return pl.ds(pl.multiple_of(chunk * own, own), own)
+
+    def ahead_chunk(turn):
+        return lax.rem(2 * chip + 2 + turn, peers)
+
+    def back_chunk(turn):
+        return lax.rem(2 * chip + turn, peers)
+
+    def remote(source, target, out_sem, in_sem, device):
         return pltpu.make_async_remote_copy(
-            x_ref.at[rows],
-            blocks_ref.at[me, rows],
-            x_out.at[turn, step],
-            x_in.at[turn, step],
-            device_id={"mp": target},
-            device_id_type=MESH,
-        )
-
-    def y_copy(turn):
-        return pltpu.make_async_remote_copy(
-            y_send.at[turn],
-            y_ref.at[me],
-            y_out.at[turn],
-            y_in.at[turn],
-            device_id={"mp": other(turn + 1)},
-            device_id_type=MESH,
-        )
-
-    def d_copy(step):
-        target = other(step)
-        return pltpu.make_async_remote_copy(
-            dy_send.at[pl.ds(target * here, here)],
-            dy_ref.at[:, pl.ds(pl.multiple_of(me * own, own), own), :],
-            d_out.at[step],
-            d_in.at[step],
-            device_id={"mp": target},
-            device_id_type=MESH,
+            source, target, out_sem, in_sem, device_id={"dp": dp, "mp": device}, device_id_type=MESH
+        )
+
+    def x_far(turn):
+        rows = rows_of(back_chunk(turn))
+        return remote(
+            x_ref.at[rows], blocks_ref.at[me, rows], x_out.at[0, turn], x_in.at[0, turn], far
+        )
+
+    def x_near(turn):
+        rows = rows_of(ahead_chunk(turn))
+        return remote(
+            x_ref.at[rows], blocks_ref.at[me, rows], x_out.at[1, turn], x_in.at[1, turn], near
+        )
+
+    def x_hand(turn):
+        rows = rows_of(ahead_chunk(turn))
+        block = blocks_ref.at[far, rows]
+        return remote(block, block, x_out.at[2, turn], x_in.at[2, turn], near)
+
+    def y_copy(turn, relation, device):
+        return remote(
+            y_send.at[turn], y_ref.at[me], y_out.at[relation], y_in.at[relation], device
+        )
+
+    def d_copy(relation, device):
+        return remote(
+            dy_send.at[pl.ds(device * here, here)],
+            dy_ref.at[:, rows_of(me), :],
+            d_out.at[relation],
+            d_in.at[relation],
+            device,
+        )
+
+    def g_near(turn):
+        rows = rows_of(back_chunk(turn))
+        return remote(
+            dx_send.at[near, rows], dx_near.at[rows], g_out.at[0, turn], g_in.at[0, turn], near
+        )
+
+    def g_help(turn):
+        rows = rows_of(back_chunk(turn))
+        return remote(
+            dx_send.at[across, rows], dx_help.at[rows], g_out.at[1, turn], g_in.at[1, turn], near
+        )
+
+    def g_far(turn):
+        rows = rows_of(back_chunk(turn))
+        return remote(
+            dx_sum.at[rows], dx_far.at[rows], g_out.at[2, turn], g_in.at[2, turn], far
         )
 
     for turn in range(peers):
-        for step in range(1, peers):
-            x_copy(turn, step).start()
+        x_far(turn).start()
+        x_near(turn).start()
     blocks_ref[me] = x_ref[...]
     limit = count_ref[0]
 
+    x_far(0).wait_recv()
+    x_hand(0).start()
+
     def expert_step(turn, _):
-        for step in range(1, peers):
-            x_copy(turn, step).wait_recv()
-        chunk = lax.rem(me + turn + 1, peers)
-        rows = pl.ds(pl.multiple_of(chunk * own, own), own)
+        x_near(turn).wait_recv()
+        x_hand(turn).wait_recv()
+
+        @pl.when(turn < peers - 1)
+        def _():
+            x_far(turn + 1).wait_recv()
+            x_hand(turn + 1).start()
+
+        chunk = ahead_chunk(turn)
+        rows = rows_of(chunk)
         x = jnp.concatenate([blocks_ref[block, rows] for block in range(peers)], axis=1)
         for e in range(here):
             w_in = w_ref[:, e, :in_rows, :].reshape(peers * width, hid)
@@ -518,16 +582,23 @@
             w_out = w_ref[:, e, in_rows:, :].reshape(out_width, hid)
             y_send[turn, e] = (dot(hid_ref[e, rows, :], w_out, NT) + b2_ref[e]).astype(LOW)
 
-        @pl.when(turn < peers - 1)
+        @pl.when(turn < 2)
         def _():
-            y_copy(turn).start()
+            y_copy(turn, 1 + lax.rem(side + turn, 2), chunk).start()
+
+        @pl.when(jnp.logical_and(turn >= 2, chunk != me))
+        def _():
+            y_copy(turn, 0, chunk).start()
+
+        @pl.when(chunk == me)
+        def _():
+            y_ref[me] = y_send[turn]
 
         return 0
 
     lax.fori_loop(0, peers, expert_step, 0)
-    y_ref[me] = y_send[peers - 1]
-
-    own_rows = pl.ds(pl.multiple_of(me * own, own), own)
+
+    own_rows = rows_of(me)
     x_own = jnp.concatenate([blocks_ref[block, own_rows] for block in range(peers)], axis=1)
     logits = dot(x_own, wg_ref[...], NT) + bg_ref[...]
     for k in range(tasks):
@@ -545,8 +616,8 @@
 
     x_square = lax.fori_loop(0, samples // 64, square_step, jnp.zeros((8, width), F32))
     stats_ref[experts + tasks, :, :width] = x_square
-    for turn in range(peers - 1):
-        y_copy(turn).wait_recv()
+    for relation, device in enumerate((near, far, across)):
+        y_copy(0, relation, device).wait_recv()
 
     tile_rows = 16
 
@@ -623,8 +694,9 @@
         return 0
 
     lax.fori_loop(0, own // tile_rows, dy_step, 0)
-    for step in range(1, peers):
-        d_copy(step).start()
+    d_copy(1, far).start()
+    d_copy(2, across).start()
+    d_copy(0, near).start()
     dy_ref[:, own_rows, :] = dy_send[pl.ds(me * here, here)]
     ones = jnp.ones((8, own), LOW)
     for e in range(experts):
@@ -654,7 +726,6 @@
     same = lax.broadcasted_iota(I32, flat, 0) // experts == lax.broadcasted_iota(I32, flat, 1) // experts
     mean = dot(gates * dg, same.astype(F32), precision=HIGH)
     dgl = (gates * (dg - mean)).astype(LOW)
-    dgl_ref[...] = dgl
     pack_ref[rest_at : rest_at + 1, : tasks * experts] = jnp.sum(
         dgl.astype(F32), axis=0, keepdims=True
     )
@@ -664,68 +735,6 @@
         pack_ref[at : at + tasks * experts, :] = g_gating[:, part * 128 : (part + 1) * 128]
     small_ref[:, tasks * tower_hid :] = pack_ref[...].astype(LOW)
 
-    for turn in range(peers):
-        for step in range(1, peers):
-            x_copy(turn, step).wait_send()
-    for turn in range(peers - 1):
-        y_copy(turn).wait_send()
-    for step in range(1, peers):
-        d_copy(step).wait()
-
-
-def back_kernel(
-    dy_ref,
-    hid_ref,
-    slope_ref,
-    blocks_ref,
-    w_ref,
-    dgl_ref,
-    wg_ref,
-    small_ref,
-    dx_ref,
-    parts_ref,
-    b1_ref,
-    share_ref,
-    dpre_ref,
-    dx_send,
-    dx_recv,
-    core_recv,
-    pair_send,
-    pair_recv,
-    x_out,
-    x_in,
-    s_out,
-    s_in,
-):
-    peers, samples, width = blocks_ref.shape
-    here, _, out_width = dy_ref.shape
-    own = samples // peers
-    hid = hid_ref.shape[2]
-    shards, rows_both = w_ref.shape[0], w_ref.shape[2]
-    in_rows = peers * width // shards
-    out_rows = rows_both - in_rows
-    features = peers * width
-    dp = lax.axis_index("dp")
-    dp_side = lax.rem(dp, 2)
-    pair = dp + 1 - 2 * dp_side
-    me = meet(peers, pair)
-    side = lax.rem(me, 2)
-    near = me + 1 - 2 * side
-
-    def chunk_rows(turn):
-        return pl.ds(pl.multiple_of(lax.rem(me + turn, peers) * own, own), own)
-
-    def x_copy(turn, step):
-        target = lax.rem(me + step, peers)
-        rows = chunk_rows(turn)
-        return pltpu.make_async_remote_copy(
-            dx_send.at[target, rows],
-            dx_recv.at[me, rows],
-            x_out.at[turn, step],
-            x_in.at[turn, step],
-            device_id={"mp": target},
-            device_id_type=MESH,
-        )
 
     share = share_ref.shape[0]
 
@@ -757,28 +766,52 @@
         return mine + core_recv[share_rows(part), :].astype(F32)
 
     core_copy().start()
-    b1_ref[...] = jnp.zeros_like(b1_ref)
+    g_b1_ref[...] = jnp.zeros_like(g_b1_ref)
+
+    gate_ref[...] = dot(dgl, wg_ref[...])
+
+    def hand_on(turn):
+        rows = rows_of(back_chunk(turn))
+        g_help(turn).wait_recv()
+        total = dx_send[far, rows].astype(F32) + dx_help[rows].astype(F32)
+        dx_sum[rows] = total.astype(LOW)
+        g_far(turn).start()
+
+    act = jnp.ones((8, own), LOW)
 
     def chunk_step(turn, _):
-        rows = chunk_rows(turn)
-        mine = jnp.where(turn == 0, 1.0, 0.0)
-        gate = (dgl_ref[...].astype(F32) * mine).astype(LOW)
-        total = dot(gate, wg_ref[...])
+        chunk = back_chunk(turn)
+        rows = rows_of(chunk)
+
+        @pl.when(jnp.logical_and(turn < 2, chunk != me))
+        def _():
+            d_copy(0, chunk).wait_recv()
+
+        @pl.when(turn >= 2)
+        def _():
+            d_copy(1 + lax.rem(side + turn, 2), chunk).wait_recv()
+
+        total = gate_ref[...] * jnp.where(chunk == me, 1.0, 0.0)
         for e in range(here):
             w_out = w_ref[:, e, in_rows:, :].reshape(out_width, hid)
             dpre = (dot(dy_ref[e, rows, :], w_out) * slope_ref[e, rows, :]).astype(LOW)
             dpre_ref[e, rows, :] = dpre
-            b1_ref[e] += dot(jnp.ones((8, own), LOW), dpre)
+            g_b1_ref[e] += dot(act, dpre)
             w_in = w_ref[:, e, :in_rows, :].reshape(features, hid)
             total += dot(dpre, w_in, NT)
         for target in range(peers):
             dx_send[target, rows] = total[:, target * width : (target + 1) * width].astype(LOW)
-        for step in range(1, peers):
-            x_copy(turn, step).start()
+        g_near(turn).start()
+        g_help(turn).start()
+
+        @pl.when(turn > 0)
+        def _():
+            hand_on(turn - 1)
+
         return 0
 
     lax.fori_loop(0, peers, chunk_step, 0)
-
+    hand_on(peers - 1)
     core_copy().wait()
     pair_send[...] = core_sum(1 - dp_side).astype(LOW)
     pair_copy().start()
@@ -827,15 +860,20 @@
 
         lax.fori_loop(0, out_width // 128, out_step, 0)
 
-    for turn in range(peers):
-        for step in range(1, peers):
-            x_copy(turn, step).wait()
     pair_copy().wait()
     share_ref[...] = (core_sum(dp_side) + pair_recv[...].astype(F32)).astype(LOW)
-    total = dx_send[me].astype(F32)
-    for step in range(1, peers):
-        total = total + dx_recv[lax.rem(me + step, peers)].astype(F32)
-    dx_ref[...] = total
+    for turn in range(peers):
+        g_near(turn).wait()
+        g_far(turn).wait()
+    dx_ref[...] = dx_send[me].astype(F32) + dx_near[...].astype(F32) + dx_far[...].astype(F32)
+    for turn in range(peers):
+        g_help(turn).wait_send()
+        x_far(turn).wait_send()
+        x_near(turn).wait_send()
+        x_hand(turn).wait_send()
+    for relation, device in enumerate((near, far, across)):
+        y_copy(0, relation, device).wait_send()
+        d_copy(relation, device).wait_send()
 
 
 def total_kernel(
@@ -1100,20 +1138,26 @@
     def scratch(shape, kind=F32):
         return pltpu.VMEM(shape, kind)
 
-    blocks, hidden, slopes, output_rows, gate_logit_grad, small_grads, stat_parts = pl.pallas_call(
-        ahead_kernel,
+    pack_shape = (pack_rows // 4, TASKS * tower_hid + 128)
+    x_shape = (samples, tables_here * d_emb)
+    stat_parts, embed_grad, grad_parts, inner_parts, share = pl.pallas_call(
+        dense_kernel,
         out_shape=(
-            jax.ShapeDtypeStruct((mp_count, samples, tables_here * d_emb), LOW),
-            jax.ShapeDtypeStruct((experts_here, samples, hid), LOW),
-            jax.ShapeDtypeStruct((experts_here, samples, hid), F32),
-            jax.ShapeDtypeStruct((experts_here, samples, width_out), LOW),
-            jax.ShapeDtypeStruct((own, all_gates), LOW),
-            jax.ShapeDtypeStruct((pack_rows, TASKS * tower_hid + 128), LOW),
             jax.ShapeDtypeStruct((EXPERTS + TASKS + 2, 8, width_out), F32),
+            jax.ShapeDtypeStruct(x_shape, F32),
+            jax.ShapeDtypeStruct(
+                (2, dp_count // 2, mp_count, experts_here * in_out_rows, hid_here), LOW
+            ),
+            jax.ShapeDtypeStruct((experts_here, 8, hid), F32),
+            jax.ShapeDtypeStruct(pack_shape, LOW),
         ),
         in_specs=[SMEM] + [VMEM] * 9 + [SMEM] + [VMEM] * 2,
-        out_specs=(VMEM,) * 7,
+        out_specs=(VMEM,) * 5,
         scratch_shapes=[
+            scratch((mp_count,) + x_shape, LOW),
+            scratch((experts_here, samples, hid), LOW),
+            scratch((experts_here, samples, hid)),
+            scratch((experts_here, samples, width_out), LOW),
             scratch((mp_count, experts_here, own, width_out), LOW),
             scratch((mp_count, experts_here, own, width_out), LOW),
             scratch((own, all_gates)),
@@ -1121,19 +1165,34 @@
             scratch((TASKS, own, width_out)),
             scratch((own, all_gates)),
             scratch((EXPERTS, own, width_out), LOW),
+            scratch((pack_rows, TASKS * tower_hid + 128), LOW),
             scratch((pack_rows, 128)),
             scratch((own, hid)),
-            sems(mp_count, mp_count),
-            sems(mp_count, mp_count),
-            sems(mp_count),
-            sems(mp_count),
-            sems(mp_count),
-            sems(mp_count),
+            scratch((own, features)),
+            scratch((experts_here, samples, hid), LOW),
+            scratch((mp_count,) + x_shape, LOW),
+            scratch(x_shape, LOW),
+            scratch(x_shape, LOW),
+            scratch(x_shape, LOW),
+            scratch(x_shape, LOW),
+            scratch((2 * pack_shape[0], pack_shape[1]), LOW),
+            scratch(pack_shape, LOW),
+            scratch(pack_shape, LOW),
+            sems(3, mp_count),
+            sems(3, mp_count),
+            sems(3),
+            sems(3),
+            sems(3),
+            sems(3),
+            sems(3, mp_count),
+            sems(3, mp_count),
+            sems(2),
+            sems(2),
         ],
         compiler_params=pltpu.CompilerParams(
-            vmem_limit_bytes=56 * MIB, collective_id=0, has_side_effects=True
+            vmem_limit_bytes=60 * MIB, collective_id=0, has_side_effects=True
         ),
-        name="ahead",
+        name="dense",
     )(
         lax.dynamic_slice_in_dim(counts, lax.axis_index("dp"), 1, 0),
         embedded,
@@ -1149,36 +1208,6 @@
         labels,
         label_mask,
     )
-    pack_shape = (pack_rows // 4, TASKS * tower_hid + 128)
-    embed_grad, grad_parts, inner_parts, share = pl.pallas_call(
-        back_kernel,
-        out_shape=(
-            jax.ShapeDtypeStruct((samples, tables_here * d_emb), F32),
-            jax.ShapeDtypeStruct(
-                (2, dp_count // 2, mp_count, experts_here * in_out_rows, hid_here), LOW
-            ),
-            jax.ShapeDtypeStruct((experts_here, 8, hid), F32),
-            jax.ShapeDtypeStruct(pack_shape, LOW),
-        ),
-        in_specs=[VMEM] * 8,
-        out_specs=(VMEM,) * 4,
-        scratch_shapes=[
-            scratch((experts_here, samples, hid), LOW),
-            scratch((mp_count, samples, tables_here * d_emb), LOW),
-            scratch((mp_count, samples, tables_here * d_emb), LOW),
-            scratch((2 * pack_shape[0], pack_shape[1]), LOW),
-            scratch(pack_shape, LOW),
-            scratch(pack_shape, LOW),
-            sems(mp_count, mp_count),
-            sems(mp_count, mp_count),
-            sems(2),
-            sems(2),
-        ],
-        compiler_params=pltpu.CompilerParams(
-            vmem_limit_bytes=56 * MIB, collective_id=1, has_side_effects=True
-        ),
-        name="back",
-    )(output_rows, hidden, slopes, blocks, expert_w, gate_logit_grad, gating_low, small_grads)
 
     back_rows = pl.pallas_call(
         send_kernel,

time: 406 us -> 374 us (0.921)
  Pallas kernels: 285 us -> 252 us
    pallas_call x2 -> x1, Pallas kernels: 114 us -> 82.3 us  [body(): pl.pallas_call(dense_kernel, out_shape=(jax.ShapeDtypeStruct((EXPERTS + T...]
  transfers between devices with their start and end apart: 5 -> 5, of which waited for: 2 -> 2; matrix products, arithmetic and copies ran while one was open for 3% -> 4% of each run, Pallas kernels for 37% -> 39%
where the time goes in v4:
time: 374 us; the launch traced here: 373 us
  Pallas kernels  252 us (67%)
  waiting for transfers between devices  47.2 us (13%)
  other arithmetic  28.4 us (8%)
  local copies, waits for them, and re-layouts  20.1 us (5%)
  between operations  14.6 us (4%)
  starting transfers between devices  9.76 us (3%)
    pallas_call x1, Pallas kernels, body(): pl.pallas_call(dense_kernel, out_shape=(jax.ShapeDtypeStruct((EXPERTS + T...  82.3 us
    all_to_all x1, waiting for transfers between devices, body(): lax.all_to_all(found.reshape(devices, height, lanes), AXES, split_axis=0,...  39.5 us
    pallas_call x1, Pallas kernels, body(): pl.pallas_call(table_kernel, grid=(pairs,), out_shape=(jax.ShapeDtypeStru...  39.3 us
    pallas_call x1, Pallas kernels, body(): pl.pallas_call(swap_kernel, out_shape=(jax.ShapeDtypeStruct((devices, hei...  39.1 us
    pallas_call x1, Pallas kernels, body(): pl.pallas_call(functools.partial(find_kernel, mp_count), grid=(mp_count,)...  25.9 us
    pallas_call x1, Pallas kernels, body(): pl.pallas_call(functools.partial(add_kernel, mp_count), out_shape=(jax.Sh...  22.6 us
    pallas_call x1, Pallas kernels, body(): pl.pallas_call(functools.partial(total_kernel, features, width_out), out_...  15.2 us
    pallas_call x1, Pallas kernels, body(): pl.pallas_call(ask_kernel, out_shape=(jax.ShapeDtypeStruct((devices, 1, c...  13.6 us
  transfers between devices with their start and end apart: 5, of which 2 were waited for; matrix products, arithmetic and copies ran while one was open for 4% of the time, Pallas kernels for 39%

profile of v4, /device:TPU:0, one launch (start us, length us, event | category | flops | bytes accessed | tf_op | source)
XLA Modules:
  0.0 372.5 jit_solution(6120766268818869111)
XLA Ops:
  8.0 2.0 route.1
  10.0 1.1 copy.88
  11.1 1.0 copy.89
  12.2 13.6 %ask.1 = (s32[32,1,256]{2,1,0:T(1,128)S(1)}, bf16[2,192,512]{2,1,0:T(8,128)(2,1)}) custom-call(s32[32,1,256]{2,1,0:T(1,128)S(1)} %get-tuple-element.55.codes_ref, bf16[8,192,128]{2,1,0:T(8,128)(2,1)S(1)} %maximum_bitcast_fusion.shard_ref), custom_call_target="tpu_custom_call" | custom-call | tf_op jit(solution)/shard_map/ask/pallas_call | solution.py:1061
  27.1 25.9 %find.1 = bf16[8,4,128,128]{3,2,1,0:T(8,128)(2,1)} custom-call(s32[8192]{0:T(1024)} %bitcast.131, s32[32]{0:T(128)} %fusion.6.counts_ref, f32[16,64,4096]{2,1,0:T(8,128)} %bitcast.116), custom_call_target="tpu_custom_call" | custom-call | tf_op jit(solution)/shard_map/find/pallas_call | solution.py:1088
  53.0 3.6 all-to-all-start
  56.7 3.0 convert_element_type.57.w3_ref
  64.9 39.5 %all-to-all-done = bf16[32,128,128]{2,1,0:T(8,128)(2,1)S(1)} async-done(((bf16[32,128,128]{2,1,0:T(8,128)(2,1)}), bf16[32,128,128]{2,1,0:T(8,128)(2,1)S(1)}, u32[]{:S(2)}, u32[]{:S(2)}) %all-to-all-start) | async-done | bytes 1048608 | tf_op jit(solution)/shard_map/all_to_all | solution.py:1105
  104.4 5.0 %place.1.x_ref = bf16[1024,256]{1,0:T(8,128)(2,1)S(1)} custom-call(s32[4096]{0:T(1024)S(1)} %bitcast.110, bf16[4096,128]{1,0:T(8,128)(2,1)S(1)} %bitcast.106), custom_call_target="tpu_custom_call" | custom-call | tf_op jit(solution)/shard_map/place/pallas_call | solution.py:1108
  110.2 82.3 %dense.1 = (f32[15,8,512]{2,1,0:T(8,128)}, f32[1024,256]{1,0:T(8,128)}, bf16[2,4,4,384,128]{4,3,2,1,0:T(8,128)(2,1)}, f32[2,8,512]{2,1,0:T(8,128)}, bf16[128,1408]{1,0:T(8,128)(2,1)}) custom-call(s32[1]{0:T(128)} %dynamic_slice.10.count_ref, bf16[1024,256]{1,0:T(8,128)(2,1)} %copy-done, bf16[8,2,192,512]{3,2,1,0:T(8,128)(2,1)} %bitcast.128, ...), custom_call_target="tpu_custom_call" | custom-call | tf_op jit(solution)/shard_map/dense/pallas_call | solution.py:1143
  192.6 1.7 slice_bitcast_fusion
  194.9 7.4 %send.1 = bf16[4096,128]{1,0:T(8,128)(2,1)S(1)} custom-call(s32[4096]{0:T(1024)S(1)} %get-tuple-element.110.slot_ref, s32[4096]{0:T(1024)S(1)} %get-tuple-element.109.from_ref, f32[1024,256]{1,0:T(8,128)S(1)} %copy-done.2), custom_call_target="tpu_custom_call" | custom-call | tf_op jit(solution)/shard_map/send/pallas_call | solution.py:1212
  202.3 39.1 %swap.1 = (bf16[32,128,128]{2,1,0:T(8,128)(2,1)S(1)}, bf16[8,16,1408]{2,1,0:T(8,128)(2,1)S(1)}) custom-call(bf16[32,128,128]{2,1,0:T(8,128)(2,1)S(1)} %bitcast.107, bf16[8,16,1408]{2,1,0:T(8,128)(2,1)S(1)} %bitcast.109), custom_call_target="tpu_custom_call" | custom-call | tf_op jit(solution)/shard_map/swap/pallas_call | solution.py:1225
  241.4 1.0 copy-done.1
  242.4 1.6 fusion
  244.0 5.2 %all-to-all-start.1 = ((bf16[16,384,128]{2,1,0:T(8,128)(2,1)}), bf16[16,384,128]{2,1,0:T(8,128)(2,1)S(1)}, u32[]{:S(2)}, u32[]{:S(2)}) async-start(bf16[16,384,128]{2,1,0:T(8,128)(2,1)} %bitcast.122), calls=%async_computation.1 | async-start | bytes 3145728 | tf_op jit(solution)/shard_map/all_to_all | solution.py:1251
  251.8 22.6 %add.247 = (f32[32768,128]{1,0:T(8,128)}, f32[8,128]{1,0:T(8,128)}) custom-call(s32[8192]{0:T(1024)} %get-tuple-element.103.at_ref, s32[8192]{0:T(1024)} %get-tuple-element.102.part_at_ref, s32[32]{0:T(128)} %fusion.6.counts_ref, bf16[4096,128]{1,0:T(8,128)(2,1)} %bitcast.108), custom_call_target="tpu_custom_call" | custom-call | tf_op jit(solution)/shard_map/add/pallas_call | solution.py:1265
  274.4 7.6 %all-to-all-done.1 = bf16[16,384,128]{2,1,0:T(8,128)(2,1)S(1)} async-done(((bf16[16,384,128]{2,1,0:T(8,128)(2,1)}), bf16[16,384,128]{2,1,0:T(8,128)(2,1)S(1)}, u32[]{:S(2)}, u32[]{:S(2)}) %all-to-all-start.1) | async-done | bytes 1572896 | tf_op jit(solution)/shard_map/all_to_all | solution.py:1251
  283.0 15.2 %total.1 = (f32[4,8,128]{2,1,0:T(8,128)S(1)}, f32[8,128]{1,0:T(8,128)S(1)}) custom-call(s32[1]{0:T(128)} %bitcast.17.valid_ref, f32[2,8,512]{2,1,0:T(8,128)S(1)} %copy-done.5, f32[15,8,512]{2,1,0:T(8,128)S(1)} %copy-done.4, f32[8,128]{1,0:T(8,128)S(1)} %copy-done.8, f32[16,1408]{1,0:T(8,128)S(1)} %convert_reduce_fusion.1.shares_ref, f32[1536,128]{1,0:T(8,128)S(1)} %bitcast.105), custom_call_target="tpu_custom_call" | custom-call | tf_op jit(solution)/shard_map/total/pallas_call | solution.py:1285
  298.8 39.3 %tables.1 = (f32[16,64,4096]{2,1,0:T(8,128)}, f32[16,64,4096]{2,1,0:T(8,128)}, f32[16,64,4096]{2,1,0:T(8,128)}) custom-call(f32[8,128]{1,0:T(8,128)} %copy-done.7, f32[16,64,4096]{2,1,0:T(8,128)} %bitcast.117, f32[16,64,4096]{2,1,0:T(8,128)} %bitcast.118, f32[16,64,4096]{2,1,0:T(8,128)} %bitcast.119, f32[8,4096,128]{2,1,0:T(8,128)} %bitcast.120), custom_call_target="tpu_custom_call" | custom-call | tf_op jit(solution)/shard_map/tables/pallas_call | solution.py:1314
  338.1 1.4 fusion.17
  339.5 1.5 copy.70
  342.7 1.2 slice_bitcast_fusion.2
  343.9 1.3 slice_multiply_fusion.2
  345.2 1.3 slice_bitcast_fusion.5
  347.1 1.2 slice_bitcast_fusion.6
  348.3 8.9 %multiply_subtract_fusion = (f32[512,1280]{1,0:T(8,128)}, f32[512,1280]{1,0:T(8,128)}, f32[512,1280]{1,0:T(8,128)}) fusion(f32[512,1280]{1,0:T(8,128)} %param.41, f32[]{:T(128)} %bitcast.32, bf16[512,1408]{1,0:T(8,128)(2,1)S(1)} %bitcast.124, f32[512,1280]{1,0:T(8,128)} %param.42, f32[512,1280]{1,0:T(8,128)} %param.43), kind=kLoop, calls=%fused_computation.6 | loop fusion | flops 10485760 | bytes 17039364 | tf_op jit(solution)/shard_map/sub | solution.py:46
  357.3 1.3 pad_maximum_fusion
  358.7 2.3 fusion.14
  361.1 1.7 fusion.12
  362.9 1.3 multiply_subtract_fusion.4
  364.8 0.8 multiply_subtract_fusion.3
  (121 shorter events, 15.9 us)
Async XLA Ops:
  7.2 103.0 %all-gather.5.cloned.1.call-start = ((), (), s32[]{:S(2)}) async-start(), calls=%async_computation.2 | async-start | bytes 3538944 | tf_op jit(solution)/shard_map/all_gather | solution.py:1075
  53.0 6.7 %copy-start.29 = (s32[256,5]{0,1:T(8,128)S(1)}, s32[256,5]{0,1:T(8,128)}, u32[]{:S(2)}) copy-start(s32[256,5]{0,1:T(8,128)} %param.27) | copy-start | bytes 15364
  53.0 7.5 %copy-start.30 = (s32[256,5]{0,1:T(8,128)S(1)}, s32[256,5]{0,1:T(8,128)}, u32[]{:S(2)}) copy-start(s32[256,5]{0,1:T(8,128)} %param.28) | copy-start | bytes 15364
  53.0 51.4 %all-to-all-start = ((bf16[32,128,128]{2,1,0:T(8,128)(2,1)}), bf16[32,128,128]{2,1,0:T(8,128)(2,1)S(1)}, u32[]{:S(2)}, u32[]{:S(2)}) async-start(bf16[32,128,128]{2,1,0:T(8,128)(2,1)} %bitcast.125), calls=%async_computation | async-start | bytes 2097152 | tf_op jit(solution)/shard_map/all_to_all | solution.py:1105
  56.7 4.6 %copy-start.22 = (f32[9517]{0:T(1024)S(1)}, f32[9517]{0:T(1024)}, u32[]{:S(2)}) copy-start(f32[9517]{0:T(1024)} %param.47) | copy-start | bytes 114208
  56.7 5.3 %copy-start.35 = (s32[8]{0:T(128)S(1)}, s32[8]{0:T(128)}, u32[]{:S(2)}) copy-start(s32[8]{0:T(128)} %param.26) | copy-start | bytes 100
  56.7 7.6 %copy-start.13 = (f32[1024,40]{0,1:T(8,128)S(1)}, f32[1024,40]{0,1:T(8,128)}, u32[]{:S(2)}) copy-start(f32[1024,40]{0,1:T(8,128)} %param.38) | copy-start | bytes 491524
  192.6 9.7 %copy-start.3 = (bf16[128,1408]{1,0:T(8,128)(2,1)S(1)}, bf16[128,1408]{1,0:T(8,128)(2,1)}, u32[]{:S(2)}) copy-start(bf16[128,1408]{1,0:T(8,128)(2,1)} %get-tuple-element.59) | copy-start | bytes 1081348
  192.6 49.8 %copy-start.9 = (bf16[2,4,4,384,128]{4,3,2,1,0:T(8,128)(2,1)S(1)}, bf16[2,4,4,384,128]{4,3,2,1,0:T(8,128)(2,1)}, u32[]{:S(2)}) copy-start(bf16[2,4,4,384,128]{4,3,2,1,0:T(8,128)(2,1)} %get-tuple-element.63) | copy-start | bytes 9437188
  194.3 48.1 %collective-permute-start = (bf16[4,4,384,128]{3,2,1,0:T(8,128)(2,1)S(1)}, bf16[4,4,384,128]{3,2,1,0:T(8,128)(2,1)S(1)}, u32[]{:S(2)}, u32[]{:S(2)}) collective-permute-start(bf16[4,4,384,128]{3,2,1,0:T(8,128)(2,1)S(1)} %slice_bitcast_fusion), channel_id=1, source_target_pairs={{0,4},{4,0},{8,12},{12,8},{16,20},{20,16},{24,28},{28,24},{1,5},{5... | collective-permute-start | bytes 4718600 | tf_op jit(solution)/shard_map/ppermute | solution.py:1245
  244.0 7.2 %copy-start.17 = (s32[32,1,256]{2,1,0:T(1,128)S(1)}, s32[32,1,256]{2,1,0:T(1,128)}, u32[]{:S(2)}) copy-start(s32[32,1,256]{2,1,0:T(1,128)} %add_maximum_fusion) | copy-start | bytes 98308
  244.0 38.1 %all-to-all-start.1 = ((bf16[16,384,128]{2,1,0:T(8,128)(2,1)}), bf16[16,384,128]{2,1,0:T(8,128)(2,1)S(1)}, u32[]{:S(2)}, u32[]{:S(2)}) async-start(bf16[16,384,128]{2,1,0:T(8,128)(2,1)} %bitcast.122), calls=%async_computation.1 | async-start | bytes 3145728 | tf_op jit(solution)/shard_map/all_to_all | solution.py:1251
  249.1 33.2 %copy-start.4 = (f32[15,8,512]{2,1,0:T(8,128)S(1)}, f32[15,8,512]{2,1,0:T(8,128)}, u32[]{:S(2)}) copy-start(f32[15,8,512]{2,1,0:T(8,128)} %get-tuple-element.62.stats_ref) | copy-start | bytes 737284
  249.2 33.2 %copy-start.5 = (f32[2,8,512]{2,1,0:T(8,128)S(1)}, f32[2,8,512]{2,1,0:T(8,128)}, u32[]{:S(2)}) copy-start(f32[2,8,512]{2,1,0:T(8,128)} %get-tuple-element.61.inner_ref) | copy-start | bytes 98308
  249.2 90.3 %all-gather.7.cloned.1.call-start = ((), (), s32[]{:S(2)}) async-start(), calls=%async_computation.3 | async-start | bytes 1486848 | tf_op jit(solution)/shard_map/all_gather | solution.py:1243
  348.3 8.9 %copy-start.36 = (f32[13]{0:T(128)S(1)}, f32[13]{0:T(128)}, u32[]{:S(2)}) copy-start(f32[13]{0:T(128)} %slice_bitcast_fusion.5) | copy-start | bytes 160
  348.3 10.3 %copy-start.10 = (f32[128,8,128]{2,1,0:T(8,128)S(1)}, f32[128,8,128]{2,1,0:T(8,128)}, u32[]{:S(2)}) copy-start(f32[128,8,128]{2,1,0:T(8,128)} %param.32) | copy-start | bytes 1572868
  348.3 10.3 %copy-start.15 = (f32[128,8,128]{2,1,0:T(8,128)S(1)}, f32[128,8,128]{2,1,0:T(8,128)}, u32[]{:S(2)}) copy-start(f32[128,8,128]{2,1,0:T(8,128)} %param.33) | copy-start | bytes 1572868
  348.3 10.3 %copy-start.16 = (f32[128,8,128]{2,1,0:T(8,128)S(1)}, f32[128,8,128]{2,1,0:T(8,128)}, u32[]{:S(2)}) copy-start(f32[128,8,128]{2,1,0:T(8,128)} %param.34) | copy-start | bytes 1572868
  358.6 4.2 %copy-start.24 = (f32[4096]{0:T(1024)S(1)}, f32[4096]{0:T(1024)}, u32[]{:S(2)}) copy-start(f32[4096]{0:T(1024)} %slice_bitcast_fusion.1) | copy-start | bytes 49156
  358.6 4.2 %copy-start.28 = (f32[1280]{0:T(1024)S(1)}, f32[1280]{0:T(1024)}, u32[]{:S(2)}) copy-start(f32[1280]{0:T(1024)} %get-tuple-element.98) | copy-start | bytes 15364
  358.6 4.2 %copy-start.33 = (f32[5]{0:T(128)S(1)}, f32[5]{0:T(128)}, u32[]{:S(2)}) copy-start(f32[5]{0:T(128)} %slice_bitcast_fusion.3) | copy-start | bytes 64
  358.6 4.3 %copy-start.23 = (f32[9517]{0:T(1024)S(1)}, f32[9517]{0:T(1024)}, u32[]{:S(2)}) copy-start(f32[9517]{0:T(1024)} %param.47) | copy-start | bytes 114208
  358.6 4.2 %copy-start.25 = (f32[9517]{0:T(1024)S(1)}, f32[9517]{0:T(1024)}, u32[]{:S(2)}) copy-start(f32[9517]{0:T(1024)} %param.48) | copy-start | bytes 114208
  358.6 4.2 %copy-start.26 = (f32[9517]{0:T(1024)S(1)}, f32[9517]{0:T(1024)}, u32[]{:S(2)}) copy-start(f32[9517]{0:T(1024)} %param.49) | copy-start | bytes 114208
  358.7 5.5 %copy-start.27 = (f32[5,256]{1,0:T(8,128)S(1)}, f32[5,256]{1,0:T(8,128)}, u32[]{:S(2)}) copy-start(f32[5,256]{1,0:T(8,128)} %heads_ref.1) | copy-start | bytes 15364
  358.7 5.5 %copy-start.31 = (f32[5,256]{1,0:T(8,128)S(1)}, f32[5,256]{1,0:T(8,128)}, u32[]{:S(2)}) copy-start(f32[5,256]{1,0:T(8,128)} %param.45) | copy-start | bytes 15364
  358.7 5.5 %copy-start.32 = (f32[5,256]{1,0:T(8,128)S(1)}, f32[5,256]{1,0:T(8,128)}, u32[]{:S(2)}) copy-start(f32[5,256]{1,0:T(8,128)} %param.46) | copy-start | bytes 15364
  358.7 6.1 %copy-start.12 = (f32[320,128]{1,0:T(8,128)S(1)}, f32[320,128]{1,0:T(8,128)}, u32[]{:S(2)}) copy-start(f32[320,128]{1,0:T(8,128)} %slice_multiply_fusion.2) | copy-start | bytes 491524
  358.7 6.1 %copy-start.14 = (f32[1024,40]{0,1:T(8,128)S(1)}, f32[1024,40]{0,1:T(8,128)}, u32[]{:S(2)}) copy-start(f32[1024,40]{0,1:T(8,128)} %param.38) | copy-start | bytes 491524
  358.7 6.1 %copy-start.20 = (f32[1024,40]{0,1:T(8,128)S(1)}, f32[1024,40]{0,1:T(8,128)}, u32[]{:S(2)}) copy-start(f32[1024,40]{0,1:T(8,128)} %param.39) | copy-start | bytes 491524
  358.7 6.1 %copy-start.21 = (f32[1024,40]{0,1:T(8,128)S(1)}, f32[1024,40]{0,1:T(8,128)}, u32[]{:S(2)}) copy-start(f32[1024,40]{0,1:T(8,128)} %param.40) | copy-start | bytes 491524
  (10 other events, 21.7 us)
Sparse Core Ops, SparseCore 0:
  26.0 78.4 all-gather.4
  253.5 64.5 all-gather.6

commit v5 on v4

--- a/solution.py
+++ b/solution.py
@@ -195,18 +195,7 @@
     dp, mp = lax.axis_index("dp"), lax.axis_index("mp")
     mine = lax.div(dp, 2) * (peers // 2) + lax.div(mp, 2)
     me = dp * peers + mp
-    barrier = pltpu.get_barrier_semaphore()
-
-    def place_of(device):
-        return {"dp": lax.div(device, peers), "mp": lax.rem(device, peers)}
-
-    def greet(step, _):
-        target = lax.rem(me + step, devices)
-        pl.semaphore_signal(barrier, inc=1, device_id=place_of(target), device_id_type=MESH)
-        return 0
-
-    lax.fori_loop(1, devices, greet, 0)
-    pl.semaphore_wait(barrier, devices - 1)
+    greet_all(devices, peers, me)
 
     def r_copy(step):
         target = lax.rem(me + step, devices)
@@ -215,7 +204,7 @@
             out_ref.at[me],
             r_out.at[step],
             r_in.at[step],
-            device_id=place_of(target),
+            device_id=place_of(target, peers),
             device_id_type=MESH,
         )
 
@@ -346,6 +335,24 @@
     return me
 
 
+def greet_all(devices, peers, me):
+    barrier = pltpu.get_barrier_semaphore()
+
+    def greet(step, _):
+        target = lax.rem(me + step, devices)
+        pl.semaphore_signal(
+            barrier, inc=1, device_id=place_of(target, peers), device_id_type=MESH
+        )
+        return 0
+
+    lax.fori_loop(1, devices, greet, 0)
+    pl.semaphore_wait(barrier, devices - 1)
+
+
+def place_of(device, peers):
+    return {"dp": lax.div(device, peers), "mp": lax.rem(device, peers)}
+
+
 def ask_kernel(codes_ref, shard_ref, out_ref, full_ref, c_out, c_in, w_out, w_in):
     devices = codes_ref.shape[0]
     here, _, full = full_ref.shape
@@ -353,21 +360,10 @@
     peers = full // width
     mp = lax.axis_index("mp")
     me = lax.axis_index("dp") * peers + mp
-    barrier = pltpu.get_barrier_semaphore()
-
-    def place_of(device):
-        return {"dp": lax.div(device, peers), "mp": lax.rem(device, peers)}
-
-    def greet(step, _):
-        target = lax.rem(me + step, devices)
-        pl.semaphore_signal(barrier, inc=1, device_id=place_of(target), device_id_type=MESH)
-        return 0
-
-    lax.fori_loop(1, devices, greet, 0)
     columns = pl.ds(pl.multiple_of(mp * width, width), width)
     full_ref[:, :, columns] = shard_ref[pl.ds(mp * here, here)]
     out_ref[me] = codes_ref[me]
-    pl.semaphore_wait(barrier, devices - 1)
+    greet_all(devices, peers, me)
 
     def c_copy(step):
         target = lax.rem(me + step, devices)
@@ -376,7 +372,7 @@
             out_ref.at[me],
             c_out.at[step],
             c_in.at[step],
-            device_id=place_of(target),
+            device_id=place_of(target, peers),
             device_id_type=MESH,
         )
 
@@ -408,9 +404,18 @@
 
 
 def dense_kernel(
+    lines,
+    *refs,
+):
+    mine, theirs = refs[:lines], refs[lines : 2 * lines]
+    dense_part(mine, theirs, *refs[2 * lines :])
+
+
+def dense_part(
+    mine_refs,
+    theirs_refs,
     count_ref,
     x_ref,
-    w_ref,
     b1_ref,
     b2_ref,
     wg_ref,
@@ -426,6 +431,7 @@
     parts_ref,
     g_b1_ref,
     share_ref,
+    w_ref,
     blocks_ref,
     hid_ref,
     slope_ref,
@@ -460,6 +466,7 @@
     g_in,
     s_out,
     s_in,
+    w_in_sem,
 ):
     peers, samples, width = blocks_ref.shape
     here = hid_ref.shape[0]
@@ -475,6 +482,20 @@
     dp = lax.axis_index("dp")
     dp_side = lax.rem(dp, 2)
     pair = dp + 1 - 2 * dp_side
+    lines = len(mine_refs)
+    w_copies = []
+    for at in range(lines):
+        first = lax.rem(lax.div(dp, 2) + lines - at, lines) * 2
+        w_copies += [
+            pltpu.make_async_copy(
+                mine_refs[at], w_ref.at[first + dp_side], w_in_sem.at[0, at]
+            ),
+            pltpu.make_async_copy(
+                theirs_refs[at], w_ref.at[first + 1 - dp_side], w_in_sem.at[1, at]
+            ),
+        ]
+    for copy in w_copies:
+        copy.start()
     me = meet(peers, pair)
     side = lax.rem(me, 2)
     chip = lax.div(me, 2)
@@ -550,6 +571,8 @@
         x_near(turn).start()
     blocks_ref[me] = x_ref[...]
     limit = count_ref[0]
+    for copy in w_copies:
+        copy.wait()
 
     x_far(0).wait_recv()
     x_hand(0).start()
@@ -900,12 +923,9 @@
     me = lax.axis_index("dp") * peers + lax.axis_index("mp")
     barrier = pltpu.get_barrier_semaphore()
 
-    def place_of(device):
-        return {"dp": lax.div(device, peers), "mp": lax.rem(device, peers)}
-
     def greet(step, _):
         target = lax.rem(me + step, devices)
-        pl.semaphore_signal(barrier, inc=1, device_id=place_of(target), device_id_type=MESH)
+        pl.semaphore_signal(barrier, inc=1, device_id=place_of(target, peers), device_id_type=MESH)
         return 0
 
     lax.fori_loop(1, devices, greet, 0)
@@ -941,7 +961,7 @@
             got_ref.at[me],
             t_out.at[step],
             t_in.at[step],
-            device_id=place_of(target),
+            device_id=place_of(target, peers),
             device_id_type=MESH,
         )
 
@@ -987,6 +1007,88 @@
     results = adamw(weight_ref[...], first_ref[...], second_ref[...], gradient, rate_table)
     for out, result in zip(outs, results):
         out[...] = result
+
+
+def small_kernel(
+    tasks,
+    experts,
+    result_ref,
+    whole_ref,
+    t0_ref,
+    t1_ref,
+    t2_ref,
+    g0_ref,
+    g1_ref,
+    g2_ref,
+    h0_ref,
+    h1_ref,
+    h2_ref,
+    t0_out,
+    t1_out,
+    t2_out,
+    g0_out,
+    g1_out,
+    g2_out,
+    h0_out,
+    h1_out,
+    h2_out,
+    pack_ref,
+):
+    step = pl.program_id(0)
+    peers = lax.axis_size("mp")
+    groups = lax.axis_size("dp")
+    rows, width = t0_ref.shape
+    unit = whole_ref.shape[1]
+    factor = result_ref[:1, :1]
+    core, side = lax.div(step, 2), lax.rem(step, 2)
+    for first in range(groups // 2):
+        for second in range(peers // 2):
+            source = (2 * first + side) * peers + 2 * second + core
+            at = (first * (peers // 2) + second) * unit
+            value = whole_ref[source]
+            here = slice(at, at + unit)
+            results = adamw(
+                t0_ref[here, :],
+                t1_ref[here, :],
+                t2_ref[here, :],
+                value[:, :width].astype(F32) * factor,
+                rate_dense,
+            )
+            for out, result in zip((t0_out, t1_out, t2_out), results):
+                out[here, :] = result
+            pack_ref[pl.ds(step * rows + at, unit), :] = value[:, width:].astype(F32)
+
+    @pl.when(step == pl.num_programs(0) - 1)
+    def _():
+        gates = tasks * experts
+        features = g0_ref.shape[1]
+        for part in range(features // 128):
+            lane = slice(part * 128, (part + 1) * 128)
+            results = adamw(
+                g0_ref[:, lane],
+                g1_ref[:, lane],
+                g2_ref[:, lane],
+                pack_ref[part * gates : (part + 1) * gates, :] * factor,
+                rate_dense,
+            )
+            for out, result in zip((g0_out, g1_out, g2_out), results):
+                out[:, lane] = result
+        heads_at = features // 128 * gates
+        parts = h0_ref.shape[1] // 128
+        for task in range(tasks):
+            for part in range(parts):
+                lane = slice(part * 128, (part + 1) * 128)
+                at = heads_at + task * parts + part
+                row = slice(task, task + 1)
+                results = adamw(
+                    h0_ref[row, lane],
+                    h1_ref[row, lane],
+                    h2_ref[row, lane],
+                    pack_ref[at : at + 1, :] * factor,
+                    rate_dense,
+                )
+                for out, result in zip((h0_out, h1_out, h2_out), results):
+                    out[row, lane] = result
 
 
 def body(
@@ -1054,6 +1156,18 @@
     in_out_rows = in_rows + out_rows
     hid_here = hid // mp_count
     shard = jnp.concatenate([expert_in, expert_out], axis=0).astype(LOW).transpose(1, 0, 2)
+    sides = [
+        [d * mp_count + m for d in range(x, dp_count, 2) for m in range(mp_count)] for x in range(2)
+    ]
+    partners = [(d, d ^ 1) for d in range(dp_count)]
+
+    def exchange_side(parts):
+        return lax.all_to_all(
+            parts, AXES, split_axis=0, concat_axis=0, axis_index_groups=sides, tiled=True
+        )
+
+    def exchange_all(parts):
+        return lax.all_to_all(parts, AXES, split_axis=0, concat_axis=0, tiled=True)
 
     def sems(*shape):
         return pltpu.SemaphoreType.DMA(shape)
@@ -1072,7 +1186,11 @@
         ),
         name="ask",
     )(outgoing, shard)
-    expert_w = lax.all_gather(shard, "dp", axis=0, tiled=False)
+    w_far = []
+    for ahead in range(1, dp_count // 2):
+        steps = [(d, (d + 2 * ahead) % dp_count) for d in range(dp_count)]
+        w_far.append(lax.ppermute(shard, "dp", steps))
+    w_near = lax.ppermute(shard, "dp", partners)
     codes = codes.reshape(devices, capacity)
     asked = codes[:, 0] >> 16
     plain = codes & 65535
@@ -1102,9 +1220,10 @@
         compiler_params=params(60),
         name="find",
     )(found_at.reshape(-1), asked, table_view)
-    returned = lax.all_to_all(
-        found.reshape(devices, height, lanes), AXES, split_axis=0, concat_axis=0, tiled=True
-    )
+    w_far, w_near, found = lax.optimization_barrier((w_far, w_near, found))
+    w_mine = [shard] + w_far
+    w_theirs = [w_near] + [lax.ppermute(line, "dp", partners) for line in w_far]
+    returned = exchange_all(found.reshape(devices, height, lanes))
     embedded = pl.pallas_call(
         place_kernel,
         out_shape=jax.ShapeDtypeStruct((samples, tables_here * d_emb), LOW),
@@ -1141,7 +1260,7 @@
     pack_shape = (pack_rows // 4, TASKS * tower_hid + 128)
     x_shape = (samples, tables_here * d_emb)
     stat_parts, embed_grad, grad_parts, inner_parts, share = pl.pallas_call(
-        dense_kernel,
+        functools.partial(dense_kernel, dp_count // 2),
         out_shape=(
             jax.ShapeDtypeStruct((EXPERTS + TASKS + 2, 8, width_out), F32),
             jax.ShapeDtypeStruct(x_shape, F32),
@@ -1151,9 +1270,14 @@
             jax.ShapeDtypeStruct((experts_here, 8, hid), F32),
             jax.ShapeDtypeStruct(pack_shape, LOW),
         ),
-        in_specs=[SMEM] + [VMEM] * 9 + [SMEM] + [VMEM] * 2,
+        in_specs=[pl.BlockSpec(memory_space=pl.ANY)] * dp_count
+        + [SMEM]
+        + [VMEM] * 8
+        + [SMEM]
+        + [VMEM] * 2,
         out_specs=(VMEM,) * 5,
         scratch_shapes=[
+            scratch((dp_count, experts_here, in_out_rows, hid), LOW),
             scratch((mp_count,) + x_shape, LOW),
             scratch((experts_here, samples, hid), LOW),
             scratch((experts_here, samples, hid)),
@@ -1188,15 +1312,17 @@
             sems(3, mp_count),
             sems(2),
             sems(2),
+            sems(2, dp_count // 2),
         ],
         compiler_params=pltpu.CompilerParams(
             vmem_limit_bytes=60 * MIB, collective_id=0, has_side_effects=True
         ),
         name="dense",
     )(
+        *w_mine,
+        *w_theirs,
         lax.dynamic_slice_in_dim(counts, lax.axis_index("dp"), 1, 0),
         embedded,
-        expert_w,
         inner_here,
         outer_here,
         gating_low,
@@ -1236,25 +1362,12 @@
         ),
         name="swap",
     )(back_rows.reshape(devices, height, lanes), share)
-    def exchange_all(parts):
-        return lax.all_to_all(parts, AXES, split_axis=0, concat_axis=0, tiled=True)
-
     share = jnp.sum(shares.astype(F32), axis=0)
-    whole = lax.all_gather(share.astype(LOW), AXES, axis=0, tiled=False)
-
-    partner = lax.ppermute(grad_parts[1], "dp", [(d, d ^ 1) for d in range(dp_count)])
+    partner = lax.ppermute(grad_parts[1], "dp", partners)
     partner, arrived = lax.optimization_barrier((partner, arrived))
     grad_parts = (grad_parts[0].astype(F32) + partner.astype(F32)).astype(LOW)
-    sides = [
-        [d * mp_count + m for d in range(x, dp_count, 2) for m in range(mp_count)] for x in range(2)
-    ]
-    grad_parts = lax.all_to_all(
-        grad_parts.reshape(devices // 2, experts_here * in_out_rows, hid_here),
-        AXES,
-        split_axis=0,
-        concat_axis=0,
-        axis_index_groups=sides,
-        tiled=True,
+    grad_parts = exchange_side(
+        grad_parts.reshape(devices // 2, experts_here * in_out_rows, hid_here)
     )
     grad_sum = jnp.sum(
         grad_parts.reshape(dp_count // 2, mp_count, experts_here, in_out_rows, -1).astype(F32), 0
@@ -1269,7 +1382,7 @@
             jax.ShapeDtypeStruct((8, lanes), F32),
         ),
         in_specs=[SMEM, SMEM, SMEM, VMEM],
-        out_specs=(pl.BlockSpec(memory_space=pl.ANY), VMEM),
+        out_specs=(VMEM, VMEM),
         scratch_shapes=[
             pltpu.VMEM((4 * slots + 8, lanes), F32),
             pltpu.SemaphoreType.DMA((mp_count,)),
@@ -1309,6 +1422,8 @@
         grad_sum.reshape(-1, 128),
     )
     factor = result[0, 0]
+    share_low, result = lax.optimization_barrier((share.astype(LOW), result))
+    whole = exchange_all(jnp.broadcast_to(share_low[None], (devices,) + share_low.shape))
 
     table_spec = pl.BlockSpec((2, d_emb, rows_dev), lambda p: (p, 0, 0))
     embed_out = pl.pallas_call(
@@ -1323,7 +1438,7 @@
             pl.BlockSpec((1, rows_dev, lanes), lambda p: (p, 0, 0)),
         ],
         out_specs=(table_spec,) * 3,
-        compiler_params=params(58),
+        compiler_params=params(40),
         name="tables",
     )(
         result,
@@ -1336,18 +1451,49 @@
     in_out = adamw(expert_in, in_first, in_second, in_sum * factor, rate_dense)
     out_out = adamw(expert_out, out_first, out_second, out_sum * factor, rate_dense)
     whole, embed_out = lax.optimization_barrier((whole, embed_out))
-    whole = whole.reshape(dp_count // 2, 2, mp_count // 2, 2, pack_rows // devices, -1)
-    whole = whole.transpose(3, 1, 0, 2, 4, 5).reshape(pack_rows, -1)
-    towers_sum = whole[:, : TASKS * tower_hid].astype(F32)
-    packed = whole[:, TASKS * tower_hid :].astype(F32)
     blocks_x = features // 128
     heads_at = blocks_x * all_gates
     tower_at = heads_at + TASKS * tower_hid // 128
     outer_at = tower_at + TASKS * tower_hid // 128
     rest_at = outer_at + EXPERTS * width_out // 128
-    gating_sum = packed[:heads_at].reshape(blocks_x, all_gates, 128).transpose(1, 0, 2)
-    gating_sum = gating_sum.reshape(all_gates, features).T
-    heads_sum = packed[heads_at:tower_at].reshape(TASKS, tower_hid)
+    tower_spec = pl.BlockSpec((pack_rows // 4, TASKS * tower_hid), lambda c: (c, 0))
+    gate_spec = pl.BlockSpec((all_gates, features), lambda c: (0, 0))
+    head_spec = pl.BlockSpec((TASKS, tower_hid), lambda c: (0, 0))
+    *small_out, packed = pl.pallas_call(
+        functools.partial(small_kernel, TASKS, EXPERTS),
+        grid=(4,),
+        out_shape=(jax.ShapeDtypeStruct(towers.shape, F32),) * 3
+        + (jax.ShapeDtypeStruct((all_gates, features), F32),) * 3
+        + (jax.ShapeDtypeStruct(heads.shape, F32),) * 3
+        + (jax.ShapeDtypeStruct((pack_rows, 128), F32),),
+        in_specs=[
+            pl.BlockSpec((8, 128), lambda c: (0, 0)),
+            pl.BlockSpec(whole.shape, lambda c: (0, 0, 0)),
+        ]
+        + [tower_spec] * 3
+        + [gate_spec] * 3
+        + [head_spec] * 3,
+        out_specs=(tower_spec,) * 3
+        + (gate_spec,) * 3
+        + (head_spec,) * 3
+        + (pl.BlockSpec((pack_rows, 128), lambda c: (0, 0)),),
+        compiler_params=params(48),
+        name="small",
+    )(
+        result,
+        whole,
+        towers,
+        towers_first,
+        towers_second,
+        gating.T,
+        gating_first.T,
+        gating_second.T,
+        heads,
+        heads_first,
+        heads_second,
+    )
+    towers_out, heads_out = small_out[:3], small_out[6:]
+    gating_out = [value.T for value in small_out[3:6]]
     bias_sum = jnp.concatenate(
         [
             inner_sum.reshape(-1),
@@ -1357,9 +1503,6 @@
             packed[rest_at + 1, :TASKS],
         ]
     )
-    gating_out = adamw(gating, gating_first, gating_second, gating_sum * factor, rate_dense)
-    towers_out = adamw(towers, towers_first, towers_second, towers_sum * factor, rate_dense)
-    heads_out = adamw(heads, heads_first, heads_second, heads_sum * factor, rate_dense)
     biases_out = adamw(biases, biases_first, biases_second, bias_sum * factor, rate_dense)
     stats = jnp.concatenate([result[3, stat_end + 2][None], result[3, 2 : stat_end + 2]])
     loss = result[2, :2]

time: 374 us -> 354 us (0.947)
  starting transfers between devices: 9.76 us -> 30.3 us
  waiting for transfers between devices: 47.2 us -> 29.3 us
  between operations: 14.6 us -> 1.23 us
  other arithmetic: 28.4 us -> 15.9 us
  Pallas kernels: 252 us -> 259 us
    all_to_all x2 -> x3, waiting for transfers between devices: 47.1 us -> 22.3 us  [the longest x2 16 us: exchange_all(): return lax.all_to_all(parts, AXES, split_axis=0, concat_axis=0, tiled=True)]
    all_to_all x2 -> x3, starting transfers between devices: 8.83 us -> 20.7 us  [the longest x2 14.5 us: exchange_all(): return lax.all_to_all(parts, AXES, split_axis=0, concat_axis=0, tiled=True)]
    sub x4 -> x1, other arithmetic: 11.7 us -> 2.13 us  [adamw(): weight - rate * (corrected / (scaled + adam_eps) + decay * weight)]
    ppermute x1 -> x8, starting transfers between devices: 0.63 us -> 9.55 us  [the longest x3 3.88 us: body(): w_far.append(lax.ppermute(shard, 'dp', steps))]
    ppermute x1 -> x8, waiting for transfers between devices: 0.01 us -> 7.05 us  [the longest x3 7.03 us: body(): w_theirs = [w_near] + [lax.ppermute(line, 'dp', partners) for line in w_far]]
    pallas_call x1 -> x2, Pallas kernels: 82.3 us -> 88.4 us  [the longest x1 80.4 us: body(): pl.pallas_call(functools.partial(dense_kernel, dp_count // 2), out_shape=...]
    unnamed x86 -> x76, local copies, waits for them, and re-layouts: 7.8 us -> 8.83 us
  transfers between devices with their start and end apart: 5 -> 11, of which waited for: 2 -> 3; matrix products, arithmetic and copies ran while one was open for 4% -> 5% of each run, Pallas kernels for 39% -> 38%
where the time goes in v5:
time: 354 us; the launch traced here: 353 us
  Pallas kernels  259 us (73%)
  starting transfers between devices  30.3 us (9%)
  waiting for transfers between devices  29.3 us (8%)
  local copies, waits for them, and re-layouts  17.2 us (5%)
  other arithmetic  15.9 us (4%)
    pallas_call x1, Pallas kernels, body(): pl.pallas_call(functools.partial(dense_kernel, dp_count // 2), out_shape=...  80.4 us
    pallas_call x1, Pallas kernels, body(): pl.pallas_call(swap_kernel, out_shape=(jax.ShapeDtypeStruct((devices, hei...  39.2 us
    pallas_call x1, Pallas kernels, body(): pl.pallas_call(table_kernel, grid=(pairs,), out_shape=(jax.ShapeDtypeStru...  38.9 us
    pallas_call x1, Pallas kernels, body(): pl.pallas_call(functools.partial(find_kernel, mp_count), grid=(mp_count,)...  25.6 us
    pallas_call x1, Pallas kernels, body(): pl.pallas_call(functools.partial(add_kernel, mp_count), out_shape=(jax.Sh...  23.5 us
    all_to_all x2, waiting for transfers between devices, exchange_all(): return lax.all_to_all(parts, AXES, split_axis=0, concat_axis=0, tiled=True)  16 us
    pallas_call x1, Pallas kernels, body(): pl.pallas_call(functools.partial(total_kernel, features, width_out), out_...  15.7 us
    all_to_all x2, starting transfers between devices, exchange_all(): return lax.all_to_all(parts, AXES, split_axis=0, concat_axis=0, tiled=True)  14.5 us
  transfers between devices with their start and end apart: 11, of which 3 were waited for; matrix products, arithmetic and copies ran while one was open for 5% of the time, Pallas kernels for 38%

profile of v5, /device:TPU:0, one launch (start us, length us, event | category | flops | bytes accessed | tf_op | source)
XLA Modules:
  0.0 352.8 jit_solution(3858741561461034836)
XLA Ops:
  1.4 2.0 route.1
  3.4 1.1 copy.74
  4.6 1.0 copy.75
  5.6 12.9 %ask.1 = (s32[32,1,256]{2,1,0:T(1,128)S(1)}, bf16[2,192,512]{2,1,0:T(8,128)(2,1)S(1)}) custom-call(s32[32,1,256]{2,1,0:T(1,128)S(1)} %get-tuple-element.71.codes_ref, bf16[8,192,128]{2,1,0:T(8,128)(2,1)S(1)} %maximum_bitcast_fusion.shard_ref), custom_call_target="tpu_custom_call" | custom-call | tf_op jit(solution)/shard_map/ask/pallas_call | solution.py:1175
  20.1 2.3 collective-permute-start.2
  24.3 25.6 %find.1 = bf16[8,4,128,128]{3,2,1,0:T(8,128)(2,1)} custom-call(s32[8192]{0:T(1024)} %bitcast.106, s32[32]{0:T(128)} %fusion.4.counts_ref, f32[16,64,4096]{2,1,0:T(8,128)} %bitcast.97), custom_call_target="tpu_custom_call" | custom-call | tf_op jit(solution)/shard_map/find/pallas_call | solution.py:1206
  50.7 8.2 %all-to-all-start = ((bf16[32,128,128]{2,1,0:T(8,128)(2,1)}), bf16[32,128,128]{2,1,0:T(8,128)(2,1)}, u32[]{:S(2)}, u32[]{:S(2)}) async-start(bf16[32,128,128]{2,1,0:T(8,128)(2,1)} %bitcast.103), calls=%async_computation | async-start | bytes 2097152 | tf_op jit(solution)/shard_map/all_to_all | solution.py:1170
  59.5 1.5 collective-permute-start.4
  61.6 1.5 collective-permute-start.6
  63.7 1.2 convert_element_type.38.refs_14_
  68.9 16.0 %all-to-all-done = bf16[32,128,128]{2,1,0:T(8,128)(2,1)} async-done(((bf16[32,128,128]{2,1,0:T(8,128)(2,1)}), bf16[32,128,128]{2,1,0:T(8,128)(2,1)}, u32[]{:S(2)}, u32[]{:S(2)}) %all-to-all-start) | async-done | bytes 1048608 | tf_op jit(solution)/shard_map/all_to_all | solution.py:1170
  84.9 5.4 %place.1.refs_9_ = bf16[1024,256]{1,0:T(8,128)(2,1)S(1)} custom-call(s32[4096]{0:T(1024)S(1)} %bitcast.91, bf16[4096,128]{1,0:T(8,128)(2,1)} %bitcast.5.rows_ref), custom_call_target="tpu_custom_call" | custom-call | tf_op jit(solution)/shard_map/place/pallas_call | solution.py:1227
  91.2 7.0 %collective-permute-done.6.refs_7_ = bf16[2,192,512]{2,1,0:T(8,128)(2,1)} collective-permute-done((bf16[2,192,512]{2,1,0:T(8,128)(2,1)}, bf16[2,192,512]{2,1,0:T(8,128)(2,1)}, u32[]{:S(2)}, u32[]{:S(2)}) %collective-permute-start.6) | collective-permute-done | bytes 393248 | tf_op jit(solution)/shard_map/ppermute | solution.py:1225
  98.2 80.4 %dense.1 = (f32[15,8,512]{2,1,0:T(8,128)}, f32[1024,256]{1,0:T(8,128)}, bf16[2,4,4,384,128]{4,3,2,1,0:T(8,128)(2,1)}, f32[2,8,512]{2,1,0:T(8,128)}, bf16[128,1408]{1,0:T(8,128)(2,1)}) custom-call(bf16[2,192,512]{2,1,0:T(8,128)(2,1)} %copy-done.6, bf16[2,192,512]{2,1,0:T(8,128)(2,1)} %copy-done.22, bf16[2,192,512]{2,1,0:T(8,128)(2,1)} %collective-permute-done.1.refs_2_, ...), custom_call_target="tpu_custom_call" | custom-call | tf_op jit(solution)/shard_map/dense/pallas_call | solution.py:1262
  178.7 1.7 slice_bitcast_fusion
  180.4 1.5 collective-permute-start.7
  181.9 7.4 %send.1 = bf16[4096,128]{1,0:T(8,128)(2,1)S(1)} custom-call(s32[4096]{0:T(1024)S(1)} %get-tuple-element.132.slot_ref, s32[4096]{0:T(1024)S(1)} %get-tuple-element.131.from_ref, f32[1024,256]{1,0:T(8,128)S(1)} %copy-done.3), custom_call_target="tpu_custom_call" | custom-call | tf_op jit(solution)/shard_map/send/pallas_call | solution.py:1338
  189.2 39.2 %swap.1 = (bf16[32,128,128]{2,1,0:T(8,128)(2,1)S(1)}, bf16[8,16,1408]{2,1,0:T(8,128)(2,1)S(1)}) custom-call(bf16[32,128,128]{2,1,0:T(8,128)(2,1)S(1)} %bitcast.85, bf16[8,16,1408]{2,1,0:T(8,128)(2,1)S(1)} %bitcast.88), custom_call_target="tpu_custom_call" | custom-call | tf_op jit(solution)/shard_map/swap/pallas_call | solution.py:1351
  229.4 1.6 fusion
  231.0 6.3 %all-to-all-start.1 = ((bf16[16,384,128]{2,1,0:T(8,128)(2,1)}), bf16[16,384,128]{2,1,0:T(8,128)(2,1)}, u32[]{:S(2)}, u32[]{:S(2)}) async-start(bf16[16,384,128]{2,1,0:T(8,128)(2,1)} %bitcast.102), calls=%async_computation.1 | async-start | bytes 3145728 | tf_op jit(solution)/shard_map/all_to_all | solution.py:1165
  239.5 23.5 %add.166 = (f32[32768,128]{1,0:T(8,128)}, f32[8,128]{1,0:T(8,128)}) custom-call(s32[8192]{0:T(1024)} %get-tuple-element.126.at_ref, s32[8192]{0:T(1024)} %get-tuple-element.125.part_at_ref, s32[32]{0:T(128)} %fusion.4.counts_ref, bf16[4096,128]{1,0:T(8,128)(2,1)} %bitcast.86), custom_call_target="tpu_custom_call" | custom-call | tf_op jit(solution)/shard_map/add/pallas_call | solution.py:1378
  263.0 6.2 %all-to-all-done.1 = bf16[16,384,128]{2,1,0:T(8,128)(2,1)} async-done(((bf16[16,384,128]{2,1,0:T(8,128)(2,1)}), bf16[16,384,128]{2,1,0:T(8,128)(2,1)}, u32[]{:S(2)}, u32[]{:S(2)}) %all-to-all-start.1) | async-done | bytes 1572896 | tf_op jit(solution)/shard_map/all_to_all | solution.py:1165
  269.3 1.7 convert_reduce_fusion
  272.6 15.7 %total.1 = (f32[4,8,128]{2,1,0:T(8,128)S(1)}, f32[8,128]{1,0:T(8,128)S(1)}) custom-call(s32[1]{0:T(128)} %bitcast.15.valid_ref, f32[2,8,512]{2,1,0:T(8,128)S(1)} %copy-done.12, f32[15,8,512]{2,1,0:T(8,128)S(1)} %copy-done.8, f32[8,128]{1,0:T(8,128)S(1)} %copy-done.16, f32[16,1408]{1,0:T(8,128)S(1)} %convert_reduce_fusion.1.shares_ref, f32[1536,128]{1,0:T(8,128)S(1)} %bitcast.84), custom_call_target="tpu_custom_call" | custom-call | tf_op jit(solution)/shard_map/total/pallas_call | solution.py:1398
  288.3 1.2 broadcast_in_dim.7
  289.5 6.3 %all-to-all-start.2 = ((bf16[32,16,1408]{2,1,0:T(8,128)(2,1)}), bf16[32,16,1408]{2,1,0:T(8,128)(2,1)}, u32[]{:S(2)}, u32[]{:S(2)}) async-start(bf16[32,16,1408]{2,1,0:T(8,128)(2,1)} %broadcast_in_dim.7), calls=%async_computation.2 | async-start | bytes 2883584 | tf_op jit(solution)/shard_map/all_to_all | solution.py:1170
  297.1 38.9 %tables.1 = (f32[16,64,4096]{2,1,0:T(8,128)}, f32[16,64,4096]{2,1,0:T(8,128)}, f32[16,64,4096]{2,1,0:T(8,128)}) custom-call(f32[8,128]{1,0:T(8,128)S(1)} %get-tuple-element.92.factor_ref.result_ref, f32[16,64,4096]{2,1,0:T(8,128)} %bitcast.98, f32[16,64,4096]{2,1,0:T(8,128)} %bitcast.99, f32[16,64,4096]{2,1,0:T(8,128)} %bitcast.100, f32[8,4096,128]{2,1,0:T(8,128)} %bitcast.101), custom_call_target="tpu_custom_call" | custom-call | tf_op jit(solution)/shard_map/tables/pallas_call | solution.py:1429
  336.6 1.2 pad_maximum_fusion
  338.5 1.8 fusion.6
  340.3 2.2 fusion.8
  342.6 8.0 %small.1 = (f32[512,1280]{1,0:T(8,128)}, f32[512,1280]{1,0:T(8,128)}, f32[512,1280]{1,0:T(8,128)}, f32[40,1024]{1,0:T(8,128)}, f32[40,1024]{1,0:T(8,128)}, /*ind...) custom-call(f32[8,128]{1,0:T(8,128)S(1)} %get-tuple-element.92.factor_ref, ...), custom_call_target="tpu_custom_call" | custom-call | tf_op jit(solution)/shard_map/small/pallas_call | solution.py:1462
  350.7 2.1 multiply_subtract_fusion.2
  (117 shorter events, 18.8 us)
Async XLA Ops:
  18.5 31.5 %copy-start.6 = (bf16[2,192,512]{2,1,0:T(8,128)(2,1)}, bf16[2,192,512]{2,1,0:T(8,128)(2,1)S(1)}, u32[]{:S(2)}) copy-start(bf16[2,192,512]{2,1,0:T(8,128)(2,1)S(1)} %get-tuple-element.72.refs_0_) | copy-start | bytes 1179652
  18.5 31.4 %collective-permute-start = (bf16[2,192,512]{2,1,0:T(8,128)(2,1)S(1)}, bf16[2,192,512]{2,1,0:T(8,128)(2,1)S(1)}, u32[]{:S(2)}, u32[]{:S(2)}) collective-permute-start(bf16[2,192,512]{2,1,0:T(8,128)(2,1)S(1)} %get-tuple-element.72.refs_0_), channel_id=1, source_target_pairs={{0,8},{4,12},{8,16},{12,20},{16,24},{20,28},{24,0},{28,4},{1,9},{5... | collective-permute-start | bytes 1179656 | tf_op jit(solution)/shard_map/ppermute | solution.py:1192
  19.3 30.7 %collective-permute-start.1 = (bf16[2,192,512]{2,1,0:T(8,128)(2,1)S(1)}, bf16[2,192,512]{2,1,0:T(8,128)(2,1)}, u32[]{:S(2)}, u32[]{:S(2)}) collective-permute-start(bf16[2,192,512]{2,1,0:T(8,128)(2,1)S(1)} %get-tuple-element.72.refs_0_), channel_id=1, source_target_pairs={{0,16},{4,20},{8,24},{12,28},{16,0},{20,4},{24,8},{28,12},{1,17},{... | collective-permute-start | bytes 1179656 | tf_op jit(solution)/shard_map/ppermute | solution.py:1192
  20.1 29.9 %collective-permute-start.2 = (bf16[2,192,512]{2,1,0:T(8,128)(2,1)S(1)}, bf16[2,192,512]{2,1,0:T(8,128)(2,1)}, u32[]{:S(2)}, u32[]{:S(2)}) collective-permute-start(bf16[2,192,512]{2,1,0:T(8,128)(2,1)S(1)} %get-tuple-element.72.refs_0_), channel_id=1, source_target_pairs={{0,24},{4,28},{8,0},{12,4},{16,8},{20,12},{24,16},{28,20},{1,25},{... | collective-permute-start | bytes 1179656 | tf_op jit(solution)/shard_map/ppermute | solution.py:1192
  22.4 27.6 %collective-permute-start.3 = (bf16[2,192,512]{2,1,0:T(8,128)(2,1)S(1)}, bf16[2,192,512]{2,1,0:T(8,128)(2,1)}, u32[]{:S(2)}, u32[]{:S(2)}) collective-permute-start(bf16[2,192,512]{2,1,0:T(8,128)(2,1)S(1)} %get-tuple-element.72.refs_0_), channel_id=1, source_target_pairs={{0,4},{4,0},{8,12},{12,8},{16,20},{20,16},{24,28},{28,24},{1,5},{5... | collective-permute-start | bytes 1179656 | tf_op jit(solution)/shard_map/ppermute | solution.py:1193
  24.3 34.6 %copy-start.27 = (f32[9517]{0:T(1024)S(1)}, f32[9517]{0:T(1024)}, u32[]{:S(2)}) copy-start(f32[9517]{0:T(1024)} %param.47) | copy-start | bytes 114208
  24.3 39.3 %copy-start = (f32[512,1280]{1,0:T(8,128)S(1)}, f32[512,1280]{1,0:T(8,128)}, u32[]{:S(2)}) copy-start(f32[512,1280]{1,0:T(8,128)} %t0_ref.1) | copy-start | bytes 7864324
  50.7 14.2 %copy-start.29 = (s32[256,5]{0,1:T(8,128)S(1)}, s32[256,5]{0,1:T(8,128)}, u32[]{:S(2)}) copy-start(s32[256,5]{0,1:T(8,128)} %param.27) | copy-start | bytes 15364
  50.7 34.2 %all-to-all-start = ((bf16[32,128,128]{2,1,0:T(8,128)(2,1)}), bf16[32,128,128]{2,1,0:T(8,128)(2,1)}, u32[]{:S(2)}, u32[]{:S(2)}) async-start(bf16[32,128,128]{2,1,0:T(8,128)(2,1)} %bitcast.103), calls=%async_computation | async-start | bytes 2097152 | tf_op jit(solution)/shard_map/all_to_all | solution.py:1170
  58.9 6.8 %copy-start.30 = (s32[256,5]{0,1:T(8,128)S(1)}, s32[256,5]{0,1:T(8,128)}, u32[]{:S(2)}) copy-start(s32[256,5]{0,1:T(8,128)} %param.28) | copy-start | bytes 15364
  58.9 8.1 %copy-start.31 = (s32[8]{0:T(128)S(1)}, s32[8]{0:T(128)}, u32[]{:S(2)}) copy-start(s32[8]{0:T(128)} %param.26) | copy-start | bytes 100
  58.9 9.3 %copy-start.4 = (f32[1024,40]{0,1:T(8,128)S(1)}, f32[1024,40]{0,1:T(8,128)}, u32[]{:S(2)}) copy-start(f32[1024,40]{0,1:T(8,128)} %param.38) | copy-start | bytes 491524
  59.5 31.6 %collective-permute-start.4 = (bf16[2,192,512]{2,1,0:T(8,128)(2,1)}, bf16[2,192,512]{2,1,0:T(8,128)(2,1)}, u32[]{:S(2)}, u32[]{:S(2)}) collective-permute-start(bf16[2,192,512]{2,1,0:T(8,128)(2,1)} %copy-done.22), channel_id=1, source_target_pairs={{0,4},{4,0},{8,12},{12,8},{16,20},{20,16},{24,28},{28,24},{1,5},{5... | collective-permute-start | bytes 1179656 | tf_op jit(solution)/shard_map/ppermute | solution.py:1225
  61.1 30.1 %collective-permute-start.5 = (bf16[2,192,512]{2,1,0:T(8,128)(2,1)}, bf16[2,192,512]{2,1,0:T(8,128)(2,1)}, u32[]{:S(2)}, u32[]{:S(2)}) collective-permute-start(bf16[2,192,512]{2,1,0:T(8,128)(2,1)} %collective-permute-done.1.refs_2_), channel_id=1, source_target_pairs={{0,4},{4,0},{8,12},{12,8},{16,20},{20,16},{24,28},{28,24},{1,5},{5... | collective-permute-start | bytes 1179656 | tf_op jit(solution)/shard_map/ppermute | solution.py:1225
  61.6 36.6 %collective-permute-start.6 = (bf16[2,192,512]{2,1,0:T(8,128)(2,1)}, bf16[2,192,512]{2,1,0:T(8,128)(2,1)}, u32[]{:S(2)}, u32[]{:S(2)}) collective-permute-start(bf16[2,192,512]{2,1,0:T(8,128)(2,1)} %collective-permute-done.2.refs_3_), channel_id=1, source_target_pairs={{0,4},{4,0},{8,12},{12,8},{16,20},{20,16},{24,28},{28,24},{1,5},{5... | collective-permute-start | bytes 1179656 | tf_op jit(solution)/shard_map/ppermute | solution.py:1225
  178.7 10.6 %copy-start.7 = (bf16[128,1408]{1,0:T(8,128)(2,1)S(1)}, bf16[128,1408]{1,0:T(8,128)(2,1)}, u32[]{:S(2)}) copy-start(bf16[128,1408]{1,0:T(8,128)(2,1)} %get-tuple-element.81) | copy-start | bytes 1081348
  178.7 50.7 %copy-start.17 = (bf16[2,4,4,384,128]{4,3,2,1,0:T(8,128)(2,1)S(1)}, bf16[2,4,4,384,128]{4,3,2,1,0:T(8,128)(2,1)}, u32[]{:S(2)}) copy-start(bf16[2,4,4,384,128]{4,3,2,1,0:T(8,128)(2,1)} %get-tuple-element.85) | copy-start | bytes 9437188
  180.4 49.0 %collective-permute-start.7 = (bf16[4,4,384,128]{3,2,1,0:T(8,128)(2,1)S(1)}, bf16[4,4,384,128]{3,2,1,0:T(8,128)(2,1)S(1)}, u32[]{:S(2)}, u32[]{:S(2)}) collective-permute-start(bf16[4,4,384,128]{3,2,1,0:T(8,128)(2,1)S(1)} %slice_bitcast_fusion), channel_id=1, source_target_pairs={{0,4},{4,0},{8,12},{12,8},{16,20},{20,16},{24,28},{28,24},{1,5},{5... | collective-permute-start | bytes 4718600 | tf_op jit(solution)/shard_map/ppermute | solution.py:1366
  231.0 7.2 %copy-start.23 = (s32[32,1,256]{2,1,0:T(1,128)S(1)}, s32[32,1,256]{2,1,0:T(1,128)}, u32[]{:S(2)}) copy-start(s32[32,1,256]{2,1,0:T(1,128)} %add_maximum_fusion) | copy-start | bytes 98308
  231.0 38.3 %all-to-all-start.1 = ((bf16[16,384,128]{2,1,0:T(8,128)(2,1)}), bf16[16,384,128]{2,1,0:T(8,128)(2,1)}, u32[]{:S(2)}, u32[]{:S(2)}) async-start(bf16[16,384,128]{2,1,0:T(8,128)(2,1)} %bitcast.102), calls=%async_computation.1 | async-start | bytes 3145728 | tf_op jit(solution)/shard_map/all_to_all | solution.py:1165
  237.2 33.8 %copy-start.12 = (f32[2,8,512]{2,1,0:T(8,128)S(1)}, f32[2,8,512]{2,1,0:T(8,128)}, u32[]{:S(2)}) copy-start(f32[2,8,512]{2,1,0:T(8,128)} %get-tuple-element.83.inner_ref) | copy-start | bytes 98308
  269.2 19.1 %copy-start.26 = (bf16[16,1408]{1,0:T(8,128)(2,1)S(1)}, bf16[16,1408]{1,0:T(8,128)(2,1)}, u32[]{:S(2)}) copy-start(bf16[16,1408]{1,0:T(8,128)(2,1)} %convert_element_type.40) | copy-start | bytes 135172
  289.5 52.9 %all-to-all-start.2 = ((bf16[32,16,1408]{2,1,0:T(8,128)(2,1)}), bf16[32,16,1408]{2,1,0:T(8,128)(2,1)}, u32[]{:S(2)}, u32[]{:S(2)}) async-start(bf16[32,16,1408]{2,1,0:T(8,128)(2,1)} %broadcast_in_dim.7), calls=%async_computation.2 | async-start | bytes 2883584 | tf_op jit(solution)/shard_map/all_to_all | solution.py:1170
  297.0 41.4 %copy-start.19 = (f32[64,8,128]{2,1,0:T(8,128)S(1)}, f32[64,8,128]{2,1,0:T(8,128)}, u32[]{:S(2)}) copy-start(f32[64,8,128]{2,1,0:T(8,128)} %param.35) | copy-start | bytes 786436
  297.0 41.4 %copy-start.24 = (f32[64,8,128]{2,1,0:T(8,128)S(1)}, f32[64,8,128]{2,1,0:T(8,128)}, u32[]{:S(2)}) copy-start(f32[64,8,128]{2,1,0:T(8,128)} %param.36) | copy-start | bytes 786436
  297.0 41.3 %copy-start.25 = (f32[64,8,128]{2,1,0:T(8,128)S(1)}, f32[64,8,128]{2,1,0:T(8,128)}, u32[]{:S(2)}) copy-start(f32[64,8,128]{2,1,0:T(8,128)} %param.37) | copy-start | bytes 786436
  297.1 43.2 %copy-start.18 = (f32[128,8,128]{2,1,0:T(8,128)S(1)}, f32[128,8,128]{2,1,0:T(8,128)}, u32[]{:S(2)}) copy-start(f32[128,8,128]{2,1,0:T(8,128)} %param.32) | copy-start | bytes 1572868
  297.1 43.2 %copy-start.20 = (f32[128,8,128]{2,1,0:T(8,128)S(1)}, f32[128,8,128]{2,1,0:T(8,128)}, u32[]{:S(2)}) copy-start(f32[128,8,128]{2,1,0:T(8,128)} %param.33) | copy-start | bytes 1572868
  297.1 43.2 %copy-start.21 = (f32[128,8,128]{2,1,0:T(8,128)S(1)}, f32[128,8,128]{2,1,0:T(8,128)}, u32[]{:S(2)}) copy-start(f32[128,8,128]{2,1,0:T(8,128)} %param.34) | copy-start | bytes 1572868
  338.4 4.1 %copy-start.5 = (f32[1024,40]{0,1:T(8,128)S(1)}, f32[1024,40]{0,1:T(8,128)}, u32[]{:S(2)}) copy-start(f32[1024,40]{0,1:T(8,128)} %param.38) | copy-start | bytes 491524
  338.4 4.1 %copy-start.9 = (f32[1024,40]{0,1:T(8,128)S(1)}, f32[1024,40]{0,1:T(8,128)}, u32[]{:S(2)}) copy-start(f32[1024,40]{0,1:T(8,128)} %param.39) | copy-start | bytes 491524
  342.5 8.2 %copy-start.28 = (f32[9517]{0:T(1024)S(1)}, f32[9517]{0:T(1024)}, u32[]{:S(2)}) copy-start(f32[9517]{0:T(1024)} %param.47) | copy-start | bytes 114208
  (11 other events, 24.4 us)

commit v6 on v5

--- a/solution.py
+++ b/solution.py
@@ -49,7 +49,7 @@
     )
 
 
-def route_kernel(row_bits, ids_ref, out_ref, place_ref, slot_ref, from_ref):
+def route(row_bits, ids_ref, out_ref, place_ref, slot_ref, from_ref):
     devices, _, capacity = out_ref.shape
     tables, samples = ids_ref.shape
     rows_dev = 1 << row_bits
@@ -103,15 +103,19 @@
     left = left_lanes((1, lanes))
     part = 512
 
+    total = tables // 2 * rows_dev
+
     def turn_step(step, _):
-        table = lax.div(step, rows_dev // part)
+        pair = lax.div(step, rows_dev // part)
         first = pl.multiple_of(lax.rem(step, rows_dev // part) * part, part)
-        columns = table_ref[table, :, pl.ds(first, part)]
-        there = pl.ds(pl.multiple_of(step * part, part), part)
-        turned_ref[there, :] = jnp.concatenate([columns, columns], axis=0).T
-        return 0
-
-    lax.fori_loop(0, tables * (rows_dev // part), turn_step, 0)
+        columns = table_ref[pl.ds(2 * pair, 2), :, pl.ds(first, part)]
+        rows = columns.reshape(2 * width, part).T
+        at = pl.multiple_of(step * part, part)
+        turned_ref[pl.ds(at, part), :] = rows
+        turned_ref[pl.ds(total + at, part), :] = pltpu.roll(rows, width, 1)
+        return 0
+
+    lax.fori_loop(0, total // part, turn_step, 0)
 
     def block_step(block, _):
         source = block * groups + group
@@ -119,8 +123,8 @@
 
         def step(outer, _):
             got = []
-            for inner in range(8):
-                at = outer * 8 + inner
+            for inner in range(16):
+                at = outer * 16 + inner
                 even = turned_ref[pl.ds(at_ref[base + 2 * at], 1), :]
                 odd = turned_ref[pl.ds(at_ref[base + 2 * at + 1], 1), :]
                 got.append((at, jnp.where(left, even, odd)))
@@ -128,7 +132,7 @@
                 rows_ref[pl.ds(at, 1), :] = row
             return 0
 
-        lax.fori_loop(0, (counts_ref[source] + 15) // 16, step, 0)
+        lax.fori_loop(0, (counts_ref[source] + 31) // 32, step, 0)
         out_ref[block, 0] = rows_ref[...].astype(LOW)
         return 0
 
@@ -237,7 +241,7 @@
 
 
 def add_kernel(
-    groups, at_ref, part_at_ref, counts_ref, rows_ref, out_ref, square_ref, parts_ref, sems, *sums
+    groups, at_ref, part_at_ref, counts_ref, rows_ref, out_ref, square_ref, parts_ref, low_ref, sems, *sums
 ):
     count, lanes = rows_ref.shape
     sources = counts_ref.shape[0]
@@ -280,22 +284,26 @@
         return 0
 
     lax.fori_loop(0, sources // groups, block_step, 0)
-    copies = [
-        pltpu.make_async_copy(
-            sums[group], out_ref.at[pl.ds(group * table_rows, table_rows)], sems.at[group]
-        )
-        for group in range(groups)
-    ]
-    for copy in copies:
-        copy.start()
-
-    def square(at, total):
-        for table in sums:
-            rows = table[pl.ds(pl.multiple_of(at * 64, 64), 64), :]
-            total = total + jnp.sum((rows * rows).reshape(8, 8, lanes), axis=0)
-        return total
-
-    square_ref[...] = lax.fori_loop(0, table_rows // 64, square, jnp.zeros((8, lanes), F32))
+    copies = []
+    squares = jnp.zeros((8, lanes), F32)
+    for group in range(groups):
+
+        def square(at, total):
+            here = pl.ds(pl.multiple_of(at * 64, 64), 64)
+            rows = sums[group][here, :]
+            low_ref[group, here, :] = rows.astype(LOW)
+            return total + jnp.sum((rows * rows).reshape(8, 8, lanes), axis=0)
+
+        squares = lax.fori_loop(0, table_rows // 64, square, squares)
+        copies.append(
+            pltpu.make_async_copy(
+                low_ref.at[group],
+                out_ref.at[pl.ds(group * table_rows, table_rows)],
+                sems.at[group],
+            )
+        )
+        copies[-1].start()
+    square_ref[...] = squares
     for copy in copies:
         copy.wait()
 
@@ -335,7 +343,7 @@
     return me
 
 
-def greet_all(devices, peers, me):
+def greet_all(devices, peers, me, between=None):
     barrier = pltpu.get_barrier_semaphore()
 
     def greet(step, _):
@@ -346,6 +354,8 @@
         return 0
 
     lax.fori_loop(1, devices, greet, 0)
+    if between is not None:
+        between()
     pl.semaphore_wait(barrier, devices - 1)
 
 
@@ -353,7 +363,23 @@
     return {"dp": lax.div(device, peers), "mp": lax.rem(device, peers)}
 
 
-def ask_kernel(codes_ref, shard_ref, out_ref, full_ref, c_out, c_in, w_out, w_in):
+def ask_kernel(
+    row_bits,
+    ids_ref,
+    first_ref,
+    second_ref,
+    out_ref,
+    full_ref,
+    place_ref,
+    slot_ref,
+    from_ref,
+    codes_ref,
+    shard_ref,
+    c_out,
+    c_in,
+    w_out,
+    w_in,
+):
     devices = codes_ref.shape[0]
     here, _, full = full_ref.shape
     width = shard_ref.shape[2]
@@ -361,9 +387,17 @@
     mp = lax.axis_index("mp")
     me = lax.axis_index("dp") * peers + mp
     columns = pl.ds(pl.multiple_of(mp * width, width), width)
-    full_ref[:, :, columns] = shard_ref[pl.ds(mp * here, here)]
-    out_ref[me] = codes_ref[me]
-    greet_all(devices, peers, me)
+    in_rows = first_ref.shape[0]
+
+    def prepare():
+        route(row_bits, ids_ref, codes_ref, place_ref, slot_ref, from_ref)
+        for e in range(peers * here):
+            shard_ref[e, :in_rows, :] = first_ref[:, e, :].astype(LOW)
+            shard_ref[e, in_rows:, :] = second_ref[:, e, :].astype(LOW)
+        full_ref[:, :, columns] = shard_ref[pl.ds(mp * here, here)]
+        out_ref[me] = codes_ref[me]
+
+    greet_all(devices, peers, me, prepare)
 
     def c_copy(step):
         target = lax.rem(me + step, devices)
@@ -440,6 +474,7 @@
     y_ref,
     gates_ref,
     mixb_ref,
+    dz_ref,
     dmix_ref,
     dg_ref,
     dy_send,
@@ -470,8 +505,7 @@
 ):
     peers, samples, width = blocks_ref.shape
     here = hid_ref.shape[0]
-    out_width = y_ref.shape[3]
-    own = y_ref.shape[2]
+    own, out_width = y_ref.shape[2], y_ref.shape[3]
     experts = peers * here
     tasks, tower_hid = heads_ref.shape
     shards, hid = w_ref.shape[0], w_ref.shape[3]
@@ -506,8 +540,19 @@
     def rows_of(chunk):
         return pl.ds(pl.multiple_of(chunk * own, own), own)
 
-    def ahead_chunk(turn):
-        return lax.rem(2 * chip + 2 + turn, peers)
+    half = own // 2
+
+    def part_rows(device, part):
+        at = device * own + part * half
+        return pl.ds(pl.multiple_of(at, half), half)
+
+    def half_rows(part):
+        return pl.ds(pl.multiple_of(part * half, half), half)
+
+    def ahead_rows(pair_of, turn):
+        first = lax.rem(2 * pair_of + 2 + 2 * lax.div(turn, 2), peers)
+        part = lax.rem(turn, 2)
+        return first, part, [part_rows(first + at, part) for at in range(2)]
 
     def back_chunk(turn):
         return lax.rem(2 * chip + turn, peers)
@@ -518,33 +563,54 @@
         )
 
     def x_far(turn):
-        rows = rows_of(back_chunk(turn))
+        rows = ahead_rows(1 - chip, turn)[2]
+        return [
+            remote(
+                x_ref.at[rows[at]],
+                blocks_ref.at[me, rows[at]],
+                x_out.at[0, turn, at],
+                x_in.at[0, turn, at],
+                far,
+            )
+            for at in range(2)
+        ]
+
+    def x_near(turn):
+        rows = ahead_rows(chip, turn)[2]
+        return [
+            remote(
+                x_ref.at[rows[at]],
+                blocks_ref.at[me, rows[at]],
+                x_out.at[1, turn, at],
+                x_in.at[1, turn, at],
+                near,
+            )
+            for at in range(2)
+        ]
+
+    def x_hand(turn):
+        rows = ahead_rows(chip, turn)[2]
+        blocks = [blocks_ref.at[far, rows[at]] for at in range(2)]
+        return [
+            remote(blocks[at], blocks[at], x_out.at[2, turn, at], x_in.at[2, turn, at], near)
+            for at in range(2)
+        ]
+
+    def y_copy(turn, at, part, relation, device):
         return remote(
-            x_ref.at[rows], blocks_ref.at[me, rows], x_out.at[0, turn], x_in.at[0, turn], far
-        )
-
-    def x_near(turn):
-        rows = rows_of(ahead_chunk(turn))
+            y_send.at[turn, at],
+            y_ref.at[me, :, half_rows(part), :],
+            y_out.at[relation, part],
+            y_in.at[relation, part],
+            device,
+        )
+
+    def d_copy(part, relation, device):
         return remote(
-            x_ref.at[rows], blocks_ref.at[me, rows], x_out.at[1, turn], x_in.at[1, turn], near
-        )
-
-    def x_hand(turn):
-        rows = rows_of(ahead_chunk(turn))
-        block = blocks_ref.at[far, rows]
-        return remote(block, block, x_out.at[2, turn], x_in.at[2, turn], near)
-
-    def y_copy(turn, relation, device):
-        return remote(
-            y_send.at[turn], y_ref.at[me], y_out.at[relation], y_in.at[relation], device
-        )
-
-    def d_copy(relation, device):
-        return remote(
-            dy_send.at[pl.ds(device * here, here)],
-            dy_ref.at[:, rows_of(me), :],
-            d_out.at[relation],
-            d_in.at[relation],
+            dy_send.at[pl.ds(device * here, here), half_rows(part), :],
+            dy_ref.at[:, part_rows(me, part), :],
+            d_out.at[relation, part],
+            d_in.at[relation, part],
             device,
         )
 
@@ -567,28 +633,37 @@
         )
 
     for turn in range(peers):
-        x_far(turn).start()
-        x_near(turn).start()
+        for copy in x_far(turn) + x_near(turn):
+            copy.start()
     blocks_ref[me] = x_ref[...]
     limit = count_ref[0]
     for copy in w_copies:
         copy.wait()
 
-    x_far(0).wait_recv()
-    x_hand(0).start()
+    def pass_on(turn):
+        for copy in x_far(turn):
+            copy.wait_recv()
+        for copy in x_hand(turn):
+            copy.start()
+
+    pass_on(0)
 
     def expert_step(turn, _):
-        x_near(turn).wait_recv()
-        x_hand(turn).wait_recv()
+        for copy in x_near(turn) + x_hand(turn):
+            copy.wait_recv()
 
         @pl.when(turn < peers - 1)
         def _():
-            x_far(turn + 1).wait_recv()
-            x_hand(turn + 1).start()
-
-        chunk = ahead_chunk(turn)
-        rows = rows_of(chunk)
-        x = jnp.concatenate([blocks_ref[block, rows] for block in range(peers)], axis=1)
+            pass_on(turn + 1)
+
+        first, part, rows = ahead_rows(chip, turn)
+        x = jnp.concatenate(
+            [
+                jnp.concatenate([blocks_ref[block, rows[at]] for block in range(peers)], axis=1)
+                for at in range(2)
+            ],
+            axis=0,
+        )
         for e in range(here):
             w_in = w_ref[:, e, :in_rows, :].reshape(peers * width, hid)
             act_ref[...] = dot(x, w_in) + b1_ref[e]
@@ -596,26 +671,33 @@
             def gelu_step(tile, _):
                 at = pl.multiple_of(tile * 32, 32)
                 value, slope = gelu_parts(act_ref[pl.ds(at, 32), :])
-                there = pl.ds(pl.multiple_of(chunk * own + at, 32), 32)
+                place = lax.div(at, half)
+                there = (first + place) * own + part * half + at - place * half
+                there = pl.ds(pl.multiple_of(there, 32), 32)
                 hid_ref[e, there, :] = value.astype(LOW)
                 slope_ref[e, there, :] = slope
                 return 0
 
             lax.fori_loop(0, own // 32, gelu_step, 0)
             w_out = w_ref[:, e, in_rows:, :].reshape(out_width, hid)
-            y_send[turn, e] = (dot(hid_ref[e, rows, :], w_out, NT) + b2_ref[e]).astype(LOW)
-
-        @pl.when(turn < 2)
-        def _():
-            y_copy(turn, 1 + lax.rem(side + turn, 2), chunk).start()
-
-        @pl.when(jnp.logical_and(turn >= 2, chunk != me))
-        def _():
-            y_copy(turn, 0, chunk).start()
-
-        @pl.when(chunk == me)
-        def _():
-            y_ref[me] = y_send[turn]
+            hidden = jnp.concatenate([hid_ref[e, rows[at], :] for at in range(2)], axis=0)
+            y = (dot(hidden, w_out, NT) + b2_ref[e]).astype(LOW)
+            for at in range(2):
+                y_send[turn, at, e] = y[at * half : (at + 1) * half]
+        for at in range(2):
+            device = first + at
+
+            @pl.when(turn < 2)
+            def _():
+                y_copy(turn, at, part, 1 + lax.rem(side + at, 2), device).start()
+
+            @pl.when(jnp.logical_and(turn >= 2, device != me))
+            def _():
+                y_copy(turn, at, part, 0, device).start()
+
+            @pl.when(device == me)
+            def _():
+                y_ref[me, :, half_rows(part), :] = y_send[turn, at]
 
         return 0
 
@@ -639,9 +721,6 @@
 
     x_square = lax.fori_loop(0, samples // 64, square_step, jnp.zeros((8, width), F32))
     stats_ref[experts + tasks, :, :width] = x_square
-    for relation, device in enumerate((near, far, across)):
-        y_copy(0, relation, device).wait_recv()
-
     tile_rows = 16
 
     def tile_of(tile):
@@ -666,43 +745,39 @@
             mixb_ref[k, rows, :] = mixed[k].astype(LOW)
         return 0
 
-    lax.fori_loop(0, own // tile_rows, mix_step, 0)
-
     pack_ref[...] = jnp.zeros_like(pack_ref)
     blocks_x = peers * width // 128
     heads_at = blocks_x * tasks * experts
     tower_at = heads_at + tasks * tower_hid // 128
     outer_at = tower_at + tasks * tower_hid // 128
     rest_at = outer_at + experts * out_width // 128
-    loss = jnp.zeros((1, 1), F32)
-    weight_sum = jnp.zeros((1, 1), F32)
-    row_id = lax.broadcasted_iota(I32, (own, 1), 0) + me * own
-    for k in range(tasks):
+    def tower_step(k, part):
+        rows = half_rows(part)
         cols = slice(k * tower_hid, (k + 1) * tower_hid)
-        z, slope = gelu_parts(dot(mixb_ref[k], w3_ref[:, cols]) + tb1_ref[k : k + 1, :])
+        z, slope = gelu_parts(dot(mixb_ref[k, rows, :], w3_ref[:, cols]) + tb1_ref[k : k + 1, :])
         head = heads_ref[k : k + 1, :]
         logit = jnp.sum(z * head, axis=1, keepdims=True) + tb2_ref[0, k]
         small = jnp.exp(-jnp.abs(logit))
-        label = labels_ref[:, k : k + 1].astype(F32)
-        weight = jnp.where(row_id < limit, mask_ref[:, k : k + 1].astype(F32), 0.0)
+        label = labels_ref[rows, k : k + 1].astype(F32)
+        row_id = lax.broadcasted_iota(I32, (half, 1), 0) + (me * own + part * half)
+        weight = jnp.where(row_id < limit, mask_ref[rows, k : k + 1].astype(F32), 0.0)
         soft = jnp.maximum(logit, 0.0) + jnp.log1p(small)
-        loss += jnp.sum(weight * (soft - label * logit), axis=0, keepdims=True)
-        weight_sum += jnp.sum(weight, axis=0, keepdims=True)
+        loss = jnp.sum(weight * (soft - label * logit), axis=0, keepdims=True)
+        stats_ref[experts + tasks + 1, :1, :1] += loss
+        stats_ref[experts + tasks + 1, :1, 1:2] += jnp.sum(weight, axis=0, keepdims=True)
         chance = jnp.where(logit >= 0.0, 1.0, small) / (1.0 + small)
         dl = weight * (chance - label)
         g_head = jnp.sum(dl * z, axis=0, keepdims=True)
         dz = (dl * head * slope).astype(LOW)
         g_bias = jnp.sum(dz.astype(F32), axis=0, keepdims=True)
-        for part in range(tower_hid // 128):
-            lane = slice(part * 128, (part + 1) * 128)
-            at = k * (tower_hid // 128) + part
-            pack_ref[heads_at + at : heads_at + at + 1, :] = g_head[:, lane]
-            pack_ref[tower_at + at : tower_at + at + 1, :] = g_bias[:, lane]
-        pack_ref[rest_at + 1 : rest_at + 2, k : k + 1] = jnp.sum(dl, axis=0, keepdims=True)
-        dmix_ref[k] = dot(dz, w3_ref[:, cols], NT)
-        small_ref[:, cols] = dot(mixb_ref[k], dz, TN).astype(LOW)
-    stats_ref[experts + tasks + 1, :1, :1] = loss
-    stats_ref[experts + tasks + 1, :1, 1:2] = weight_sum
+        for piece in range(tower_hid // 128):
+            lane = slice(piece * 128, (piece + 1) * 128)
+            at = k * (tower_hid // 128) + piece
+            pack_ref[heads_at + at : heads_at + at + 1, :] += g_head[:, lane]
+            pack_ref[tower_at + at : tower_at + at + 1, :] += g_bias[:, lane]
+        pack_ref[rest_at + 1 : rest_at + 2, k : k + 1] += jnp.sum(dl, axis=0, keepdims=True)
+        dz_ref[k, rows, :] = dz
+        dmix_ref[k, rows, :] = dot(dz, w3_ref[:, cols], NT)
 
     def dy_step(tile, _):
         at, rows = tile_of(tile)
@@ -716,11 +791,24 @@
             dy_send[e, rows, :] = total.astype(LOW)
         return 0
 
-    lax.fori_loop(0, own // tile_rows, dy_step, 0)
-    d_copy(1, far).start()
-    d_copy(2, across).start()
-    d_copy(0, near).start()
+    def half_step(part, _):
+        for relation, device in enumerate((near, far, across)):
+            y_copy(0, 0, part, relation, device).wait_recv()
+        tiles = half // tile_rows
+        lax.fori_loop(part * tiles, (part + 1) * tiles, mix_step, 0)
+        for k in range(tasks):
+            tower_step(k, part)
+        lax.fori_loop(part * tiles, (part + 1) * tiles, dy_step, 0)
+        d_copy(part, 1, far).start()
+        d_copy(part, 2, across).start()
+        d_copy(part, 0, near).start()
+        return 0
+
+    lax.fori_loop(0, 2, half_step, 0)
     dy_ref[:, own_rows, :] = dy_send[pl.ds(me * here, here)]
+    for k in range(tasks):
+        cols = slice(k * tower_hid, (k + 1) * tower_hid)
+        small_ref[:, cols] = dot(mixb_ref[k], dz_ref[k], TN).astype(LOW)
     ones = jnp.ones((8, own), LOW)
     for e in range(experts):
         g_outer = dot(ones, dy_send[e])
@@ -808,11 +896,13 @@
 
         @pl.when(jnp.logical_and(turn < 2, chunk != me))
         def _():
-            d_copy(0, chunk).wait_recv()
+            for part in range(2):
+                d_copy(part, 0, chunk).wait_recv()
 
         @pl.when(turn >= 2)
         def _():
-            d_copy(1 + lax.rem(side + turn, 2), chunk).wait_recv()
+            for part in range(2):
+                d_copy(part, 1 + lax.rem(side + turn, 2), chunk).wait_recv()
 
         total = gate_ref[...] * jnp.where(chunk == me, 1.0, 0.0)
         for e in range(here):
@@ -891,12 +981,12 @@
     dx_ref[...] = dx_send[me].astype(F32) + dx_near[...].astype(F32) + dx_far[...].astype(F32)
     for turn in range(peers):
         g_help(turn).wait_send()
-        x_far(turn).wait_send()
-        x_near(turn).wait_send()
-        x_hand(turn).wait_send()
+        for copy in x_far(turn) + x_near(turn) + x_hand(turn):
+            copy.wait_send()
     for relation, device in enumerate((near, far, across)):
-        y_copy(0, relation, device).wait_send()
-        d_copy(relation, device).wait_send()
+        for part in range(2):
+            y_copy(0, 0, part, relation, device).wait_send()
+            d_copy(part, relation, device).wait_send()
 
 
 def total_kernel(
@@ -1003,7 +1093,7 @@
 
 def table_kernel(factor_ref, weight_ref, first_ref, second_ref, grad_ref, *outs):
     pair, width, rows = weight_ref.shape
-    gradient = grad_ref[0].T.reshape(pair, width, rows) * factor_ref[:1, :1].reshape(1, 1, 1)
+    gradient = grad_ref[0].astype(F32).T.reshape(pair, width, rows) * factor_ref[:1, :1].reshape(1, 1, 1)
     results = adamw(weight_ref[...], first_ref[...], second_ref[...], gradient, rate_table)
     for out, result in zip(outs, results):
         out[...] = result
@@ -1140,52 +1230,48 @@
     width_out = out_rows * dp_count
     tower_hid = towers.shape[1] // TASKS
 
-    outgoing, place, slot, source = pl.pallas_call(
-        functools.partial(route_kernel, row_bits),
+    in_out_rows = in_rows + out_rows
+    hid_here = hid // mp_count
+    sides = [
+        [d * mp_count + m for d in range(x, dp_count, 2) for m in range(mp_count)] for x in range(2)
+    ]
+    partners = [(d, d ^ 1) for d in range(dp_count)]
+
+    def exchange_side(parts):
+        return lax.all_to_all(
+            parts, AXES, split_axis=0, concat_axis=0, axis_index_groups=sides, tiled=True
+        )
+
+    def exchange_all(parts):
+        return lax.all_to_all(parts, AXES, split_axis=0, concat_axis=0, tiled=True)
+
+    def sems(*shape):
+        return pltpu.SemaphoreType.DMA(shape)
+
+    codes, shard, place, slot, source = pl.pallas_call(
+        functools.partial(ask_kernel, row_bits),
         out_shape=(
             jax.ShapeDtypeStruct((devices, 1, capacity), I32),
+            jax.ShapeDtypeStruct((experts_here, in_out_rows, hid), LOW),
             jax.ShapeDtypeStruct((tables_here, samples), I32),
             jax.ShapeDtypeStruct((tables_here, samples), I32),
             jax.ShapeDtypeStruct((tables_here, samples), I32),
         ),
-        in_specs=[VMEM],
-        out_specs=(VMEM,) * 4,
-        compiler_params=params(32),
-        name="route",
-    )(row_ids.T)
-    in_out_rows = in_rows + out_rows
-    hid_here = hid // mp_count
-    shard = jnp.concatenate([expert_in, expert_out], axis=0).astype(LOW).transpose(1, 0, 2)
-    sides = [
-        [d * mp_count + m for d in range(x, dp_count, 2) for m in range(mp_count)] for x in range(2)
-    ]
-    partners = [(d, d ^ 1) for d in range(dp_count)]
-
-    def exchange_side(parts):
-        return lax.all_to_all(
-            parts, AXES, split_axis=0, concat_axis=0, axis_index_groups=sides, tiled=True
-        )
-
-    def exchange_all(parts):
-        return lax.all_to_all(parts, AXES, split_axis=0, concat_axis=0, tiled=True)
-
-    def sems(*shape):
-        return pltpu.SemaphoreType.DMA(shape)
-
-    codes, shard = pl.pallas_call(
-        ask_kernel,
-        out_shape=(
-            jax.ShapeDtypeStruct((devices, 1, capacity), I32),
-            jax.ShapeDtypeStruct((experts_here, in_out_rows, hid), LOW),
-        ),
-        in_specs=[VMEM, VMEM],
-        out_specs=(VMEM, VMEM),
-        scratch_shapes=[sems(devices), sems(devices), sems(mp_count), sems(mp_count)],
+        in_specs=[VMEM] * 3,
+        out_specs=(VMEM,) * 5,
+        scratch_shapes=[
+            pltpu.VMEM((devices, 1, capacity), I32),
+            pltpu.VMEM((EXPERTS, in_out_rows, hid_here), LOW),
+            sems(devices),
+            sems(devices),
+            sems(mp_count),
+            sems(mp_count),
+        ],
         compiler_params=pltpu.CompilerParams(
-            vmem_limit_bytes=16 * MIB, collective_id=2, has_side_effects=True
+            vmem_limit_bytes=32 * MIB, collective_id=2, has_side_effects=True
         ),
         name="ask",
-    )(outgoing, shard)
+    )(row_ids.T, expert_in, expert_out)
     w_far = []
     for ahead in range(1, dp_count // 2):
         steps = [(d, (d + 2 * ahead) % dp_count) for d in range(dp_count)]
@@ -1198,6 +1284,7 @@
     table_at = found_at >> row_bits
     sum_at = (table_at >> 1) * rows_dev + (found_at & (rows_dev - 1))
     number = jnp.arange(capacity, dtype=I32)[None, :]
+    turned_at = ((table_at ^ number) & 1) * group_rows + sum_at
     part_at = ((number & 1) * 2 + (table_at & 1)) * slots + (number >> 1)
     part_at = part_at + jnp.arange(devices, dtype=I32)[:, None] * height
     part_at = jnp.where(plain > 0, part_at, 4 * slots)
@@ -1219,7 +1306,7 @@
         ],
         compiler_params=params(60),
         name="find",
-    )(found_at.reshape(-1), asked, table_view)
+    )(turned_at.reshape(-1), asked, table_view)
     w_far, w_near, found = lax.optimization_barrier((w_far, w_near, found))
     w_mine = [shard] + w_far
     w_theirs = [w_near] + [lax.ppermute(line, "dp", partners) for line in w_far]
@@ -1282,10 +1369,11 @@
             scratch((experts_here, samples, hid), LOW),
             scratch((experts_here, samples, hid)),
             scratch((experts_here, samples, width_out), LOW),
-            scratch((mp_count, experts_here, own, width_out), LOW),
+            scratch((mp_count, 2, experts_here, own // 2, width_out), LOW),
             scratch((mp_count, experts_here, own, width_out), LOW),
             scratch((own, all_gates)),
             scratch((TASKS, own, width_out), LOW),
+            scratch((TASKS, own, tower_hid), LOW),
             scratch((TASKS, own, width_out)),
             scratch((own, all_gates)),
             scratch((EXPERTS, own, width_out), LOW),
@@ -1302,12 +1390,12 @@
             scratch((2 * pack_shape[0], pack_shape[1]), LOW),
             scratch(pack_shape, LOW),
             scratch(pack_shape, LOW),
-            sems(3, mp_count),
-            sems(3, mp_count),
-            sems(3),
-            sems(3),
-            sems(3),
-            sems(3),
+            sems(3, mp_count, 2),
+            sems(3, mp_count, 2),
+            sems(3, 2),
+            sems(3, 2),
+            sems(3, 2),
+            sems(3, 2),
             sems(3, mp_count),
             sems(3, mp_count),
             sems(2),
@@ -1378,13 +1466,14 @@
     table_grad, table_sq = pl.pallas_call(
         functools.partial(add_kernel, mp_count),
         out_shape=(
-            jax.ShapeDtypeStruct((pairs * rows_dev, lanes), F32),
+            jax.ShapeDtypeStruct((pairs * rows_dev, lanes), LOW),
             jax.ShapeDtypeStruct((8, lanes), F32),
         ),
         in_specs=[SMEM, SMEM, SMEM, VMEM],
-        out_specs=(VMEM, VMEM),
+        out_specs=(pl.BlockSpec(memory_space=pl.ANY), VMEM),
         scratch_shapes=[
             pltpu.VMEM((4 * slots + 8, lanes), F32),
+            pltpu.VMEM((mp_count, group_rows, lanes), LOW),
             pltpu.SemaphoreType.DMA((mp_count,)),
         ]
         + [pltpu.VMEM((group_rows, lanes), F32)] * mp_count,
@@ -1438,7 +1527,7 @@
             pl.BlockSpec((1, rows_dev, lanes), lambda p: (p, 0, 0)),
         ],
         out_specs=(table_spec,) * 3,
-        compiler_params=params(40),
+        compiler_params=params(58),
         name="tables",
     )(
         result,

time: 354 us -> 349 us (0.986)
  Pallas kernels: 259 us -> 251 us
    pallas_call x2 -> x1, Pallas kernels: 14.9 us -> 12.8 us  [body(): pl.pallas_call(functools.partial(ask_kernel, row_bits), out_shape=(jax.Sh...]
    unnamed x76 -> x78, local copies, waits for them, and re-layouts: 8.83 us -> 7.98 us
  transfers between devices with their start and end apart: 11 -> 11, of which waited for: 3 -> 4; matrix products, arithmetic and copies ran while one was open for 5% -> 5% of each run, Pallas kernels for 38% -> 37%
where the time goes in v6:
time: 349 us; the launch traced here: 348 us
  Pallas kernels  251 us (72%)
  starting transfers between devices  32.1 us (9%)
  waiting for transfers between devices  31 us (9%)
  local copies, waits for them, and re-layouts  16.2 us (5%)
  other arithmetic  16 us (5%)
    pallas_call x1, Pallas kernels, body(): pl.pallas_call(functools.partial(dense_kernel, dp_count // 2), out_shape=...  78.6 us
    pallas_call x1, Pallas kernels, body(): pl.pallas_call(table_kernel, grid=(pairs,), out_shape=(jax.ShapeDtypeStru...  39 us
    pallas_call x1, Pallas kernels, body(): pl.pallas_call(swap_kernel, out_shape=(jax.ShapeDtypeStruct((devices, hei...  38.2 us
    pallas_call x1, Pallas kernels, body(): pl.pallas_call(functools.partial(add_kernel, mp_count), out_shape=(jax.Sh...  23.5 us
    pallas_call x1, Pallas kernels, body(): pl.pallas_call(functools.partial(find_kernel, mp_count), grid=(mp_count,)...  22.6 us
    all_to_all x2, starting transfers between devices, exchange_all(): return lax.all_to_all(parts, AXES, split_axis=0, concat_axis=0, tiled=True)  16.9 us
    all_to_all x2, waiting for transfers between devices, exchange_all(): return lax.all_to_all(parts, AXES, split_axis=0, concat_axis=0, tiled=True)  16 us
    pallas_call x1, Pallas kernels, body(): pl.pallas_call(functools.partial(total_kernel, features, width_out), out_...  15.5 us
  transfers between devices with their start and end apart: 11, of which 4 were waited for; matrix products, arithmetic and copies ran while one was open for 5% of the time, Pallas kernels for 37%

profile of v6, /device:TPU:0, one launch (start us, length us, event | category | flops | bytes accessed | tf_op | source)
XLA Modules:
  0.0 347.5 jit_solution(6307599302722896284)
XLA Ops:
  0.7 1.0 copy-done.2
  3.4 12.8 %ask.1 = (s32[32,1,256]{2,1,0:T(1,128)S(1)}, bf16[2,192,512]{2,1,0:T(8,128)(2,1)S(1)}, s32[4,1024]{1,0:T(4,128)S(1)}, s32[4,1024]{1,0:T(4,128)S(1)}, s32[4,1024]{1,0:T(4,128)S(1)}) custom-call(s32[4,1024]{1,0:T(4,128)S(1)} %bitcast.94, f32[128,8,128]{2,1,0:T(8,128)S(1)} %copy-done.2, f32[64,8,128]{2,1,0:T(8,128)S(1)} %copy-done.4), custom_call_target="tpu_custom_call" | custom-call | tf_op jit(solution)/shard_map/ask/pallas_call | solution.py:1251
  16.8 1.9 collective-permute-start.1
  18.7 1.4 collective-permute-start.2
  20.1 1.4 collective-permute-start.3
  23.2 22.6 %find.1 = bf16[8,4,128,128]{3,2,1,0:T(8,128)(2,1)} custom-call(s32[8192]{0:T(1024)} %get-tuple-element.122.at_ref, s32[32]{0:T(128)} %fusion.4.counts_ref, f32[16,64,4096]{2,1,0:T(8,128)} %bitcast.99), custom_call_target="tpu_custom_call" | custom-call | tf_op jit(solution)/shard_map/find/pallas_call | solution.py:1293
  46.6 10.6 %all-to-all-start = ((bf16[32,128,128]{2,1,0:T(8,128)(2,1)}), bf16[32,128,128]{2,1,0:T(8,128)(2,1)}, u32[]{:S(2)}, u32[]{:S(2)}) async-start(bf16[32,128,128]{2,1,0:T(8,128)(2,1)} %bitcast.105), calls=%async_computation | async-start | bytes 2097152 | tf_op jit(solution)/shard_map/all_to_all | solution.py:1246
  57.8 1.5 collective-permute-start.4
  59.9 1.5 collective-permute-start.6
  62.0 1.2 convert_element_type.37.refs_14_
  67.2 16.0 %all-to-all-done = bf16[32,128,128]{2,1,0:T(8,128)(2,1)} async-done(((bf16[32,128,128]{2,1,0:T(8,128)(2,1)}), bf16[32,128,128]{2,1,0:T(8,128)(2,1)}, u32[]{:S(2)}, u32[]{:S(2)}) %all-to-all-start) | async-done | bytes 1048608 | tf_op jit(solution)/shard_map/all_to_all | solution.py:1246
  83.2 5.4 %place.1.refs_9_ = bf16[1024,256]{1,0:T(8,128)(2,1)S(1)} custom-call(s32[4096]{0:T(1024)S(1)} %bitcast.93, bf16[4096,128]{1,0:T(8,128)(2,1)} %bitcast.5.rows_ref), custom_call_target="tpu_custom_call" | custom-call | tf_op jit(solution)/shard_map/place/pallas_call | solution.py:1314
  89.5 6.9 %collective-permute-done.6.refs_7_ = bf16[2,192,512]{2,1,0:T(8,128)(2,1)} collective-permute-done((bf16[2,192,512]{2,1,0:T(8,128)(2,1)}, bf16[2,192,512]{2,1,0:T(8,128)(2,1)}, u32[]{:S(2)}, u32[]{:S(2)}) %collective-permute-start.6) | collective-permute-done | bytes 393248 | tf_op jit(solution)/shard_map/ppermute | solution.py:1312
  96.4 78.6 %dense.1 = (f32[15,8,512]{2,1,0:T(8,128)}, f32[1024,256]{1,0:T(8,128)}, bf16[2,4,4,384,128]{4,3,2,1,0:T(8,128)(2,1)}, f32[2,8,512]{2,1,0:T(8,128)}, bf16[128,1408]{1,0:T(8,128)(2,1)}) custom-call(bf16[2,192,512]{2,1,0:T(8,128)(2,1)} %copy-done.10, bf16[2,192,512]{2,1,0:T(8,128)(2,1)} %collective-permute-done.refs_1_, ...), custom_call_target="tpu_custom_call" | custom-call | tf_op jit(solution)/shard_map/dense/pallas_call | solution.py:1349
  175.0 1.7 slice_bitcast_fusion
  177.3 7.4 %send.1 = bf16[4096,128]{1,0:T(8,128)(2,1)S(1)} custom-call(s32[4096]{0:T(1024)S(1)} %get-tuple-element.133.slot_ref, s32[4096]{0:T(1024)S(1)} %get-tuple-element.132.from_ref, f32[1024,256]{1,0:T(8,128)S(1)} %copy-done.6), custom_call_target="tpu_custom_call" | custom-call | tf_op jit(solution)/shard_map/send/pallas_call | solution.py:1426
  184.7 38.2 %swap.1 = (bf16[32,128,128]{2,1,0:T(8,128)(2,1)S(1)}, bf16[8,16,1408]{2,1,0:T(8,128)(2,1)S(1)}) custom-call(bf16[32,128,128]{2,1,0:T(8,128)(2,1)S(1)} %bitcast.87, bf16[8,16,1408]{2,1,0:T(8,128)(2,1)S(1)} %bitcast.90), custom_call_target="tpu_custom_call" | custom-call | tf_op jit(solution)/shard_map/swap/pallas_call | solution.py:1439
  223.0 1.0 copy-done.7
  223.9 1.6 fusion
  225.5 5.8 %all-to-all-start.1 = ((bf16[16,384,128]{2,1,0:T(8,128)(2,1)}), bf16[16,384,128]{2,1,0:T(8,128)(2,1)}, u32[]{:S(2)}, u32[]{:S(2)}) async-start(bf16[16,384,128]{2,1,0:T(8,128)(2,1)} %bitcast.104), calls=%async_computation.1 | async-start | bytes 3145728 | tf_op jit(solution)/shard_map/all_to_all | solution.py:1241
  232.6 23.5 %add.175 = (bf16[32768,128]{1,0:T(8,128)(2,1)}, f32[8,128]{1,0:T(8,128)}) custom-call(s32[8192]{0:T(1024)} %get-tuple-element.121.at_ref, s32[8192]{0:T(1024)} %get-tuple-element.125.part_at_ref, s32[32]{0:T(128)} %fusion.4.counts_ref, bf16[4096,128]{1,0:T(8,128)(2,1)} %bitcast.88), custom_call_target="tpu_custom_call" | custom-call | tf_op jit(solution)/shard_map/add/pallas_call | solution.py:1466
  256.1 7.2 %all-to-all-done.1 = bf16[16,384,128]{2,1,0:T(8,128)(2,1)} async-done(((bf16[16,384,128]{2,1,0:T(8,128)(2,1)}), bf16[16,384,128]{2,1,0:T(8,128)(2,1)}, u32[]{:S(2)}, u32[]{:S(2)}) %all-to-all-start.1) | async-done | bytes 1572896 | tf_op jit(solution)/shard_map/all_to_all | solution.py:1241
  263.3 1.7 convert_reduce_fusion
  266.7 15.5 %total.1 = (f32[4,8,128]{2,1,0:T(8,128)S(1)}, f32[8,128]{1,0:T(8,128)S(1)}) custom-call(s32[1]{0:T(128)} %bitcast.15.valid_ref, f32[2,8,512]{2,1,0:T(8,128)S(1)} %copy-done.16, f32[15,8,512]{2,1,0:T(8,128)S(1)} %copy-done.12, f32[8,128]{1,0:T(8,128)S(1)} %copy-done.22, f32[16,1408]{1,0:T(8,128)S(1)} %convert_reduce_fusion.1.shares_ref, f32[1536,128]{1,0:T(8,128)S(1)} %bitcast.86), custom_call_target="tpu_custom_call" | custom-call | tf_op jit(solution)/shard_map/total/pallas_call | solution.py:1487
  282.2 1.2 broadcast_in_dim.7
  283.4 6.3 %all-to-all-start.2 = ((bf16[32,16,1408]{2,1,0:T(8,128)(2,1)}), bf16[32,16,1408]{2,1,0:T(8,128)(2,1)}, u32[]{:S(2)}, u32[]{:S(2)}) async-start(bf16[32,16,1408]{2,1,0:T(8,128)(2,1)} %broadcast_in_dim.7), calls=%async_computation.2 | async-start | bytes 2883584 | tf_op jit(solution)/shard_map/all_to_all | solution.py:1246
  290.9 39.0 %tables.1 = (f32[16,64,4096]{2,1,0:T(8,128)}, f32[16,64,4096]{2,1,0:T(8,128)}, f32[16,64,4096]{2,1,0:T(8,128)}) custom-call(f32[8,128]{1,0:T(8,128)} %copy-done.17, f32[16,64,4096]{2,1,0:T(8,128)} %bitcast.100, f32[16,64,4096]{2,1,0:T(8,128)} %bitcast.101, f32[16,64,4096]{2,1,0:T(8,128)} %bitcast.102, bf16[8,4096,128]{2,1,0:T(8,128)(2,1)} %bitcast.103), custom_call_target="tpu_custom_call" | custom-call | tf_op jit(solution)/shard_map/tables/pallas_call | solution.py:1518
  330.6 1.2 pad_maximum_fusion
  332.4 2.7 fusion.6
  335.1 2.1 fusion.8
  337.3 8.0 %small.1 = (f32[512,1280]{1,0:T(8,128)}, f32[512,1280]{1,0:T(8,128)}, f32[512,1280]{1,0:T(8,128)}, f32[40,1024]{1,0:T(8,128)}, f32[40,1024]{1,0:T(8,128)}, /*ind...) custom-call(f32[8,128]{1,0:T(8,128)S(1)} %copy-done.18, ...), custom_call_target="tpu_custom_call" | custom-call | tf_op jit(solution)/shard_map/small/pallas_call | solution.py:1551
  345.5 2.1 multiply_subtract_fusion.2
  (117 shorter events, 17.3 us)
Async XLA Ops:
  16.1 29.7 %copy-start.10 = (bf16[2,192,512]{2,1,0:T(8,128)(2,1)}, bf16[2,192,512]{2,1,0:T(8,128)(2,1)S(1)}, u32[]{:S(2)}) copy-start(bf16[2,192,512]{2,1,0:T(8,128)(2,1)S(1)} %get-tuple-element.70.refs_0_) | copy-start | bytes 1179652
  16.2 29.7 %collective-permute-start = (bf16[2,192,512]{2,1,0:T(8,128)(2,1)S(1)}, bf16[2,192,512]{2,1,0:T(8,128)(2,1)}, u32[]{:S(2)}, u32[]{:S(2)}) collective-permute-start(bf16[2,192,512]{2,1,0:T(8,128)(2,1)S(1)} %get-tuple-element.70.refs_0_), channel_id=1, source_target_pairs={{0,8},{4,12},{8,16},{12,20},{16,24},{20,28},{24,0},{28,4},{1,9},{5... | collective-permute-start | bytes 1179656 | tf_op jit(solution)/shard_map/ppermute | solution.py:1278
  16.8 29.8 %collective-permute-start.1 = (bf16[2,192,512]{2,1,0:T(8,128)(2,1)S(1)}, bf16[2,192,512]{2,1,0:T(8,128)(2,1)}, u32[]{:S(2)}, u32[]{:S(2)}) collective-permute-start(bf16[2,192,512]{2,1,0:T(8,128)(2,1)S(1)} %get-tuple-element.70.refs_0_), channel_id=1, source_target_pairs={{0,16},{4,20},{8,24},{12,28},{16,0},{20,4},{24,8},{28,12},{1,17},{... | collective-permute-start | bytes 1179656 | tf_op jit(solution)/shard_map/ppermute | solution.py:1278
  18.7 27.9 %collective-permute-start.2 = (bf16[2,192,512]{2,1,0:T(8,128)(2,1)S(1)}, bf16[2,192,512]{2,1,0:T(8,128)(2,1)}, u32[]{:S(2)}, u32[]{:S(2)}) collective-permute-start(bf16[2,192,512]{2,1,0:T(8,128)(2,1)S(1)} %get-tuple-element.70.refs_0_), channel_id=1, source_target_pairs={{0,24},{4,28},{8,0},{12,4},{16,8},{20,12},{24,16},{28,20},{1,25},{... | collective-permute-start | bytes 1179656 | tf_op jit(solution)/shard_map/ppermute | solution.py:1278
  20.1 26.5 %collective-permute-start.3 = (bf16[2,192,512]{2,1,0:T(8,128)(2,1)S(1)}, bf16[2,192,512]{2,1,0:T(8,128)(2,1)}, u32[]{:S(2)}, u32[]{:S(2)}) collective-permute-start(bf16[2,192,512]{2,1,0:T(8,128)(2,1)S(1)} %get-tuple-element.70.refs_0_), channel_id=1, source_target_pairs={{0,4},{4,0},{8,12},{12,8},{16,20},{20,16},{24,28},{28,24},{1,5},{5... | collective-permute-start | bytes 1179656 | tf_op jit(solution)/shard_map/ppermute | solution.py:1279
  23.2 34.0 %copy-start.28 = (f32[9517]{0:T(1024)S(1)}, f32[9517]{0:T(1024)}, u32[]{:S(2)}) copy-start(f32[9517]{0:T(1024)} %param.47) | copy-start | bytes 114208
  23.2 38.8 %copy-start = (f32[512,1280]{1,0:T(8,128)S(1)}, f32[512,1280]{1,0:T(8,128)}, u32[]{:S(2)}) copy-start(f32[512,1280]{1,0:T(8,128)} %t0_ref.1) | copy-start | bytes 7864324
  46.6 16.5 %copy-start.30 = (s32[256,5]{0,1:T(8,128)S(1)}, s32[256,5]{0,1:T(8,128)}, u32[]{:S(2)}) copy-start(s32[256,5]{0,1:T(8,128)} %param.27) | copy-start | bytes 15364
  46.6 36.6 %all-to-all-start = ((bf16[32,128,128]{2,1,0:T(8,128)(2,1)}), bf16[32,128,128]{2,1,0:T(8,128)(2,1)}, u32[]{:S(2)}, u32[]{:S(2)}) async-start(bf16[32,128,128]{2,1,0:T(8,128)(2,1)} %bitcast.105), calls=%async_computation | async-start | bytes 2097152 | tf_op jit(solution)/shard_map/all_to_all | solution.py:1246
  57.2 6.8 %copy-start.31 = (s32[256,5]{0,1:T(8,128)S(1)}, s32[256,5]{0,1:T(8,128)}, u32[]{:S(2)}) copy-start(s32[256,5]{0,1:T(8,128)} %param.28) | copy-start | bytes 15364
  57.2 8.1 %copy-start.32 = (s32[8]{0:T(128)S(1)}, s32[8]{0:T(128)}, u32[]{:S(2)}) copy-start(s32[8]{0:T(128)} %param.26) | copy-start | bytes 100
  57.2 9.3 %copy-start.8 = (f32[1024,40]{0,1:T(8,128)S(1)}, f32[1024,40]{0,1:T(8,128)}, u32[]{:S(2)}) copy-start(f32[1024,40]{0,1:T(8,128)} %param.38) | copy-start | bytes 491524
  57.8 31.6 %collective-permute-start.4 = (bf16[2,192,512]{2,1,0:T(8,128)(2,1)}, bf16[2,192,512]{2,1,0:T(8,128)(2,1)}, u32[]{:S(2)}, u32[]{:S(2)}) collective-permute-start(bf16[2,192,512]{2,1,0:T(8,128)(2,1)} %collective-permute-done.refs_1_), channel_id=1, source_target_pairs={{0,4},{4,0},{8,12},{12,8},{16,20},{20,16},{24,28},{28,24},{1,5},{5... | collective-permute-start | bytes 1179656 | tf_op jit(solution)/shard_map/ppermute | solution.py:1312
  59.4 30.1 %collective-permute-start.5 = (bf16[2,192,512]{2,1,0:T(8,128)(2,1)}, bf16[2,192,512]{2,1,0:T(8,128)(2,1)}, u32[]{:S(2)}, u32[]{:S(2)}) collective-permute-start(bf16[2,192,512]{2,1,0:T(8,128)(2,1)} %collective-permute-done.1.refs_2_), channel_id=1, source_target_pairs={{0,4},{4,0},{8,12},{12,8},{16,20},{20,16},{24,28},{28,24},{1,5},{5... | collective-permute-start | bytes 1179656 | tf_op jit(solution)/shard_map/ppermute | solution.py:1312
  59.9 36.6 %collective-permute-start.6 = (bf16[2,192,512]{2,1,0:T(8,128)(2,1)}, bf16[2,192,512]{2,1,0:T(8,128)(2,1)}, u32[]{:S(2)}, u32[]{:S(2)}) collective-permute-start(bf16[2,192,512]{2,1,0:T(8,128)(2,1)} %collective-permute-done.2.refs_3_), channel_id=1, source_target_pairs={{0,4},{4,0},{8,12},{12,8},{16,20},{20,16},{24,28},{28,24},{1,5},{5... | collective-permute-start | bytes 1179656 | tf_op jit(solution)/shard_map/ppermute | solution.py:1312
  175.0 9.7 %copy-start.11 = (bf16[128,1408]{1,0:T(8,128)(2,1)S(1)}, bf16[128,1408]{1,0:T(8,128)(2,1)}, u32[]{:S(2)}) copy-start(bf16[128,1408]{1,0:T(8,128)(2,1)} %get-tuple-element.79) | copy-start | bytes 1081348
  175.0 48.9 %copy-start.23 = (bf16[2,4,4,384,128]{4,3,2,1,0:T(8,128)(2,1)S(1)}, bf16[2,4,4,384,128]{4,3,2,1,0:T(8,128)(2,1)}, u32[]{:S(2)}) copy-start(bf16[2,4,4,384,128]{4,3,2,1,0:T(8,128)(2,1)} %get-tuple-element.83) | copy-start | bytes 9437188
  176.7 47.2 %collective-permute-start.7 = (bf16[4,4,384,128]{3,2,1,0:T(8,128)(2,1)S(1)}, bf16[4,4,384,128]{3,2,1,0:T(8,128)(2,1)S(1)}, u32[]{:S(2)}, u32[]{:S(2)}) collective-permute-start(bf16[4,4,384,128]{3,2,1,0:T(8,128)(2,1)S(1)} %slice_bitcast_fusion), channel_id=1, source_target_pairs={{0,4},{4,0},{8,12},{12,8},{16,20},{20,16},{24,28},{28,24},{1,5},{5... | collective-permute-start | bytes 4718600 | tf_op jit(solution)/shard_map/ppermute | solution.py:1454
  225.5 37.8 %all-to-all-start.1 = ((bf16[16,384,128]{2,1,0:T(8,128)(2,1)}), bf16[16,384,128]{2,1,0:T(8,128)(2,1)}, u32[]{:S(2)}, u32[]{:S(2)}) async-start(bf16[16,384,128]{2,1,0:T(8,128)(2,1)} %bitcast.104), calls=%async_computation.1 | async-start | bytes 3145728 | tf_op jit(solution)/shard_map/all_to_all | solution.py:1241
  231.3 33.8 %copy-start.16 = (f32[2,8,512]{2,1,0:T(8,128)S(1)}, f32[2,8,512]{2,1,0:T(8,128)}, u32[]{:S(2)}) copy-start(f32[2,8,512]{2,1,0:T(8,128)} %get-tuple-element.81.inner_ref) | copy-start | bytes 98308
  263.3 18.9 %copy-start.27 = (bf16[16,1408]{1,0:T(8,128)(2,1)S(1)}, bf16[16,1408]{1,0:T(8,128)(2,1)}, u32[]{:S(2)}) copy-start(bf16[16,1408]{1,0:T(8,128)(2,1)} %convert_element_type.39) | copy-start | bytes 135172
  282.2 8.6 %copy-start.17 = (f32[8,128]{1,0:T(8,128)}, f32[8,128]{1,0:T(8,128)S(1)}, u32[]{:S(2)}) copy-start(f32[8,128]{1,0:T(8,128)S(1)} %get-tuple-element.90.factor_ref.result_ref) | copy-start | bytes 12292
  283.4 53.8 %all-to-all-start.2 = ((bf16[32,16,1408]{2,1,0:T(8,128)(2,1)}), bf16[32,16,1408]{2,1,0:T(8,128)(2,1)}, u32[]{:S(2)}, u32[]{:S(2)}) async-start(bf16[32,16,1408]{2,1,0:T(8,128)(2,1)} %broadcast_in_dim.7), calls=%async_computation.2 | async-start | bytes 2883584 | tf_op jit(solution)/shard_map/all_to_all | solution.py:1246
  290.9 39.1 %copy-start.18 = (f32[8,128]{1,0:T(8,128)S(1)}, f32[8,128]{1,0:T(8,128)}, u32[]{:S(2)}) copy-start(f32[8,128]{1,0:T(8,128)} %copy-done.17) | copy-start | bytes 12292
  290.9 41.5 %copy-start.5 = (f32[64,8,128]{2,1,0:T(8,128)S(1)}, f32[64,8,128]{2,1,0:T(8,128)}, u32[]{:S(2)}) copy-start(f32[64,8,128]{2,1,0:T(8,128)} %second_ref.1) | copy-start | bytes 786436
  290.9 41.5 %copy-start.26 = (f32[64,8,128]{2,1,0:T(8,128)S(1)}, f32[64,8,128]{2,1,0:T(8,128)}, u32[]{:S(2)}) copy-start(f32[64,8,128]{2,1,0:T(8,128)} %param.36) | copy-start | bytes 786436
  290.9 44.2 %copy-start.3 = (f32[128,8,128]{2,1,0:T(8,128)S(1)}, f32[128,8,128]{2,1,0:T(8,128)}, u32[]{:S(2)}) copy-start(f32[128,8,128]{2,1,0:T(8,128)} %first_ref.1) | copy-start | bytes 1572868
  290.9 44.2 %copy-start.24 = (f32[128,8,128]{2,1,0:T(8,128)S(1)}, f32[128,8,128]{2,1,0:T(8,128)}, u32[]{:S(2)}) copy-start(f32[128,8,128]{2,1,0:T(8,128)} %param.33) | copy-start | bytes 1572868
  290.9 44.2 %copy-start.25 = (f32[128,8,128]{2,1,0:T(8,128)S(1)}, f32[128,8,128]{2,1,0:T(8,128)}, u32[]{:S(2)}) copy-start(f32[128,8,128]{2,1,0:T(8,128)} %param.34) | copy-start | bytes 1572868
  332.3 4.9 %copy-start.9 = (f32[1024,40]{0,1:T(8,128)S(1)}, f32[1024,40]{0,1:T(8,128)}, u32[]{:S(2)}) copy-start(f32[1024,40]{0,1:T(8,128)} %param.38) | copy-start | bytes 491524
  332.3 4.9 %copy-start.13 = (f32[1024,40]{0,1:T(8,128)S(1)}, f32[1024,40]{0,1:T(8,128)}, u32[]{:S(2)}) copy-start(f32[1024,40]{0,1:T(8,128)} %param.39) | copy-start | bytes 491524
  337.3 8.2 %copy-start.29 = (f32[9517]{0:T(1024)S(1)}, f32[9517]{0:T(1024)}, u32[]{:S(2)}) copy-start(f32[9517]{0:T(1024)} %param.47) | copy-start | bytes 114208
  (12 other events, 28.1 us)

commit v7 on v6

--- a/solution.py
+++ b/solution.py
@@ -96,10 +96,11 @@
     return lax.broadcasted_iota(I32, shape, len(shape) - 1) < 64
 
 
-def find_kernel(groups, at_ref, counts_ref, table_ref, out_ref, turned_ref, rows_ref):
+def find_kernel(groups, first_group, at_ref, counts_ref, table_ref, *refs):
+    out_ref, turned_ref, rows_ref = refs[-3:]
     blocks, _, height, lanes = out_ref.shape
     tables, width, rows_dev = table_ref.shape
-    group = pl.program_id(0)
+    group = pl.program_id(0) + first_group
     left = left_lanes((1, lanes))
     part = 512
 
@@ -1290,26 +1291,34 @@
     part_at = jnp.where(plain > 0, part_at, 4 * slots)
 
     table_view = jnp.transpose(embeddings, (0, 2, 1))
-    found = pl.pallas_call(
-        functools.partial(find_kernel, mp_count),
-        grid=(mp_count,),
-        out_shape=jax.ShapeDtypeStruct((dp_count, mp_count, height, lanes), LOW),
-        in_specs=[
-            SMEM,
-            SMEM,
-            pl.BlockSpec((tables_here, d_emb, rows_dev), lambda m: (m, 0, 0)),
-        ],
-        out_specs=pl.BlockSpec((dp_count, 1, height, lanes), lambda m: (0, m, 0, 0)),
-        scratch_shapes=[
-            pltpu.VMEM((tables_here * rows_dev, lanes), F32),
-            pltpu.VMEM((height, lanes), F32),
-        ],
-        compiler_params=params(60),
-        name="find",
-    )(turned_at.reshape(-1), asked, table_view)
-    w_far, w_near, found = lax.optimization_barrier((w_far, w_near, found))
-    w_mine = [shard] + w_far
-    w_theirs = [w_near] + [lax.ppermute(line, "dp", partners) for line in w_far]
+    def find(first, many, before):
+        return pl.pallas_call(
+            functools.partial(find_kernel, mp_count, first),
+            grid=(many,),
+            out_shape=jax.ShapeDtypeStruct((dp_count, mp_count, height, lanes), LOW),
+            in_specs=[
+                SMEM,
+                SMEM,
+                pl.BlockSpec((tables_here, d_emb, rows_dev), lambda m: (m + first, 0, 0)),
+            ]
+            + [pl.BlockSpec(memory_space=pl.ANY)] * len(before),
+            out_specs=pl.BlockSpec((dp_count, 1, height, lanes), lambda m: (0, m + first, 0, 0)),
+            scratch_shapes=[
+                pltpu.VMEM((tables_here * rows_dev, lanes), F32),
+                pltpu.VMEM((height, lanes), F32),
+            ],
+            input_output_aliases={3: 0} if before else {},
+            compiler_params=params(60),
+            name="find",
+        )(turned_at.reshape(-1), asked, table_view, *before)
+
+    found = find(0, mp_count // 2, [])
+    line, found = lax.optimization_barrier((w_far[0], found))
+    w_theirs = [w_near, lax.ppermute(line, "dp", partners)]
+    found = find(mp_count // 2, mp_count - mp_count // 2, [found])
+    rest, w_theirs, found = lax.optimization_barrier((w_far[1:], w_theirs, found))
+    w_mine = [shard, line] + rest
+    w_theirs = w_theirs + [lax.ppermute(line, "dp", partners) for line in rest]
     returned = exchange_all(found.reshape(devices, height, lanes))
     embedded = pl.pallas_call(
         place_kernel,

time: 349 us -> 344 us (0.986)
  waiting for transfers between devices: 31 us -> 26 us
    ppermute x3, waiting for transfers between devices: 6.95 us -> 0.01 us  [the longest x2 0.01 us: body(): w_theirs = w_theirs + [lax.ppermute(line, 'dp', partners) for line in rest]]
    pallas_call x1 -> x2, Pallas kernels: 22.6 us -> 25.4 us  [find(): pl.pallas_call(functools.partial(find_kernel, mp_count, first), grid=(man...]
  transfers between devices with their start and end apart: 11 -> 11, of which waited for: 4 -> 2; matrix products, arithmetic and copies ran while one was open for 5% -> 5% of each run, Pallas kernels for 37% -> 38%
where the time goes in v7:
time: 344 us; the launch traced here: 343 us
  Pallas kernels  252 us (73%)
  starting transfers between devices  31.8 us (9%)
  waiting for transfers between devices  26 us (8%)
  local copies, waits for them, and re-layouts  16.2 us (5%)
  other arithmetic  16 us (5%)
    pallas_call x1, Pallas kernels, body(): pl.pallas_call(functools.partial(dense_kernel, dp_count // 2), out_shape=...  78.2 us
    pallas_call x1, Pallas kernels, body(): pl.pallas_call(table_kernel, grid=(pairs,), out_shape=(jax.ShapeDtypeStru...  39 us
    pallas_call x1, Pallas kernels, body(): pl.pallas_call(swap_kernel, out_shape=(jax.ShapeDtypeStruct((devices, hei...  37.6 us
    pallas_call x2, Pallas kernels, find(): pl.pallas_call(functools.partial(find_kernel, mp_count, first), grid=(man...  25.4 us
    pallas_call x1, Pallas kernels, body(): pl.pallas_call(functools.partial(add_kernel, mp_count), out_shape=(jax.Sh...  22.3 us
    all_to_all x2, waiting for transfers between devices, exchange_all(): return lax.all_to_all(parts, AXES, split_axis=0, concat_axis=0, tiled=True)  17.9 us
    all_to_all x2, starting transfers between devices, exchange_all(): return lax.all_to_all(parts, AXES, split_axis=0, concat_axis=0, tiled=True)  17.6 us
    pallas_call x1, Pallas kernels, body(): pl.pallas_call(functools.partial(total_kernel, features, width_out), out_...  15.5 us
  transfers between devices with their start and end apart: 11, of which 2 were waited for; matrix products, arithmetic and copies ran while one was open for 5% of the time, Pallas kernels for 38%

profile of v7, /device:TPU:0, one launch (start us, length us, event | category | flops | bytes accessed | tf_op | source)
XLA Modules:
  0.0 342.9 jit_solution(14933229149000870462)
XLA Ops:
  0.7 1.0 copy-done.2
  3.4 12.8 %ask.1 = (s32[32,1,256]{2,1,0:T(1,128)S(1)}, bf16[2,192,512]{2,1,0:T(8,128)(2,1)S(1)}, s32[4,1024]{1,0:T(4,128)S(1)}, s32[4,1024]{1,0:T(4,128)S(1)}, s32[4,1024]{1,0:T(4,128)S(1)}) custom-call(s32[4,1024]{1,0:T(4,128)S(1)} %bitcast.94, f32[128,8,128]{2,1,0:T(8,128)S(1)} %copy-done.2, f32[64,8,128]{2,1,0:T(8,128)S(1)} %copy-done.4), custom_call_target="tpu_custom_call" | custom-call | tf_op jit(solution)/shard_map/ask/pallas_call | solution.py:1252
  16.8 1.9 collective-permute-start.1
  18.7 1.4 collective-permute-start.2
  20.1 1.4 collective-permute-start.3
  23.2 12.5 %find.2.refs_0_ = bf16[8,4,128,128]{3,2,1,0:T(8,128)(2,1)} custom-call(s32[8192]{0:T(1024)} %get-tuple-element.126.at_ref, s32[32]{0:T(128)} %fusion.4.counts_ref, f32[16,64,4096]{2,1,0:T(8,128)} %bitcast.99), custom_call_target="tpu_custom_call" | custom-call | tf_op jit(solution)/shard_map/find/pallas_call | solution.py:1295
  36.3 12.9 %find.3 = bf16[8,4,128,128]{3,2,1,0:T(8,128)(2,1)} custom-call(s32[8192]{0:T(1024)} %get-tuple-element.126.at_ref, s32[32]{0:T(128)} %fusion.4.counts_ref, f32[16,64,4096]{2,1,0:T(8,128)} %bitcast.100, bf16[8,4,128,128]{3,2,1,0:T(8,128)(2,1)} %find.2.refs_0_), custom_call_target="tpu_custom_call", output_to_operand_aliasing={{}: (3, {})} | custom-call | tf_op jit(solution)/shard_map/find/pallas_call | solution.py:1295
  49.3 11.3 %all-to-all-start = ((bf16[32,128,128]{2,1,0:T(8,128)(2,1)}), bf16[32,128,128]{2,1,0:T(8,128)(2,1)}, u32[]{:S(2)}, u32[]{:S(2)}) async-start(bf16[32,128,128]{2,1,0:T(8,128)(2,1)} %bitcast.104), calls=%async_computation | async-start | bytes 2097152 | tf_op jit(solution)/shard_map/all_to_all | solution.py:1247
  61.3 1.5 collective-permute-start.5
  63.9 1.2 convert_element_type.37.refs_14_
  69.1 17.9 %all-to-all-done = bf16[32,128,128]{2,1,0:T(8,128)(2,1)} async-done(((bf16[32,128,128]{2,1,0:T(8,128)(2,1)}), bf16[32,128,128]{2,1,0:T(8,128)(2,1)}, u32[]{:S(2)}, u32[]{:S(2)}) %all-to-all-start) | async-done | bytes 1048608 | tf_op jit(solution)/shard_map/all_to_all | solution.py:1247
  87.0 5.4 %place.1.refs_9_ = bf16[1024,256]{1,0:T(8,128)(2,1)S(1)} custom-call(s32[4096]{0:T(1024)S(1)} %bitcast.93, bf16[4096,128]{1,0:T(8,128)(2,1)} %bitcast.5.rows_ref), custom_call_target="tpu_custom_call" | custom-call | tf_op jit(solution)/shard_map/place/pallas_call | solution.py:1323
  93.2 78.2 %dense.1 = (f32[15,8,512]{2,1,0:T(8,128)}, f32[1024,256]{1,0:T(8,128)}, bf16[2,4,4,384,128]{4,3,2,1,0:T(8,128)(2,1)}, f32[2,8,512]{2,1,0:T(8,128)}, bf16[128,1408]{1,0:T(8,128)(2,1)}) custom-call(bf16[2,192,512]{2,1,0:T(8,128)(2,1)} %copy-done.10, bf16[2,192,512]{2,1,0:T(8,128)(2,1)} %collective-permute-done.refs_1_, ...), custom_call_target="tpu_custom_call" | custom-call | tf_op jit(solution)/shard_map/dense/pallas_call | solution.py:1358
  171.5 1.7 slice_bitcast_fusion
  173.2 1.6 collective-permute-start.7
  174.8 7.4 %send.1 = bf16[4096,128]{1,0:T(8,128)(2,1)S(1)} custom-call(s32[4096]{0:T(1024)S(1)} %get-tuple-element.137.slot_ref, s32[4096]{0:T(1024)S(1)} %get-tuple-element.136.from_ref, f32[1024,256]{1,0:T(8,128)S(1)} %copy-done.6), custom_call_target="tpu_custom_call" | custom-call | tf_op jit(solution)/shard_map/send/pallas_call | solution.py:1435
  182.2 37.6 %swap.1 = (bf16[32,128,128]{2,1,0:T(8,128)(2,1)S(1)}, bf16[8,16,1408]{2,1,0:T(8,128)(2,1)S(1)}) custom-call(bf16[32,128,128]{2,1,0:T(8,128)(2,1)S(1)} %bitcast.87, bf16[8,16,1408]{2,1,0:T(8,128)(2,1)S(1)} %bitcast.90), custom_call_target="tpu_custom_call" | custom-call | tf_op jit(solution)/shard_map/swap/pallas_call | solution.py:1448
  219.7 1.0 copy-done.7
  220.7 1.6 fusion
  222.3 4.6 %all-to-all-start.1 = ((bf16[16,384,128]{2,1,0:T(8,128)(2,1)}), bf16[16,384,128]{2,1,0:T(8,128)(2,1)}, u32[]{:S(2)}, u32[]{:S(2)}) async-start(bf16[16,384,128]{2,1,0:T(8,128)(2,1)} %bitcast.106), calls=%async_computation.1 | async-start | bytes 3145728 | tf_op jit(solution)/shard_map/all_to_all | solution.py:1242
  228.2 22.3 %add.175 = (bf16[32768,128]{1,0:T(8,128)(2,1)}, f32[8,128]{1,0:T(8,128)}) custom-call(s32[8192]{0:T(1024)} %get-tuple-element.125.at_ref, s32[8192]{0:T(1024)} %get-tuple-element.129.part_at_ref, s32[32]{0:T(128)} %fusion.4.counts_ref, bf16[4096,128]{1,0:T(8,128)(2,1)} %bitcast.88), custom_call_target="tpu_custom_call" | custom-call | tf_op jit(solution)/shard_map/add/pallas_call | solution.py:1475
  250.6 8.1 %all-to-all-done.1 = bf16[16,384,128]{2,1,0:T(8,128)(2,1)} async-done(((bf16[16,384,128]{2,1,0:T(8,128)(2,1)}), bf16[16,384,128]{2,1,0:T(8,128)(2,1)}, u32[]{:S(2)}, u32[]{:S(2)}) %all-to-all-start.1) | async-done | bytes 1572896 | tf_op jit(solution)/shard_map/all_to_all | solution.py:1242
  258.7 1.7 convert_reduce_fusion
  262.0 15.5 %total.1 = (f32[4,8,128]{2,1,0:T(8,128)S(1)}, f32[8,128]{1,0:T(8,128)S(1)}) custom-call(s32[1]{0:T(128)} %bitcast.15.valid_ref, f32[2,8,512]{2,1,0:T(8,128)S(1)} %copy-done.16, f32[15,8,512]{2,1,0:T(8,128)S(1)} %copy-done.12, f32[8,128]{1,0:T(8,128)S(1)} %copy-done.22, f32[16,1408]{1,0:T(8,128)S(1)} %convert_reduce_fusion.1.shares_ref, f32[1536,128]{1,0:T(8,128)S(1)} %bitcast.86), custom_call_target="tpu_custom_call" | custom-call | tf_op jit(solution)/shard_map/total/pallas_call | solution.py:1496
  277.6 1.2 broadcast_in_dim.7
  278.8 6.3 %all-to-all-start.2 = ((bf16[32,16,1408]{2,1,0:T(8,128)(2,1)}), bf16[32,16,1408]{2,1,0:T(8,128)(2,1)}, u32[]{:S(2)}, u32[]{:S(2)}) async-start(bf16[32,16,1408]{2,1,0:T(8,128)(2,1)} %broadcast_in_dim.7), calls=%async_computation.2 | async-start | bytes 2883584 | tf_op jit(solution)/shard_map/all_to_all | solution.py:1247
  286.3 39.0 %tables.1 = (f32[16,64,4096]{2,1,0:T(8,128)}, f32[16,64,4096]{2,1,0:T(8,128)}, f32[16,64,4096]{2,1,0:T(8,128)}) custom-call(f32[8,128]{1,0:T(8,128)} %copy-done.17, f32[16,64,4096]{2,1,0:T(8,128)} %bitcast.101, f32[16,64,4096]{2,1,0:T(8,128)} %bitcast.102, f32[16,64,4096]{2,1,0:T(8,128)} %bitcast.103, bf16[8,4096,128]{2,1,0:T(8,128)(2,1)} %bitcast.105), custom_call_target="tpu_custom_call" | custom-call | tf_op jit(solution)/shard_map/tables/pallas_call | solution.py:1527
  325.9 1.2 pad_maximum_fusion
  327.7 2.7 fusion.6
  330.4 2.1 fusion.8
  332.6 8.0 %small.1 = (f32[512,1280]{1,0:T(8,128)}, f32[512,1280]{1,0:T(8,128)}, f32[512,1280]{1,0:T(8,128)}, f32[40,1024]{1,0:T(8,128)}, f32[40,1024]{1,0:T(8,128)}, /*ind...) custom-call(f32[8,128]{1,0:T(8,128)S(1)} %copy-done.18, ...), custom_call_target="tpu_custom_call" | custom-call | tf_op jit(solution)/shard_map/small/pallas_call | solution.py:1560
  340.8 2.1 multiply_subtract_fusion.2
  (118 shorter events, 16.6 us)
Async XLA Ops:
  16.1 19.5 %copy-start.10 = (bf16[2,192,512]{2,1,0:T(8,128)(2,1)}, bf16[2,192,512]{2,1,0:T(8,128)(2,1)S(1)}, u32[]{:S(2)}) copy-start(bf16[2,192,512]{2,1,0:T(8,128)(2,1)S(1)} %get-tuple-element.72.refs_0_) | copy-start | bytes 1179652
  16.2 19.5 %collective-permute-start = (bf16[2,192,512]{2,1,0:T(8,128)(2,1)S(1)}, bf16[2,192,512]{2,1,0:T(8,128)(2,1)}, u32[]{:S(2)}, u32[]{:S(2)}) collective-permute-start(bf16[2,192,512]{2,1,0:T(8,128)(2,1)S(1)} %get-tuple-element.72.refs_0_), channel_id=1, source_target_pairs={{0,8},{4,12},{8,16},{12,20},{16,24},{20,28},{24,0},{28,4},{1,9},{5... | collective-permute-start | bytes 1179656 | tf_op jit(solution)/shard_map/ppermute | solution.py:1279
  16.8 32.4 %collective-permute-start.1 = (bf16[2,192,512]{2,1,0:T(8,128)(2,1)S(1)}, bf16[2,192,512]{2,1,0:T(8,128)(2,1)}, u32[]{:S(2)}, u32[]{:S(2)}) collective-permute-start(bf16[2,192,512]{2,1,0:T(8,128)(2,1)S(1)} %get-tuple-element.72.refs_0_), channel_id=1, source_target_pairs={{0,16},{4,20},{8,24},{12,28},{16,0},{20,4},{24,8},{28,12},{1,17},{... | collective-permute-start | bytes 1179656 | tf_op jit(solution)/shard_map/ppermute | solution.py:1279
  18.7 30.6 %collective-permute-start.2 = (bf16[2,192,512]{2,1,0:T(8,128)(2,1)S(1)}, bf16[2,192,512]{2,1,0:T(8,128)(2,1)}, u32[]{:S(2)}, u32[]{:S(2)}) collective-permute-start(bf16[2,192,512]{2,1,0:T(8,128)(2,1)S(1)} %get-tuple-element.72.refs_0_), channel_id=1, source_target_pairs={{0,24},{4,28},{8,0},{12,4},{16,8},{20,12},{24,16},{28,20},{1,25},{... | collective-permute-start | bytes 1179656 | tf_op jit(solution)/shard_map/ppermute | solution.py:1279
  20.1 29.2 %collective-permute-start.3 = (bf16[2,192,512]{2,1,0:T(8,128)(2,1)S(1)}, bf16[2,192,512]{2,1,0:T(8,128)(2,1)}, u32[]{:S(2)}, u32[]{:S(2)}) collective-permute-start(bf16[2,192,512]{2,1,0:T(8,128)(2,1)S(1)} %get-tuple-element.72.refs_0_), channel_id=1, source_target_pairs={{0,4},{4,0},{8,12},{12,8},{16,20},{20,16},{24,28},{28,24},{1,5},{5... | collective-permute-start | bytes 1179656 | tf_op jit(solution)/shard_map/ppermute | solution.py:1280
  35.7 25.0 %copy-start.28 = (f32[9517]{0:T(1024)S(1)}, f32[9517]{0:T(1024)}, u32[]{:S(2)}) copy-start(f32[9517]{0:T(1024)} %param.47) | copy-start | bytes 114208
  35.7 13.6 %collective-permute-start.4 = (bf16[2,192,512]{2,1,0:T(8,128)(2,1)}, bf16[2,192,512]{2,1,0:T(8,128)(2,1)}, u32[]{:S(2)}, u32[]{:S(2)}) collective-permute-start(bf16[2,192,512]{2,1,0:T(8,128)(2,1)} %collective-permute-done.refs_1_), channel_id=1, source_target_pairs={{0,4},{4,0},{8,12},{12,8},{16,20},{20,16},{24,28},{28,24},{1,5},{5... | collective-permute-start | bytes 1179656 | tf_op jit(solution)/shard_map/ppermute | solution.py:1317
  36.3 27.6 %copy-start = (f32[512,1280]{1,0:T(8,128)S(1)}, f32[512,1280]{1,0:T(8,128)}, u32[]{:S(2)}) copy-start(f32[512,1280]{1,0:T(8,128)} %t0_ref.1) | copy-start | bytes 7864324
  49.3 15.8 %copy-start.30 = (s32[256,5]{0,1:T(8,128)S(1)}, s32[256,5]{0,1:T(8,128)}, u32[]{:S(2)}) copy-start(s32[256,5]{0,1:T(8,128)} %param.27) | copy-start | bytes 15364
  49.3 37.7 %all-to-all-start = ((bf16[32,128,128]{2,1,0:T(8,128)(2,1)}), bf16[32,128,128]{2,1,0:T(8,128)(2,1)}, u32[]{:S(2)}, u32[]{:S(2)}) async-start(bf16[32,128,128]{2,1,0:T(8,128)(2,1)} %bitcast.104), calls=%async_computation | async-start | bytes 2097152 | tf_op jit(solution)/shard_map/all_to_all | solution.py:1247
  60.6 5.2 %copy-start.31 = (s32[256,5]{0,1:T(8,128)S(1)}, s32[256,5]{0,1:T(8,128)}, u32[]{:S(2)}) copy-start(s32[256,5]{0,1:T(8,128)} %param.28) | copy-start | bytes 15364
  60.7 6.6 %copy-start.32 = (s32[8]{0:T(128)S(1)}, s32[8]{0:T(128)}, u32[]{:S(2)}) copy-start(s32[8]{0:T(128)} %param.26) | copy-start | bytes 100
  60.7 7.8 %copy-start.8 = (f32[1024,40]{0,1:T(8,128)S(1)}, f32[1024,40]{0,1:T(8,128)}, u32[]{:S(2)}) copy-start(f32[1024,40]{0,1:T(8,128)} %param.38) | copy-start | bytes 491524
  61.3 32.0 %collective-permute-start.5 = (bf16[2,192,512]{2,1,0:T(8,128)(2,1)}, bf16[2,192,512]{2,1,0:T(8,128)(2,1)}, u32[]{:S(2)}, u32[]{:S(2)}) collective-permute-start(bf16[2,192,512]{2,1,0:T(8,128)(2,1)} %collective-permute-done.1.refs_2_), channel_id=1, source_target_pairs={{0,4},{4,0},{8,12},{12,8},{16,20},{20,16},{24,28},{28,24},{1,5},{5... | collective-permute-start | bytes 1179656 | tf_op jit(solution)/shard_map/ppermute | solution.py:1321
  62.8 30.4 %collective-permute-start.6 = (bf16[2,192,512]{2,1,0:T(8,128)(2,1)}, bf16[2,192,512]{2,1,0:T(8,128)(2,1)}, u32[]{:S(2)}, u32[]{:S(2)}) collective-permute-start(bf16[2,192,512]{2,1,0:T(8,128)(2,1)} %collective-permute-done.2.refs_3_), channel_id=1, source_target_pairs={{0,4},{4,0},{8,12},{12,8},{16,20},{20,16},{24,28},{28,24},{1,5},{5... | collective-permute-start | bytes 1179656 | tf_op jit(solution)/shard_map/ppermute | solution.py:1321
  171.5 10.7 %copy-start.11 = (bf16[128,1408]{1,0:T(8,128)(2,1)S(1)}, bf16[128,1408]{1,0:T(8,128)(2,1)}, u32[]{:S(2)}) copy-start(bf16[128,1408]{1,0:T(8,128)(2,1)} %get-tuple-element.83) | copy-start | bytes 1081348
  171.5 49.2 %copy-start.23 = (bf16[2,4,4,384,128]{4,3,2,1,0:T(8,128)(2,1)S(1)}, bf16[2,4,4,384,128]{4,3,2,1,0:T(8,128)(2,1)}, u32[]{:S(2)}) copy-start(bf16[2,4,4,384,128]{4,3,2,1,0:T(8,128)(2,1)} %get-tuple-element.87) | copy-start | bytes 9437188
  173.2 47.5 %collective-permute-start.7 = (bf16[4,4,384,128]{3,2,1,0:T(8,128)(2,1)S(1)}, bf16[4,4,384,128]{3,2,1,0:T(8,128)(2,1)S(1)}, u32[]{:S(2)}, u32[]{:S(2)}) collective-permute-start(bf16[4,4,384,128]{3,2,1,0:T(8,128)(2,1)S(1)} %slice_bitcast_fusion), channel_id=1, source_target_pairs={{0,4},{4,0},{8,12},{12,8},{16,20},{20,16},{24,28},{28,24},{1,5},{5... | collective-permute-start | bytes 4718600 | tf_op jit(solution)/shard_map/ppermute | solution.py:1463
  222.3 36.4 %all-to-all-start.1 = ((bf16[16,384,128]{2,1,0:T(8,128)(2,1)}), bf16[16,384,128]{2,1,0:T(8,128)(2,1)}, u32[]{:S(2)}, u32[]{:S(2)}) async-start(bf16[16,384,128]{2,1,0:T(8,128)(2,1)} %bitcast.106), calls=%async_computation.1 | async-start | bytes 3145728 | tf_op jit(solution)/shard_map/all_to_all | solution.py:1242
  226.9 33.5 %copy-start.16 = (f32[2,8,512]{2,1,0:T(8,128)S(1)}, f32[2,8,512]{2,1,0:T(8,128)}, u32[]{:S(2)}) copy-start(f32[2,8,512]{2,1,0:T(8,128)} %get-tuple-element.85.inner_ref) | copy-start | bytes 98308
  258.7 18.9 %copy-start.27 = (bf16[16,1408]{1,0:T(8,128)(2,1)S(1)}, bf16[16,1408]{1,0:T(8,128)(2,1)}, u32[]{:S(2)}) copy-start(bf16[16,1408]{1,0:T(8,128)(2,1)} %convert_element_type.39) | copy-start | bytes 135172
  277.5 8.6 %copy-start.17 = (f32[8,128]{1,0:T(8,128)}, f32[8,128]{1,0:T(8,128)S(1)}, u32[]{:S(2)}) copy-start(f32[8,128]{1,0:T(8,128)S(1)} %get-tuple-element.94.factor_ref.result_ref) | copy-start | bytes 12292
  278.8 53.8 %all-to-all-start.2 = ((bf16[32,16,1408]{2,1,0:T(8,128)(2,1)}), bf16[32,16,1408]{2,1,0:T(8,128)(2,1)}, u32[]{:S(2)}, u32[]{:S(2)}) async-start(bf16[32,16,1408]{2,1,0:T(8,128)(2,1)} %broadcast_in_dim.7), calls=%async_computation.2 | async-start | bytes 2883584 | tf_op jit(solution)/shard_map/all_to_all | solution.py:1247
  286.2 39.1 %copy-start.18 = (f32[8,128]{1,0:T(8,128)S(1)}, f32[8,128]{1,0:T(8,128)}, u32[]{:S(2)}) copy-start(f32[8,128]{1,0:T(8,128)} %copy-done.17) | copy-start | bytes 12292
  286.2 41.5 %copy-start.5 = (f32[64,8,128]{2,1,0:T(8,128)S(1)}, f32[64,8,128]{2,1,0:T(8,128)}, u32[]{:S(2)}) copy-start(f32[64,8,128]{2,1,0:T(8,128)} %second_ref.1) | copy-start | bytes 786436
  286.2 41.5 %copy-start.26 = (f32[64,8,128]{2,1,0:T(8,128)S(1)}, f32[64,8,128]{2,1,0:T(8,128)}, u32[]{:S(2)}) copy-start(f32[64,8,128]{2,1,0:T(8,128)} %param.36) | copy-start | bytes 786436
  286.2 44.2 %copy-start.3 = (f32[128,8,128]{2,1,0:T(8,128)S(1)}, f32[128,8,128]{2,1,0:T(8,128)}, u32[]{:S(2)}) copy-start(f32[128,8,128]{2,1,0:T(8,128)} %first_ref.1) | copy-start | bytes 1572868
  286.2 44.2 %copy-start.24 = (f32[128,8,128]{2,1,0:T(8,128)S(1)}, f32[128,8,128]{2,1,0:T(8,128)}, u32[]{:S(2)}) copy-start(f32[128,8,128]{2,1,0:T(8,128)} %param.33) | copy-start | bytes 1572868
  286.2 44.2 %copy-start.25 = (f32[128,8,128]{2,1,0:T(8,128)S(1)}, f32[128,8,128]{2,1,0:T(8,128)}, u32[]{:S(2)}) copy-start(f32[128,8,128]{2,1,0:T(8,128)} %param.34) | copy-start | bytes 1572868
  327.7 4.9 %copy-start.9 = (f32[1024,40]{0,1:T(8,128)S(1)}, f32[1024,40]{0,1:T(8,128)}, u32[]{:S(2)}) copy-start(f32[1024,40]{0,1:T(8,128)} %param.38) | copy-start | bytes 491524
  327.7 4.9 %copy-start.13 = (f32[1024,40]{0,1:T(8,128)S(1)}, f32[1024,40]{0,1:T(8,128)}, u32[]{:S(2)}) copy-start(f32[1024,40]{0,1:T(8,128)} %param.39) | copy-start | bytes 491524
  332.6 8.2 %copy-start.29 = (f32[9517]{0:T(1024)S(1)}, f32[9517]{0:T(1024)}, u32[]{:S(2)}) copy-start(f32[9517]{0:T(1024)} %param.47) | copy-start | bytes 114208
  (12 other events, 29.1 us)
